TPU v7x, 256 devices: a whole 4x4x8 slice. The times are simulated.
256 devices in a mesh: lon: 32 (over z, x_hi, core), lat: 8 (over y, x_lo).
Axes of the slice: x: 4 (x_hi: 2, x_lo: 2; x = x_hi * 2 + x_lo), y: 4, z: 8, core: 2. Of those that a mesh axis runs over, the one named last changes fastest.
Arguments:
- u_vel: float32 [3, 768, 8192], P(None, 'lat', 'lon'), may hold values from -3 to 3
- v_vel: float32 [3, 768, 8192], P(None, 'lat', 'lon'), may hold values from -3 to 3
- temp: float32 [3, 768, 8192], P(None, 'lat', 'lon'), may hold values from -5 to 5
- salt: float32 [3, 768, 8192], P(None, 'lat', 'lon'), may hold values from -5 to 5
- levels: int32 [768, 8192], P('lat', 'lon'), may hold values from 1 to 3
- land_sea: int32 [768, 8192], P('lat', 'lon'), may hold values 0 or 1
- coriolis: float32 [768, 8192], P('lat', 'lon'), may hold values from -1.5 to 1.5
- inv_dx: float32 [768, 8192], P('lat', 'lon'), may hold values from 0.5 to 2
- inv_dy: float32 [768, 8192], P('lat', 'lon'), may hold values from 0.5 to 2
Outputs:
- u_next: float32 [3, 768, 8192], P(None, 'lat', 'lon')
- v_next: float32 [3, 768, 8192], P(None, 'lat', 'lon')
- temp_next: float32 [3, 768, 8192], P(None, 'lat', 'lon')
- salt_next: float32 [3, 768, 8192], P(None, 'lat', 'lon')
All inputs are finite; a program needn't handle non-finite values. No bound on the sum of `land_sea` on one device may be relied on, other than what follows from the above.
Results may differ from a plain program's by a relative error of at most 0.00002.
Values sent between devices are 32-bit elements; how exact they have to be, the bound alone decides.
No kernel may reach another device: no remote copies, remote signals or barrier semaphores. Data moves between devices by JAX's collectives and lax.ppermute only.
A program may use at most 64 MiB of HBM per device.

v0:
```python
import jax
import jax.numpy as jnp
from jax import lax
from jax.sharding import PartitionSpec as P

STEPS = 4


def extended(block, sides, width, periodic):
    for axis, dim in sides:
        count = lax.axis_size(axis)
        forward = [(i, i + 1) for i in range(count - 1)]
        if periodic:
            forward.append((count - 1, 0))
        backward = [(target, source) for source, target in forward]
        low = lax.ppermute(
            lax.slice_in_dim(block, block.shape[dim] - width, None, axis=dim), axis, forward
        )
        high = lax.ppermute(lax.slice_in_dim(block, 0, width, axis=dim), axis, backward)
        block = jnp.concatenate([low, block, high], axis=dim)
    return block


def mirror_top(top_row):
    gathered = lax.all_gather(top_row, "lon", axis=2, tiled=True)
    width = top_row.shape[2]
    partner = lax.axis_size("lon") - 1 - lax.axis_index("lon")
    return lax.dynamic_slice_in_dim(gathered, partner * width, width, 2)


def extend(stack, signs):
    wide = extended(stack, (("lon", 3),), 1, True)
    tall = extended(wide, (("lat", 2),), 1, False)
    count = stack.shape[0] * stack.shape[1]
    top_row = wide[..., -1:, :].reshape((count, 1, wide.shape[3]))
    row_signs = jnp.repeat(signs, stack.shape[1])
    ghost = jnp.flip(mirror_top(top_row), axis=2) * row_signs[:, None, None]
    ghost = ghost.reshape(wide[..., -1:, :].shape)
    at_top = lax.axis_index("lat") == lax.axis_size("lat") - 1
    last_row = jnp.where(at_top, ghost, tall[..., -1:, :])
    return jnp.concatenate([tall[..., :-1, :], last_row], axis=2)


def centre_value(a):
    return a[..., 1:-1, 1:-1]


def east(a):
    return a[..., 1:-1, 2:]


def west(a):
    return a[..., 1:-1, :-2]


def north_value(a):
    return a[..., 2:, 1:-1]


def south_value(a):
    return a[..., :-2, 1:-1]


def advance(padded_field, wet_pad, coriolis, inv_dx, inv_dy):
    zonal_padded, meridional_padded, tracer_padded, density_padded = (
        padded_field[0],
        padded_field[1],
        padded_field[2],
        padded_field[3],
    )
    wet_centre_mask = centre_value(wet_pad)
    face_e = wet_centre_mask * east(wet_pad)
    face_w = wet_centre_mask * west(wet_pad)
    face_n = wet_centre_mask * north_value(wet_pad)
    face_s = wet_centre_mask * south_value(wet_pad)
    zonal_centre = centre_value(zonal_padded)
    meridional_centre = centre_value(meridional_padded)
    vel_e = 0.5 * (zonal_centre + east(zonal_padded))
    vel_w = 0.5 * (zonal_centre + west(zonal_padded))
    velocity_north = 0.5 * (meridional_centre + north_value(meridional_padded))
    velocity_south = 0.5 * (meridional_centre + south_value(meridional_padded))

    def laplacian_term(x):
        xc = centre_value(x)
        return inv_dx * inv_dx * (
            face_e * (east(x) - xc) - face_w * (xc - west(x))
        ) + inv_dy * inv_dy * (face_n * (north_value(x) - xc) - face_s * (xc - south_value(x)))

    def diverge(x):
        xc = centre_value(x)
        return inv_dx * (
            vel_e * face_e * 0.5 * (xc + east(x)) - vel_w * face_w * 0.5 * (xc + west(x))
        ) + inv_dy * (
            velocity_north * face_n * 0.5 * (xc + north_value(x))
            - velocity_south * face_s * 0.5 * (xc + south_value(x))
        )

    def zonal_gradient(x):
        xc = centre_value(x)
        return inv_dx * 0.5 * (face_e * (east(x) - xc) + face_w * (xc - west(x)))

    def meridional_gradient(x):
        xc = centre_value(x)
        return inv_dy * 0.5 * (face_n * (north_value(x) - xc) + face_s * (xc - south_value(x)))

    depth = (
        (jnp.arange(tracer_padded.shape[0]).astype(jnp.float32) + 0.5) / tracer_padded.shape[0]
    )[:, None, None]
    density = -0.8 * tracer_padded * (
        1.0 + 0.1 * tracer_padded + 0.3 * depth
    ) + 0.7 * density_padded * (1.0 - 0.05 * tracer_padded)
    pressure_field = 0.5 * (jnp.cumsum(density, axis=0) - 0.5 * density)
    temp_new = (
        centre_value(tracer_padded)
        + 0.1 * (-diverge(tracer_padded) + 0.3 * laplacian_term(tracer_padded))
    ) * wet_centre_mask
    salt_new = (
        centre_value(density_padded)
        + 0.1 * (-diverge(density_padded) + 0.3 * laplacian_term(density_padded))
    ) * wet_centre_mask
    u_new = (
        zonal_centre
        + 0.1
        * (
            coriolis * meridional_centre
            - zonal_gradient(pressure_field)
            - zonal_centre * zonal_gradient(zonal_padded)
            - meridional_centre * meridional_gradient(zonal_padded)
            + 0.3 * laplacian_term(zonal_padded)
        )
    ) * wet_centre_mask
    meridional_updated = (
        meridional_centre
        + 0.1
        * (
            -coriolis * zonal_centre
            - meridional_gradient(pressure_field)
            - zonal_centre * zonal_gradient(meridional_padded)
            - meridional_centre * meridional_gradient(meridional_padded)
            + 0.3 * laplacian_term(meridional_padded)
        )
    ) * wet_centre_mask
    return jnp.stack([u_new, meridional_updated, temp_new, salt_new])


def body(u_vel, v_vel, temp, salt, levels, land_sea, coriolis, inv_dx, inv_dy):
    layer = jnp.arange(u_vel.shape[0])[:, None, None]
    wet = jnp.where((land_sea[None] == 1) & (layer < levels[None]), 1.0, 0.0).astype(jnp.float32)
    signs = jnp.array([-1.0, -1.0, 1.0, 1.0], jnp.float32)
    wet_pad = extend(wet[None], jnp.ones((1,), jnp.float32))[0]
    fields = jnp.stack([u_vel, v_vel, temp, salt])
    for step in range(STEPS):
        fields = advance(extend(fields, signs), wet_pad, coriolis, inv_dx, inv_dy)
    return (fields[0], fields[1], fields[2], fields[3])


def solution(mesh):
    in_specs = (
        P(None, "lat", "lon"),
        P(None, "lat", "lon"),
        P(None, "lat", "lon"),
        P(None, "lat", "lon"),
        P("lat", "lon"),
        P("lat", "lon"),
        P("lat", "lon"),
        P("lat", "lon"),
        P("lat", "lon"),
    )
    out_specs = (
        P(None, "lat", "lon"),
        P(None, "lat", "lon"),
        P(None, "lat", "lon"),
        P(None, "lat", "lon"),
    )
    return jax.shard_map(body, mesh=mesh, in_specs=in_specs, out_specs=out_specs, check_vma=False)
```

profile of v0, /device:TPU:71, one launch (start us, length us, event | category | flops | bytes accessed | tf_op | source)
XLA Modules:
  0.0 478.6 jit_solution(5561625138875088060)
XLA Ops:
  1.5 0.9 fusion.155
  2.6 3.1 collective-permute-start.4
  5.7 1.3 pad_maximum_fusion.4
  9.2 3.3 collective-permute-start
  13.5 2.6 collective-permute-start.6
  16.2 2.7 collective-permute-start.7
  18.9 72.7 %all-gather = f32[1,3,1,8256]{1,2,0,3:T(1,128)S(1)} all-gather(f32[1,3,1,258]{1,2,0,3:T(1,128)S(1)} %copy.117), channel_id=2, replica_groups=mesh['lon'=32,'lat'=8] {'lon'}, dimensions={3}, use_global_device_ids=true | all-gather | bytes 102168 | tf_op jit(solution)/shard_map/all_gather | solution.py:25
  94.4 1.9 collective-permute-start.3
  96.4 4.3 collective-permute-start.2
  101.4 61.2 %all_gather.15 = f32[12,1,8256]{0,1,2:T(1,128)S(1)} all-gather(f32[12,1,258]{0,1,2:T(1,128)} %copy.115), channel_id=1, replica_groups=mesh['lon'=32,'lat'=8] {'lon'}, dimensions={2}, use_global_device_ids=true | all-gather | bytes 408672 | tf_op jit(solution)/shard_map/all_gather | solution.py:25
  163.2 1.6 copy.138
  164.9 2.2 reverse.1
  168.7 1.5 pad_maximum_fusion
  170.6 1.0 fusion.152
  171.6 0.9 multiply_bitcast_fusion.4
  175.3 2.4 collective-permute-start.8
  178.7 4.8 %collective-permute-done.9 = f32[4,3,96,1]{2,0,3,1:T(4,128)} collective-permute-done((f32[4,3,96,1]{2,0,3,1:T(4,128)S(1)}, f32[4,3,96,1]{2,0,3,1:T(4,128)}, u32[]{:S(2)}, u32[]{:S(2)}) %collective-permute-start.9) | collective-permute-done | bytes 4640 | tf_op jit(solution)/shard_map/ppermute | solution.py:19
  184.4 1.6 pad_maximum_fusion.20
  186.0 9.5 %collective-permute-start.11 = (f32[4,3,1,258]{3,2,1,0:T(1,128)}, f32[4,3,1,258]{3,2,1,0:T(1,128)}, u32[]{:S(2)}, u32[]{:S(2)}) collective-permute-start(f32[4,3,1,258]{3,2,1,0:T(1,128)} %get-tuple-element.17), channel_id=1, source_target_pairs={{1,0},{2,1},{3,2},{4,3},{5,4},{6,5},{7,6},{9,8},{10,9},{11,10},{12... | collective-permute-start | bytes 37160 | tf_op jit(solution)/shard_map/ppermute | solution.py:19
  195.6 1.9 collective-permute-start.10
  198.3 63.9 %all_gather.17 = f32[12,1,8256]{0,1,2:T(1,128)S(1)} all-gather(f32[12,1,258]{0,1,2:T(1,128)} %copy.124), channel_id=1, replica_groups=mesh['lon'=32,'lat'=8] {'lon'}, dimensions={2}, use_global_device_ids=true | all-gather | bytes 408672 | tf_op jit(solution)/shard_map/all_gather | solution.py:25
  262.8 1.6 copy.139
  264.5 2.2 reverse.2
  268.3 2.0 pad_maximum_fusion.1
  273.1 0.9 multiply_bitcast_fusion.3
  275.9 4.9 %collective-permute-start.12 = (f32[4,3,96,1]{2,0,3,1:T(4,128)S(1)}, f32[4,3,96,1]{2,0,3,1:T(4,128)S(1)}, u32[]{:S(2)}, u32[]{:S(2)}) collective-permute-start(f32[4,3,96,1]{2,0,3,1:T(4,128)S(1)} %copy.126), channel_id=1, source_target_pairs={{0,8},{8,16},{16,24},{24,32},{32,40},{40,48},{48,56},{56,64},{64,7... | collective-permute-start | bytes 13832 | tf_op jit(solution)/shard_map/ppermute | solution.py:16
  281.9 4.8 %collective-permute-done.13 = f32[4,3,96,1]{2,0,3,1:T(4,128)} collective-permute-done((f32[4,3,96,1]{2,0,3,1:T(4,128)S(1)}, f32[4,3,96,1]{2,0,3,1:T(4,128)}, u32[]{:S(2)}, u32[]{:S(2)}) %collective-permute-start.13) | collective-permute-done | bytes 4640 | tf_op jit(solution)/shard_map/ppermute | solution.py:19
  287.6 1.6 pad_maximum_fusion.14
  289.2 1.9 collective-permute-start.15
  291.2 4.3 collective-permute-start.14
  296.2 61.6 %all_gather.18 = f32[12,1,8256]{0,1,2:T(1,128)S(1)} all-gather(f32[12,1,258]{0,1,2:T(1,128)} %copy.130), channel_id=1, replica_groups=mesh['lon'=32,'lat'=8] {'lon'}, dimensions={2}, use_global_device_ids=true | all-gather | bytes 408672 | tf_op jit(solution)/shard_map/all_gather | solution.py:25
  358.5 1.6 copy.140
  360.1 2.2 reverse.3
  363.9 2.0 pad_maximum_fusion.2
  368.7 0.9 multiply_bitcast_fusion.1
  371.6 2.2 collective-permute-start.16
  374.8 4.8 %collective-permute-done.17 = f32[4,3,96,1]{2,0,3,1:T(4,128)} collective-permute-done((f32[4,3,96,1]{2,0,3,1:T(4,128)S(1)}, f32[4,3,96,1]{2,0,3,1:T(4,128)}, u32[]{:S(2)}, u32[]{:S(2)}) %collective-permute-start.17) | collective-permute-done | bytes 4640 | tf_op jit(solution)/shard_map/ppermute | solution.py:19
  380.5 1.6 pad_maximum_fusion.8
  382.1 6.4 %collective-permute-start.19 = (f32[4,3,1,258]{3,2,1,0:T(1,128)}, f32[4,3,1,258]{3,2,1,0:T(1,128)}, u32[]{:S(2)}, u32[]{:S(2)}) collective-permute-start(f32[4,3,1,258]{3,2,1,0:T(1,128)} %get-tuple-element.13), channel_id=1, source_target_pairs={{1,0},{2,1},{3,2},{4,3},{5,4},{6,5},{7,6},{9,8},{10,9},{11,10},{12... | collective-permute-start | bytes 37160 | tf_op jit(solution)/shard_map/ppermute | solution.py:19
  388.5 1.9 collective-permute-start.18
  391.2 71.8 %all_gather.19 = f32[12,1,8256]{0,1,2:T(1,128)S(1)} all-gather(f32[12,1,258]{0,1,2:T(1,128)} %copy.136), channel_id=1, replica_groups=mesh['lon'=32,'lat'=8] {'lon'}, dimensions={2}, use_global_device_ids=true | all-gather | bytes 408672 | tf_op jit(solution)/shard_map/all_gather | solution.py:25
  463.7 1.6 copy.141
  465.3 2.2 reverse.4
  469.1 2.0 pad_maximum_fusion.3
  472.3 1.5 fusion.55
  473.9 1.4 fusion.68
  475.3 1.6 add_multiply_fusion
  477.0 1.6 add_multiply_fusion.1
  (140 shorter events, 38.4 us)
Async XLA Ops:
  2.6 10.8 %collective-permute-start.4 = (f32[1,3,96,1]{3,2,1,0:T(8,128)S(1)}, f32[1,3,96,1]{3,2,1,0:T(8,128)S(1)}, u32[]{:S(2)}, u32[]{:S(2)}) collective-permute-start(f32[1,3,96,1]{3,2,1,0:T(8,128)S(1)} %get-tuple-element.47), channel_id=1, source_target_pairs={{0,8},{8,16},{16,24},{24,32},{32,40},{40,48},{48,56},{56,64},{64,7... | collective-permute-start | bytes 3464 | tf_op jit(solution)/shard_map/ppermute | solution.py:16
  5.7 7.7 %collective-permute-start.5 = (f32[1,3,96,1]{3,2,1,0:T(8,128)S(1)}, f32[1,3,96,1]{3,2,1,0:T(8,128)S(1)}, u32[]{:S(2)}, u32[]{:S(2)}) collective-permute-start(f32[1,3,96,1]{3,2,1,0:T(8,128)S(1)} %get-tuple-element.48), channel_id=1, source_target_pairs={{8,0},{16,8},{24,16},{32,24},{40,32},{48,40},{56,48},{64,56},{72,6... | collective-permute-start | bytes 3464 | tf_op jit(solution)/shard_map/ppermute | solution.py:19
  7.0 5.5 %copy-start = (f32[96,256]{1,0:T(8,128)S(1)}, f32[96,256]{1,0:T(8,128)}, u32[]{:S(2)}) copy-start(f32[96,256]{1,0:T(8,128)} %param.18) | copy-start | bytes 294916
  7.0 5.5 %copy-start.1 = (f32[96,256]{1,0:T(8,128)S(1)}, f32[96,256]{1,0:T(8,128)}, u32[]{:S(2)}) copy-start(f32[96,256]{1,0:T(8,128)} %param.17) | copy-start | bytes 294916
  7.1 5.5 %copy-start.23 = (f32[4]{0:T(128)S(1)}, f32[4]{0:T(128)}, u32[]{:S(2)}) copy-start(f32[4]{0:T(128)} %constant.55.clone) | copy-start | bytes 52
  7.1 5.7 %copy-start.18 = (f32[96,256]{1,0:T(8,128)S(1)}, f32[96,256]{1,0:T(8,128)}, u32[]{:S(2)}) copy-start(f32[96,256]{1,0:T(8,128)} %param.16) | copy-start | bytes 294916
  8.1 84.6 %collective-permute-start.1 = (f32[4,3,96,1]{2,0,3,1:T(4,128)}, f32[4,3,96,1]{2,0,3,1:T(4,128)}, u32[]{:S(2)}, u32[]{:S(2)}) collective-permute-start(f32[4,3,96,1]{2,0,3,1:T(4,128)} %copy.112), channel_id=1, source_target_pairs={{8,0},{16,8},{24,16},{32,24},{40,32},{48,40},{56,48},{64,56},{72,6... | collective-permute-start | bytes 13832 | tf_op jit(solution)/shard_map/ppermute | solution.py:19
  9.2 83.2 %collective-permute-start = (f32[4,3,96,1]{2,0,3,1:T(4,128)S(1)}, f32[4,3,96,1]{2,0,3,1:T(4,128)S(1)}, u32[]{:S(2)}, u32[]{:S(2)}) collective-permute-start(f32[4,3,96,1]{2,0,3,1:T(4,128)S(1)} %copy.111), channel_id=1, source_target_pairs={{0,8},{8,16},{16,24},{24,32},{32,40},{40,48},{48,56},{56,64},{64,7... | collective-permute-start | bytes 13832 | tf_op jit(solution)/shard_map/ppermute | solution.py:16
  13.5 78.7 %collective-permute-start.6 = (f32[1,3,1,258]{3,2,1,0:T(1,128)S(1)}, f32[1,3,1,258]{3,2,1,0:T(1,128)S(1)}, u32[]{:S(2)}, u32[]{:S(2)}) collective-permute-start(f32[1,3,1,258]{3,2,1,0:T(1,128)S(1)} %get-tuple-element.45), channel_id=1, source_target_pairs={{0,1},{1,2},{2,3},{3,4},{4,5},{5,6},{6,7},{8,9},{9,10},{10,11},{11... | collective-permute-start | bytes 9296 | tf_op jit(solution)/shard_map/ppermute | solution.py:16
  16.2 75.8 %collective-permute-start.7 = (f32[1,3,1,258]{3,2,1,0:T(1,128)S(1)}, f32[1,3,1,258]{3,2,1,0:T(1,128)S(1)}, u32[]{:S(2)}, u32[]{:S(2)}) collective-permute-start(f32[1,3,1,258]{3,2,1,0:T(1,128)S(1)} %get-tuple-element.46), channel_id=1, source_target_pairs={{1,0},{2,1},{3,2},{4,3},{5,4},{6,5},{7,6},{9,8},{10,9},{11,10},{12... | collective-permute-start | bytes 9296 | tf_op jit(solution)/shard_map/ppermute | solution.py:19
  91.7 2.0 copy-start.14
  91.7 2.0 copy-start.15
  91.7 2.0 copy-start.16
  91.7 2.0 copy-start.17
  94.4 73.4 %collective-permute-start.3 = (f32[4,3,1,258]{3,2,1,0:T(1,128)}, f32[4,3,1,258]{3,2,1,0:T(1,128)}, u32[]{:S(2)}, u32[]{:S(2)}) collective-permute-start(f32[4,3,1,258]{3,2,1,0:T(1,128)} %get-tuple-element.19), channel_id=1, source_target_pairs={{1,0},{2,1},{3,2},{4,3},{5,4},{6,5},{7,6},{9,8},{10,9},{11,10},{12... | collective-permute-start | bytes 37160 | tf_op jit(solution)/shard_map/ppermute | solution.py:19
  96.4 72.3 %collective-permute-start.2 = (f32[4,3,1,258]{3,2,1,0:T(1,128)S(1)}, f32[4,3,1,258]{3,2,1,0:T(1,128)}, u32[]{:S(2)}, u32[]{:S(2)}) collective-permute-start(f32[4,3,1,258]{3,2,1,0:T(1,128)S(1)} %get-tuple-element.20), channel_id=1, source_target_pairs={{0,1},{1,2},{2,3},{3,4},{4,5},{5,6},{6,7},{8,9},{9,10},{10,11},{11... | collective-permute-start | bytes 37160 | tf_op jit(solution)/shard_map/ppermute | solution.py:16
  171.6 2.8 copy-start.2
  172.5 1.8 copy-start.9
  172.5 1.0 copy-start.19
  173.5 0.9 copy-start.11
  174.3 0.7 copy-start.7
  175.3 3.2 collective-permute-start.8
  177.9 5.6 %collective-permute-start.9 = (f32[4,3,96,1]{2,0,3,1:T(4,128)S(1)}, f32[4,3,96,1]{2,0,3,1:T(4,128)}, u32[]{:S(2)}, u32[]{:S(2)}) collective-permute-start(f32[4,3,96,1]{2,0,3,1:T(4,128)S(1)} %copy.121), channel_id=1, source_target_pairs={{8,0},{16,8},{24,16},{32,24},{40,32},{48,40},{56,48},{64,56},{72,6... | collective-permute-start | bytes 13832 | tf_op jit(solution)/shard_map/ppermute | solution.py:19
  186.0 81.4 %collective-permute-start.11 = (f32[4,3,1,258]{3,2,1,0:T(1,128)}, f32[4,3,1,258]{3,2,1,0:T(1,128)}, u32[]{:S(2)}, u32[]{:S(2)}) collective-permute-start(f32[4,3,1,258]{3,2,1,0:T(1,128)} %get-tuple-element.17), channel_id=1, source_target_pairs={{1,0},{2,1},{3,2},{4,3},{5,4},{6,5},{7,6},{9,8},{10,9},{11,10},{12... | collective-permute-start | bytes 37160 | tf_op jit(solution)/shard_map/ppermute | solution.py:19
  195.6 72.7 %collective-permute-start.10 = (f32[4,3,1,258]{3,2,1,0:T(1,128)S(1)}, f32[4,3,1,258]{3,2,1,0:T(1,128)}, u32[]{:S(2)}, u32[]{:S(2)}) collective-permute-start(f32[4,3,1,258]{3,2,1,0:T(1,128)S(1)} %get-tuple-element.18), channel_id=1, source_target_pairs={{0,1},{1,2},{2,3},{3,4},{4,5},{5,6},{6,7},{8,9},{9,10},{10,11},{11... | collective-permute-start | bytes 37160 | tf_op jit(solution)/shard_map/ppermute | solution.py:16
  270.6 0.9 copy-start.20
  272.3 2.7 copy-start.5
  273.0 1.9 copy-start.6
  274.0 1.0 copy-start.12
  275.0 0.7 copy-start.13
  275.9 5.7 %collective-permute-start.12 = (f32[4,3,96,1]{2,0,3,1:T(4,128)S(1)}, f32[4,3,96,1]{2,0,3,1:T(4,128)S(1)}, u32[]{:S(2)}, u32[]{:S(2)}) collective-permute-start(f32[4,3,96,1]{2,0,3,1:T(4,128)S(1)} %copy.126), channel_id=1, source_target_pairs={{0,8},{8,16},{16,24},{24,32},{32,40},{40,48},{48,56},{56,64},{64,7... | collective-permute-start | bytes 13832 | tf_op jit(solution)/shard_map/ppermute | solution.py:16
  281.1 5.6 %collective-permute-start.13 = (f32[4,3,96,1]{2,0,3,1:T(4,128)S(1)}, f32[4,3,96,1]{2,0,3,1:T(4,128)}, u32[]{:S(2)}, u32[]{:S(2)}) collective-permute-start(f32[4,3,96,1]{2,0,3,1:T(4,128)S(1)} %copy.127), channel_id=1, source_target_pairs={{8,0},{16,8},{24,16},{32,24},{40,32},{48,40},{56,48},{64,56},{72,6... | collective-permute-start | bytes 13832 | tf_op jit(solution)/shard_map/ppermute | solution.py:19
  289.2 73.9 %collective-permute-start.15 = (f32[4,3,1,258]{3,2,1,0:T(1,128)}, f32[4,3,1,258]{3,2,1,0:T(1,128)}, u32[]{:S(2)}, u32[]{:S(2)}) collective-permute-start(f32[4,3,1,258]{3,2,1,0:T(1,128)} %get-tuple-element.15), channel_id=1, source_target_pairs={{1,0},{2,1},{3,2},{4,3},{5,4},{6,5},{7,6},{9,8},{10,9},{11,10},{12... | collective-permute-start | bytes 37160 | tf_op jit(solution)/shard_map/ppermute | solution.py:19
  291.2 72.7 %collective-permute-start.14 = (f32[4,3,1,258]{3,2,1,0:T(1,128)S(1)}, f32[4,3,1,258]{3,2,1,0:T(1,128)}, u32[]{:S(2)}, u32[]{:S(2)}) collective-permute-start(f32[4,3,1,258]{3,2,1,0:T(1,128)S(1)} %get-tuple-element.16), channel_id=1, source_target_pairs={{0,1},{1,2},{2,3},{3,4},{4,5},{5,6},{6,7},{8,9},{9,10},{10,11},{11... | collective-permute-start | bytes 37160 | tf_op jit(solution)/shard_map/ppermute | solution.py:16
  366.2 0.9 copy-start.21
  367.9 2.7 copy-start.3
  368.7 1.9 copy-start.4
  369.7 1.0 copy-start.8
  370.6 0.7 copy-start.10
  371.6 3.0 collective-permute-start.16
  374.0 5.6 %collective-permute-start.17 = (f32[4,3,96,1]{2,0,3,1:T(4,128)S(1)}, f32[4,3,96,1]{2,0,3,1:T(4,128)}, u32[]{:S(2)}, u32[]{:S(2)}) collective-permute-start(f32[4,3,96,1]{2,0,3,1:T(4,128)S(1)} %copy.133), channel_id=1, source_target_pairs={{8,0},{16,8},{24,16},{32,24},{40,32},{48,40},{56,48},{64,56},{72,6... | collective-permute-start | bytes 13832 | tf_op jit(solution)/shard_map/ppermute | solution.py:19
  382.1 86.2 %collective-permute-start.19 = (f32[4,3,1,258]{3,2,1,0:T(1,128)}, f32[4,3,1,258]{3,2,1,0:T(1,128)}, u32[]{:S(2)}, u32[]{:S(2)}) collective-permute-start(f32[4,3,1,258]{3,2,1,0:T(1,128)} %get-tuple-element.13), channel_id=1, source_target_pairs={{1,0},{2,1},{3,2},{4,3},{5,4},{6,5},{7,6},{9,8},{10,9},{11,10},{12... | collective-permute-start | bytes 37160 | tf_op jit(solution)/shard_map/ppermute | solution.py:19
  388.5 80.6 %collective-permute-start.18 = (f32[4,3,1,258]{3,2,1,0:T(1,128)S(1)}, f32[4,3,1,258]{3,2,1,0:T(1,128)}, u32[]{:S(2)}, u32[]{:S(2)}) collective-permute-start(f32[4,3,1,258]{3,2,1,0:T(1,128)S(1)} %get-tuple-element.14), channel_id=1, source_target_pairs={{0,1},{1,2},{2,3},{3,4},{4,5},{5,6},{6,7},{8,9},{9,10},{10,11},{11... | collective-permute-start | bytes 37160 | tf_op jit(solution)/shard_map/ppermute | solution.py:16
  471.4 0.9 copy-start.22
where the time goes:
time: 481 us; the launch traced here: 479 us
  blocking collectives  331 us (69%)
  starting transfers between devices  54.4 us (11%)
  other arithmetic  42 us (9%)
  local copies, waits for them, and re-layouts  33.7 us (7%)
  waiting for transfers between devices  15.9 us (3%)
    all_gather x5, blocking collectives, mirror_top(): gathered = lax.all_gather(top_row, 'lon', axis=2, tiled=True)  331 us
    ppermute x10, starting transfers between devices, extended(): lax.ppermute(lax.slice_in_dim(block, block.shape[dim] - width, None, axis...  30.9 us
    ppermute x10, starting transfers between devices, extended(): lax.ppermute(lax.slice_in_dim(block, 0, width, axis=dim), axis, backward)  23.5 us
    unnamed x57, local copies, waits for them, and re-layouts  19 us
    ppermute x10, waiting for transfers between devices, extended(): lax.ppermute(lax.slice_in_dim(block, 0, width, axis=dim), axis, backward)  14.4 us
    another operation x15, other arithmetic, advance(): return jnp.stack([u_new, meridional_updated, temp_new, salt_new])  10.8 us
  transfers between devices with their start and end apart: 20, of which 6 were waited for; matrix products, arithmetic and copies ran while one was open for 7% of the time, Pallas kernels for 0%

commit v1 on v0

v1 whole, which is shorter than its diff:
```python
import jax
import jax.numpy as jnp
from jax import lax
from jax.experimental import pallas as pl
from jax.experimental.pallas import tpu as pltpu
from jax.sharding import PartitionSpec as P

STEPS = 4
K = 3
HALO = 4
PLANES = 17
LANES = 128
OFFSET = 16
U, V, T, S, PR = range(5)
CXE, CXW, CYN, CYS, HXE, HXW, HYN, HYS, WET, WCEN, WCOR = range(11)
VMEM_LIMIT = 48 * 1024 * 1024


def plane_values(refs, p, rows, lanes):
    if p < 12:
        return refs[p // 3][p % 3, rows, lanes]
    return refs[4 + p - 12][rows, lanes].astype(jnp.float32)


def lane_index(shape):
    return lax.broadcasted_iota(jnp.int32, shape, len(shape) - 1)


def pack_columns(*refs):
    ins, (out_a, out_b) = refs[:9], refs[9:]
    rows = ins[0].shape[1]
    cols = ins[0].shape[2]
    even = lax.rem(lax.axis_index("lon"), 2) == 0
    lane = lane_index((8, LANES))
    for r in range(0, rows, 8):
        west = east = None
        for p in range(PLANES):
            w = plane_values(ins, p, slice(r, r + 8), slice(0, LANES))
            e = plane_values(ins, p, slice(r, r + 8), slice(cols - LANES, cols))
            w = pltpu.roll(w, 4 * p, 1) if p else w
            e = pltpu.roll(e, (4 * p + HALO) % LANES, 1)
            if p == 0:
                west, east = w, e
            else:
                mine = lane >= 4 * p
                west, east = jnp.where(mine, w, west), jnp.where(mine, e, east)
        out_a[r : r + 8, :] = jnp.where(even, east, west)
        out_b[r : r + 8, :] = jnp.where(even, west, east)


def pack_rows(*refs):
    south, north = refs[0:9], refs[9:18]
    col_a, col_b, out_a, out_b = refs[18:]
    rows = col_a.shape[0]
    even = lax.rem(lax.axis_index("lat"), 2) == 0
    for p in range(PLANES):
        s = plane_values(south, p, slice(0, 8), slice(None))[:HALO]
        n = plane_values(north, p, slice(0, 8), slice(None))[HALO:]
        out_a[4 * p : 4 * p + 4, :] = jnp.where(even, n, s)
        out_b[4 * p : 4 * p + 4, :] = jnp.where(even, s, n)
    for ref, lanes in ((col_a, slice(0, LANES)), (col_b, slice(LANES, 2 * LANES))):
        s = ref[0:HALO, :]
        n = ref[rows - HALO : rows, :]
        out_a[4 * PLANES : 4 * PLANES + 4, lanes] = jnp.where(even, n, s)
        out_b[4 * PLANES : 4 * PLANES + 4, lanes] = jnp.where(even, s, n)


def xor_rows(x, bit):
    row = lax.broadcasted_iota(jnp.int32, x.shape, 0)
    return jnp.where((row & bit) != 0, pltpu.roll(x, bit, 0), pltpu.roll(x, 8 - bit, 0))


def xor_lanes(x, bit):
    lane = lane_index(x.shape)
    if bit == LANES // 2:
        return pltpu.roll(x, bit, 1)
    return jnp.where((lane & bit) != 0, pltpu.roll(x, bit, 1), pltpu.roll(x, LANES - bit, 1))


def fold_rows(ref, out):
    lane = lane_index((8, LANES))
    row = lax.broadcasted_iota(jnp.int32, (8, LANES), 0)
    for r in range(0, 4 * PLANES + 4, 8):
        turned, short = [], []
        for t in range(2):
            x = ref[r : r + 8, t * LANES : (t + 1) * LANES]
            x = xor_rows(xor_rows(x, 1), 2)
            x = xor_lanes(xor_lanes(x, 1), 2)
            short.append(x)
            for bit in (4, 8, 16, 32, 64):
                x = xor_lanes(x, bit)
            turned.append(x)
        for t in range(2):
            x = turned[1 - t]
            if r < 24:
                x = -x
            if r + 8 > 4 * PLANES:
                packed = jnp.where(lane < 24, -short[t], short[t])
                x = jnp.where(row < 4, x, packed)
            out[r : r + 8, t * LANES : (t + 1) * LANES] = x


def shift_east(tiles, last):
    rolled = [pltpu.roll(x, LANES - 1, 1) for x in tiles]
    return [jnp.where(last, rolled[(t + 1) % 3], rolled[t]) for t in range(3)]


def shift_west(tiles, first):
    rolled = [pltpu.roll(x, 1, 1) for x in tiles]
    return [jnp.where(first, rolled[(t + 2) % 3], rolled[t]) for t in range(3)]


def density(t, s, k):
    depth = (k + 0.5) / K
    return t * ((-0.8 - 0.24 * depth) - 0.08 * t - 0.035 * s) + 0.7 * s


def advance_block(field, coef, src, r, write):
    lane = lane_index((8, LANES))
    first, last = lane == 0, lane == LANES - 1
    above = [None] * 3
    for k in range(K):
        def load(f, shift):
            return [field[src, f, k, t, pl.ds(r + shift, 8), :] for t in range(3)]

        c = [load(f, 0) for f in range(5)]
        n = [load(f, 1) for f in range(5)]
        s = [load(f, -1) for f in range(5)]
        e = [shift_east(x, last) for x in c]
        w = [shift_west(x, first) for x in c]
        for t in range(3):
            def get(i):
                return coef[i, k, t, pl.ds(r, 8), :]

            cxe, cxw, cyn, cys = get(CXE), get(CXW), get(CYN), get(CYS)
            hxe, hxw, hyn, hys = get(HXE), get(HXW), get(HYN), get(HYS)
            u, v = c[U][t], c[V][t]
            u2, v2 = u + u, v + v
            ae, aw = cxe - hxe * u2, cxw + hxw * u2
            an, as_ = cyn - hyn * v2, cys + hys * v2
            ac = get(WET) - ((ae + aw) + (an + as_))
            wcor = get(WCOR)
            p = c[PR][t]
            px = hxe * (e[PR][t] - p) + hxw * (p - w[PR][t])
            py = hyn * (n[PR][t] - p) + hys * (p - s[PR][t])

            def combine(f, ac, ae, aw, an, as_):
                return (ac * c[f][t] + (ae * e[f][t] + aw * w[f][t])) + (an * n[f][t] + as_ * s[f][t])

            write(U, k, t, combine(U, ac, ae, aw, an, as_) + (wcor * v - px))
            write(V, k, t, combine(V, ac, ae, aw, an, as_) - (wcor * u + py))
            ae = cxe - hxe * (u + e[U][t])
            aw = cxw + hxw * (u + w[U][t])
            an = cyn - hyn * (v + n[V][t])
            as_ = cys + hys * (v + s[V][t])
            ac = get(WCEN) + ((ae + aw) + (an + as_))
            t_new = combine(T, ac, ae, aw, an, as_)
            s_new = combine(S, ac, ae, aw, an, as_)
            write(T, k, t, t_new)
            write(S, k, t, s_new)
            rho = density(t_new, s_new, k)
            half = 0.5 * rho
            write(PR, k, t, half if k == 0 else above[t] + half)
            above[t] = rho if k == 0 else above[t] + rho


def run_steps(*refs):
    ins, (col_a, col_b, row_a, row_b), outs = refs[:9], refs[9:13], refs[13:17]
    field, coef, wet, geo, cols, north = refs[17:]
    rows = ins[0].shape[1]
    top = OFFSET + rows
    lon_even = lax.rem(lax.axis_index("lon"), 2) == 0
    lat = lax.axis_index("lat")
    lat_even = lax.rem(lat, 2) == 0
    lane = lane_index((8, LANES))
    first, last = lane == 0, lane == LANES - 1

    fold = lat == lax.axis_size("lat") - 1

    @pl.when(fold)
    def _():
        fold_rows(row_b, north)

    @pl.when(jnp.logical_not(fold))
    def _():
        north[...] = jnp.where(lat_even, row_a[...], row_b[...])

    def south_rows(p, lanes):
        rows_p = slice(4 * p, 4 * p + 4)
        return jnp.where(lat_even, row_b[rows_p, lanes], row_a[rows_p, lanes])

    def place(dst, a, b):
        for half, even_ref in ((0, b), (1, a)):
            odd_ref = a if half == 0 else b
            cols[half, dst, :] = jnp.where(lon_even, even_ref, odd_ref)

    place(slice(OFFSET, top), col_a[...], col_b[...])
    rows_c = slice(4 * PLANES, 4 * PLANES + 4)
    place(
        slice(OFFSET - HALO, OFFSET),
        south_rows(PLANES, slice(0, LANES)),
        south_rows(PLANES, slice(LANES, 2 * LANES)),
    )
    place(slice(top, top + HALO), north[rows_c, 0:LANES], north[rows_c, LANES : 2 * LANES])

    def target(p):
        if p < 12:
            return lambda t, dst: (field, (0, p // 3, p % 3, t, dst, slice(None)))
        return lambda t, dst: (geo, (p - 12, t, dst, slice(None)))

    for p in range(PLANES):
        at = target(p)
        for t in range(2):
            lanes = slice(t * LANES, (t + 1) * LANES)
            ref, idx = at(t, slice(OFFSET, top))
            ref[idx] = plane_values(ins, p, slice(None), lanes)
            ref, idx = at(t, slice(OFFSET - HALO, OFFSET))
            ref[idx] = south_rows(p, lanes)
            ref, idx = at(t, slice(top, top + HALO))
            ref[idx] = north[4 * p : 4 * p + 4, lanes]

    @pl.loop(0, (rows + 16) // 8)
    def _(b):
        r = pl.multiple_of(OFFSET - 8 + 8 * b, 8)
        west, east = cols[0, pl.ds(r, 8), :], cols[1, pl.ds(r, 8), :]
        for p in range(PLANES):
            e = pltpu.roll(east, LANES - 4 * p, 1) if p else east
            w = pltpu.roll(west, LANES - 4 * p - HALO, 1)
            ref, idx = target(p)(2, pl.ds(r, 8))
            ref[idx] = jnp.where(lane < LANES // 2, e, w)
        for t in range(3):
            wet_levels = jnp.where(geo[1, t, pl.ds(r, 8), :] == 1.0, geo[0, t, pl.ds(r, 8), :], 0.0)
            above = None
            for k in range(K):
                wet[k, t, pl.ds(r, 8), :] = jnp.where(wet_levels > k, 1.0, 0.0)
                rho = density(field[0, T, k, t, pl.ds(r, 8), :], field[0, S, k, t, pl.ds(r, 8), :], k)
                half = 0.5 * rho
                field[0, PR, k, t, pl.ds(r, 8), :] = half if k == 0 else above + half
                above = rho if k == 0 else above + rho

    @pl.loop(0, (rows + 16) // 8)
    def _(b):
        r = pl.multiple_of(OFFSET - 8 + 8 * b, 8)
        for k in range(K):
            c = [wet[k, t, pl.ds(r, 8), :] for t in range(3)]
            e, w = shift_east(c, last), shift_west(c, first)
            for t in range(3):
                n = wet[k, t, pl.ds(r + 1, 8), :]
                s = wet[k, t, pl.ds(r - 1, 8), :]
                idx, idy = geo[3, t, pl.ds(r, 8), :], geo[4, t, pl.ds(r, 8), :]
                hx, hy = 0.025 * idx, 0.025 * idy
                fe, fw, fn, fs = c[t] * e[t], c[t] * w[t], c[t] * n, c[t] * s
                hxe, hxw, hyn, hys = fe * hx, fw * hx, fn * hy, fs * hy
                cx, cy = 1.2 * idx, 1.2 * idy
                cxe, cxw, cyn, cys = hxe * cx, hxw * cx, hyn * cy, hys * cy
                total = (cxe + cxw) + (cyn + cys)
                for i, value in (
                    (CXE, cxe), (CXW, cxw), (CYN, cyn), (CYS, cys),
                    (HXE, hxe), (HXW, hxw), (HYN, hyn), (HYS, hys),
                    (WET, c[t]), (WCEN, c[t] - 2.0 * total),
                    (WCOR, 0.1 * c[t] * geo[2, t, pl.ds(r, 8), :]),
                ):
                    coef[i, k, t, pl.ds(r, 8), :] = value

    for step in range(STEPS - 1):
        @pl.loop(0, (rows + 16) // 8)
        def _(b):
            r = pl.multiple_of(OFFSET - 8 + 8 * b, 8)

            def write(f, k, t, value):
                field[(step + 1) % 2, f, k, t, pl.ds(r, 8), :] = value

            advance_block(field, coef, step % 2, r, write)

    @pl.loop(0, rows // 8)
    def _(b):
        r = pl.multiple_of(8 * b, 8)

        def write(f, k, t, value):
            if f < PR and t < 2:
                outs[f][k, pl.ds(r, 8), t * LANES : (t + 1) * LANES] = value

        advance_block(field, coef, (STEPS - 1) % 2, pl.multiple_of(OFFSET + r, 8), write)


def lon_pairs(nlon, nlat, partner):
    return [(i * nlat + j, partner(i) * nlat + j) for i in range(nlon) for j in range(nlat)]


def lat_pairs(nlon, nlat, odd):
    pairs = []
    for i in range(nlon):
        for j in range(nlat):
            up = (j % 2 == 0) != odd
            to, at = (j + 1 if up else j - 1), i
            if to < 0:
                continue
            if to == nlat:
                to, at = nlat - 1, nlon - 1 - i
            pairs.append((i * nlat + j, at * nlat + to))
    return pairs


def body(u_vel, v_vel, temp, salt, levels, land_sea, coriolis, inv_dx, inv_dy):
    args = (u_vel, v_vel, temp, salt, levels, land_sea, coriolis, inv_dx, inv_dy)
    rows, cols = levels.shape
    nlon, nlat = lax.axis_size("lon"), lax.axis_size("lat")
    axes = ("lon", "lat")
    params = pltpu.CompilerParams(vmem_limit_bytes=VMEM_LIMIT)
    f32 = jnp.float32
    column = jax.ShapeDtypeStruct((rows, LANES), f32)
    col_a, col_b = pl.pallas_call(
        pack_columns, out_shape=(column, column), compiler_params=params, name="pack_columns"
    )(*args)
    col_a = lax.ppermute(col_a, axes, lon_pairs(nlon, nlat, lambda i: i ^ 1))
    col_b = lax.ppermute(
        col_b, axes, lon_pairs(nlon, nlat, lambda i: (i + 1 if i % 2 else i - 1) % nlon)
    )

    def edge(block):
        def spec(a):
            if a.ndim == 3:
                return pl.BlockSpec((K, 8, cols), lambda i: (0, block, 0))
            return pl.BlockSpec((8, cols), lambda i: (block, 0))
        return [spec(a) for a in args]

    whole = pl.BlockSpec((rows, LANES), lambda i: (0, 0))
    row = jax.ShapeDtypeStruct((4 * PLANES + 4, cols), f32)
    row_spec = pl.BlockSpec(row.shape, lambda i: (0, 0))
    row_a, row_b = pl.pallas_call(
        pack_rows,
        grid=(1,),
        in_specs=edge(0) + edge(rows // 8 - 1) + [whole, whole],
        out_specs=(row_spec, row_spec),
        out_shape=(row, row),
        compiler_params=params,
        name="pack_rows",
    )(*args, *args, col_a, col_b)
    row_b = lax.ppermute(row_b, axes, lat_pairs(nlon, nlat, True))
    row_a = lax.ppermute(row_a, axes, lat_pairs(nlon, nlat, False))
    tall = rows + 32
    out = jax.ShapeDtypeStruct(u_vel.shape, f32)
    return pl.pallas_call(
        run_steps,
        out_shape=(out,) * 4,
        scratch_shapes=[
            pltpu.VMEM((2, 5, K, 3, tall, LANES), f32),
            pltpu.VMEM((11, K, 3, tall, LANES), f32),
            pltpu.VMEM((K, 3, tall, LANES), f32),
            pltpu.VMEM((5, 3, tall, LANES), f32),
            pltpu.VMEM((2, tall, LANES), f32),
            pltpu.VMEM(row.shape, f32),
        ],
        compiler_params=params,
        name="run_steps",
    )(*args, col_a, col_b, row_a, row_b)


def solution(mesh):
    block, plane = P(None, "lat", "lon"), P("lat", "lon")
    return jax.shard_map(
        body,
        mesh=mesh,
        in_specs=(block,) * 4 + (plane,) * 5,
        out_specs=(block,) * 4,
        check_vma=False,
    )
```

time: 481 us -> 47.7 us (0.10)
  the two profiles are of different devices: /device:TPU:71 before, /device:TPU:26 now
where the time goes in v1:
time: 47.7 us; the launch traced here: 47.3 us
  Pallas kernels  18.2 us (38%)
  starting transfers between devices  15.5 us (32%)
  local copies, waits for them, and re-layouts  8.3 us (17%)
  waiting for transfers between devices  4.66 us (10%)
  between operations  0.69 us (1%)
    pallas_call x1, Pallas kernels, body(): pl.pallas_call(run_steps, out_shape=(out,) * 4, scratch_shapes=[pltpu.VME...  17.7 us
    unnamed x18, local copies, waits for them, and re-layouts  8.3 us
    ppermute x1, starting transfers between devices, body(): lax.ppermute(col_b, axes, lon_pairs(nlon, nlat, lambda i: (i + 1 if i % 2...  7.52 us
    ppermute x1, starting transfers between devices, body(): row_b = lax.ppermute(row_b, axes, lat_pairs(nlon, nlat, True))  6.37 us
    ppermute x1, waiting for transfers between devices, body(): row_b = lax.ppermute(row_b, axes, lat_pairs(nlon, nlat, True))  2.89 us
    ppermute x1, waiting for transfers between devices, body(): lax.ppermute(col_b, axes, lon_pairs(nlon, nlat, lambda i: (i + 1 if i % 2...  1.77 us
    ppermute x1, starting transfers between devices, body(): row_a = lax.ppermute(row_a, axes, lat_pairs(nlon, nlat, False))  1.52 us
  transfers between devices with their start and end apart: 4, of which 2 were waited for; matrix products, arithmetic and copies ran while one was open for 0% of the time, Pallas kernels for 0%

profile of v1, /device:TPU:26, one launch (start us, length us, event | category | flops | bytes accessed | tf_op | source)
XLA Modules:
  0.0 47.3 jit_solution(1899526930505686201)
XLA Ops:
  0.6 0.0 copy-start
  0.6 1.0 %copy-done = f32[3,96,256]{2,1,0:T(8,128)S(1)} copy-done((f32[3,96,256]{2,1,0:T(8,128)S(1)}, f32[3,96,256]{2,1,0:T(8,128)}, u32[]{:S(2)}) %copy-start) | copy-done | bytes 294936
  1.6 0.0 copy-start.1
  1.6 1.0 %copy-done.1 = f32[3,96,256]{2,1,0:T(8,128)S(1)} copy-done((f32[3,96,256]{2,1,0:T(8,128)S(1)}, f32[3,96,256]{2,1,0:T(8,128)}, u32[]{:S(2)}) %copy-start.1) | copy-done | bytes 294936
  2.6 0.0 copy-start.2
  2.6 1.0 %copy-done.2 = f32[3,96,256]{2,1,0:T(8,128)S(1)} copy-done((f32[3,96,256]{2,1,0:T(8,128)S(1)}, f32[3,96,256]{2,1,0:T(8,128)}, u32[]{:S(2)}) %copy-start.2) | copy-done | bytes 294936
  3.5 0.0 copy-start.3
  3.5 1.0 %copy-done.3 = f32[3,96,256]{2,1,0:T(8,128)S(1)} copy-done((f32[3,96,256]{2,1,0:T(8,128)S(1)}, f32[3,96,256]{2,1,0:T(8,128)}, u32[]{:S(2)}) %copy-start.3) | copy-done | bytes 294936
  4.5 0.0 copy-start.4
  4.5 0.9 %copy-done.4 = s32[96,256]{1,0:T(8,128)S(1)} copy-done((s32[96,256]{1,0:T(8,128)S(1)}, s32[96,256]{1,0:T(8,128)}, u32[]{:S(2)}) %copy-start.4) | copy-done | bytes 98328
  5.4 0.0 copy-start.5
  5.4 0.9 %copy-done.5 = s32[96,256]{1,0:T(8,128)S(1)} copy-done((s32[96,256]{1,0:T(8,128)S(1)}, s32[96,256]{1,0:T(8,128)}, u32[]{:S(2)}) %copy-start.5) | copy-done | bytes 98328
  6.3 0.0 copy-start.6
  6.3 0.9 %copy-done.6 = f32[96,256]{1,0:T(8,128)S(1)} copy-done((f32[96,256]{1,0:T(8,128)S(1)}, f32[96,256]{1,0:T(8,128)}, u32[]{:S(2)}) %copy-start.6) | copy-done | bytes 98328
  7.2 0.0 copy-start.7
  7.2 0.9 %copy-done.7 = f32[96,256]{1,0:T(8,128)S(1)} copy-done((f32[96,256]{1,0:T(8,128)S(1)}, f32[96,256]{1,0:T(8,128)}, u32[]{:S(2)}) %copy-start.7) | copy-done | bytes 98328
  8.1 0.0 copy-start.8
  8.1 0.9 %copy-done.8 = f32[96,256]{1,0:T(8,128)S(1)} copy-done((f32[96,256]{1,0:T(8,128)S(1)}, f32[96,256]{1,0:T(8,128)}, u32[]{:S(2)}) %copy-start.8) | copy-done | bytes 98328
  8.9 0.5 %pack_columns.1 = (f32[96,128]{1,0:T(8,128)S(1)}, f32[96,128]{1,0:T(8,128)S(1)}) custom-call(f32[3,96,256]{2,1,0:T(8,128)S(1)} %copy-done, f32[3,96,256]{2,1,0:T(8,128)S(1)} %copy-done.1, f32[3,96,256]{2,1,0:T(8,128)S(1)} %copy-done.2, f32[3,96,256]{2,1,0:T(8,128)S(1)} %copy-done.3, s32[96,256]{1,0:T(8,128)S(1)} %copy-done.4, s32[96,256]{1,0:T(8,128)S(1)} %copy-done.5, ...), custom_call_target="tpu_custom_call" | custom-call | tf_op jit(solution)/shard_map/pack_columns/pallas_call | solution.py:312
  9.4 0.1 collective-permute-start
  9.5 7.5 %collective-permute-start.1 = (f32[96,128]{1,0:T(8,128)S(1)}, f32[96,128]{1,0:T(8,128)S(1)}, u32[]{:S(2)}, u32[]{:S(2)}) collective-permute-start(f32[96,128]{1,0:T(8,128)S(1)} %get-tuple-element.9), channel_id=1, source_target_pairs={{0,248},{1,249},{2,250},{3,251},{4,252},{5,253},{6,254},{7,255},{8... | collective-permute-start | bytes 147464 | tf_op jit(solution)/shard_map/ppermute | solution.py:316
  17.1 0.0 collective-permute-done.refs_18_.refs_9_
  17.1 1.8 %collective-permute-done.1.refs_19_.refs_10_ = f32[96,128]{1,0:T(8,128)S(1)} collective-permute-done((f32[96,128]{1,0:T(8,128)S(1)}, f32[96,128]{1,0:T(8,128)S(1)}, u32[]{:S(2)}, u32[]{:S(2)}) %collective-permute-start.1) | collective-permute-done | bytes 49184 | tf_op jit(solution)/shard_map/ppermute | solution.py:316
  18.9 1.5 %collective-permute-start.2 = (f32[72,256]{1,0:T(8,128)S(1)}, f32[72,256]{1,0:T(8,128)S(1)}, u32[]{:S(2)}, u32[]{:S(2)}) collective-permute-start(f32[72,256]{1,0:T(8,128)S(1)} %get-tuple-element.10), channel_id=1, source_target_pairs={{0,1},{1,0},{2,3},{3,2},{4,5},{5,4},{6,7},{7,6},{8,9},{9,8},{10,11... | collective-permute-start | bytes 221192 | tf_op jit(solution)/shard_map/ppermute | solution.py:340
  20.4 6.4 %collective-permute-start.3 = (f32[72,256]{1,0:T(8,128)S(1)}, f32[72,256]{1,0:T(8,128)S(1)}, u32[]{:S(2)}, u32[]{:S(2)}) collective-permute-start(f32[72,256]{1,0:T(8,128)S(1)} %get-tuple-element.11), channel_id=1, source_target_pairs={{1,2},{2,1},{3,4},{4,3},{5,6},{6,5},{7,255},{9,10},{10,9},{11,12},... | collective-permute-start | bytes 221192 | tf_op jit(solution)/shard_map/ppermute | solution.py:339
  26.8 0.0 collective-permute-done.2.refs_11_
  26.8 2.9 %collective-permute-done.3.refs_12_ = f32[72,256]{1,0:T(8,128)S(1)} collective-permute-done((f32[72,256]{1,0:T(8,128)S(1)}, f32[72,256]{1,0:T(8,128)S(1)}, u32[]{:S(2)}, u32[]{:S(2)}) %collective-permute-start.3) | collective-permute-done | bytes 73760 | tf_op jit(solution)/shard_map/ppermute | solution.py:339
  29.7 17.7 %run_steps.1 = (f32[3,96,256]{2,1,0:T(8,128)}, f32[3,96,256]{2,1,0:T(8,128)}, f32[3,96,256]{2,1,0:T(8,128)}, f32[3,96,256]{2,1,0:T(8,128)}) custom-call(f32[3,96,256]{2,1,0:T(8,128)S(1)} %copy-done, f32[3,96,256]{2,1,0:T(8,128)S(1)} %copy-done.1, f32[3,96,256]{2,1,0:T(8,128)S(1)} %copy-done.2, f32[3,96,256]{2,1,0:T(8,128)S(1)} %copy-done.3, ...), custom_call_target="tpu_custom_call" | custom-call | tf_op jit(solution)/shard_map/run_steps/pallas_call | solution.py:343
  (1 shorter events, 0.0 us)
Async XLA Ops:
  0.6 1.0 %copy-start = (f32[3,96,256]{2,1,0:T(8,128)S(1)}, f32[3,96,256]{2,1,0:T(8,128)}, u32[]{:S(2)}) copy-start(f32[3,96,256]{2,1,0:T(8,128)} %refs_0_.5) | copy-start | bytes 884740
  1.6 1.0 %copy-start.1 = (f32[3,96,256]{2,1,0:T(8,128)S(1)}, f32[3,96,256]{2,1,0:T(8,128)}, u32[]{:S(2)}) copy-start(f32[3,96,256]{2,1,0:T(8,128)} %refs_1_.5) | copy-start | bytes 884740
  2.6 1.0 %copy-start.2 = (f32[3,96,256]{2,1,0:T(8,128)S(1)}, f32[3,96,256]{2,1,0:T(8,128)}, u32[]{:S(2)}) copy-start(f32[3,96,256]{2,1,0:T(8,128)} %refs_2_.5) | copy-start | bytes 884740
  3.5 1.0 %copy-start.3 = (f32[3,96,256]{2,1,0:T(8,128)S(1)}, f32[3,96,256]{2,1,0:T(8,128)}, u32[]{:S(2)}) copy-start(f32[3,96,256]{2,1,0:T(8,128)} %refs_3_.5) | copy-start | bytes 884740
  4.5 0.9 %copy-start.4 = (s32[96,256]{1,0:T(8,128)S(1)}, s32[96,256]{1,0:T(8,128)}, u32[]{:S(2)}) copy-start(s32[96,256]{1,0:T(8,128)} %refs_4_.5) | copy-start | bytes 294916
  5.4 0.9 %copy-start.5 = (s32[96,256]{1,0:T(8,128)S(1)}, s32[96,256]{1,0:T(8,128)}, u32[]{:S(2)}) copy-start(s32[96,256]{1,0:T(8,128)} %refs_5_.5) | copy-start | bytes 294916
  6.3 0.9 %copy-start.6 = (f32[96,256]{1,0:T(8,128)S(1)}, f32[96,256]{1,0:T(8,128)}, u32[]{:S(2)}) copy-start(f32[96,256]{1,0:T(8,128)} %refs_6_.5) | copy-start | bytes 294916
  7.2 0.9 %copy-start.7 = (f32[96,256]{1,0:T(8,128)S(1)}, f32[96,256]{1,0:T(8,128)}, u32[]{:S(2)}) copy-start(f32[96,256]{1,0:T(8,128)} %refs_7_.5) | copy-start | bytes 294916
  8.1 0.9 %copy-start.8 = (f32[96,256]{1,0:T(8,128)S(1)}, f32[96,256]{1,0:T(8,128)}, u32[]{:S(2)}) copy-start(f32[96,256]{1,0:T(8,128)} %refs_8_.5) | copy-start | bytes 294916
  9.4 7.6 %collective-permute-start = (f32[96,128]{1,0:T(8,128)S(1)}, f32[96,128]{1,0:T(8,128)S(1)}, u32[]{:S(2)}, u32[]{:S(2)}) collective-permute-start(f32[96,128]{1,0:T(8,128)S(1)} %get-tuple-element.8), channel_id=1, source_target_pairs={{0,8},{1,9},{2,10},{3,11},{4,12},{5,13},{6,14},{7,15},{8,0},{9,1},... | collective-permute-start | bytes 147464 | tf_op jit(solution)/shard_map/ppermute | solution.py:315
  9.5 9.3 %collective-permute-start.1 = (f32[96,128]{1,0:T(8,128)S(1)}, f32[96,128]{1,0:T(8,128)S(1)}, u32[]{:S(2)}, u32[]{:S(2)}) collective-permute-start(f32[96,128]{1,0:T(8,128)S(1)} %get-tuple-element.9), channel_id=1, source_target_pairs={{0,248},{1,249},{2,250},{3,251},{4,252},{5,253},{6,254},{7,255},{8... | collective-permute-start | bytes 147464 | tf_op jit(solution)/shard_map/ppermute | solution.py:316
  18.9 7.9 %collective-permute-start.2 = (f32[72,256]{1,0:T(8,128)S(1)}, f32[72,256]{1,0:T(8,128)S(1)}, u32[]{:S(2)}, u32[]{:S(2)}) collective-permute-start(f32[72,256]{1,0:T(8,128)S(1)} %get-tuple-element.10), channel_id=1, source_target_pairs={{0,1},{1,0},{2,3},{3,2},{4,5},{5,4},{6,7},{7,6},{8,9},{9,8},{10,11... | collective-permute-start | bytes 221192 | tf_op jit(solution)/shard_map/ppermute | solution.py:340
  20.4 9.3 %collective-permute-start.3 = (f32[72,256]{1,0:T(8,128)S(1)}, f32[72,256]{1,0:T(8,128)S(1)}, u32[]{:S(2)}, u32[]{:S(2)}) collective-permute-start(f32[72,256]{1,0:T(8,128)S(1)} %get-tuple-element.11), channel_id=1, source_target_pairs={{1,2},{2,1},{3,4},{4,3},{5,6},{6,5},{7,255},{9,10},{10,9},{11,12},... | collective-permute-start | bytes 221192 | tf_op jit(solution)/shard_map/ppermute | solution.py:339

commit v2 on v1

--- a/solution.py
+++ b/solution.py
@@ -26,10 +26,14 @@
     return lax.broadcasted_iota(jnp.int32, shape, len(shape) - 1)
 
 
-def pack_columns(*refs):
-    ins, (out_a, out_b) = refs[:9], refs[9:]
-    rows = ins[0].shape[1]
-    cols = ins[0].shape[2]
+def pack_edges(*refs):
+    args, (col_a, col_b, row_a, row_b), ins, sems = refs[:9], refs[9:13], refs[13:22], refs[22]
+    copies = [pltpu.make_async_copy(a, i, sems.at[n]) for n, (a, i) in enumerate(zip(args, ins))]
+    for copy in copies:
+        copy.start()
+    for copy in copies:
+        copy.wait()
+    rows, cols = ins[4].shape
     even = lax.rem(lax.axis_index("lon"), 2) == 0
     lane = lane_index((8, LANES))
     for r in range(0, rows, 8):
@@ -44,20 +48,21 @@
             else:
                 mine = lane >= 4 * p
                 west, east = jnp.where(mine, w, west), jnp.where(mine, e, east)
-        out_a[r : r + 8, :] = jnp.where(even, east, west)
-        out_b[r : r + 8, :] = jnp.where(even, west, east)
-
-
-def pack_rows(*refs):
-    south, north = refs[0:9], refs[9:18]
-    col_a, col_b, out_a, out_b = refs[18:]
+        col_a[r : r + 8, :] = jnp.where(even, east, west)
+        col_b[r : r + 8, :] = jnp.where(even, west, east)
+    even = lax.rem(lax.axis_index("lat"), 2) == 0
+    for p in range(PLANES):
+        s = plane_values(ins, p, slice(0, 8), slice(None))[:HALO]
+        n = plane_values(ins, p, slice(rows - 8, rows), slice(None))[HALO:]
+        row_a[4 * p : 4 * p + 4, :] = jnp.where(even, n, s)
+        row_b[4 * p : 4 * p + 4, :] = jnp.where(even, s, n)
+
+
+def add_corners(col_a, col_b, in_a, in_b, out_a, out_b):
     rows = col_a.shape[0]
     even = lax.rem(lax.axis_index("lat"), 2) == 0
-    for p in range(PLANES):
-        s = plane_values(south, p, slice(0, 8), slice(None))[:HALO]
-        n = plane_values(north, p, slice(0, 8), slice(None))[HALO:]
-        out_a[4 * p : 4 * p + 4, :] = jnp.where(even, n, s)
-        out_b[4 * p : 4 * p + 4, :] = jnp.where(even, s, n)
+    out_a[...] = in_a[...]
+    out_b[...] = in_b[...]
     for ref, lanes in ((col_a, slice(0, LANES)), (col_b, slice(LANES, 2 * LANES))):
         s = ref[0:HALO, :]
         n = ref[rows - HALO : rows, :]
@@ -120,42 +125,45 @@
     first, last = lane == 0, lane == LANES - 1
     above = [None] * 3
     for k in range(K):
-        def load(f, shift):
-            return [field[src, f, k, t, pl.ds(r + shift, 8), :] for t in range(3)]
-
-        c = [load(f, 0) for f in range(5)]
-        n = [load(f, 1) for f in range(5)]
-        s = [load(f, -1) for f in range(5)]
-        e = [shift_east(x, last) for x in c]
-        w = [shift_west(x, first) for x in c]
         for t in range(3):
             def get(i):
                 return coef[i, k, t, pl.ds(r, 8), :]
 
+            def fld(f, shift=0, tt=t):
+                return field[src, f, k, tt, pl.ds(r + shift, 8), :]
+
+            def around(f):
+                c = fld(f)
+                e = pltpu.roll(jnp.where(first, fld(f, 0, (t + 1) % 3), c), LANES - 1, 1)
+                w = pltpu.roll(jnp.where(last, fld(f, 0, (t + 2) % 3), c), 1, 1)
+                return c, e, w, fld(f, 1), fld(f, -1)
+
             cxe, cxw, cyn, cys = get(CXE), get(CXW), get(CYN), get(CYS)
             hxe, hxw, hyn, hys = get(HXE), get(HXW), get(HYN), get(HYS)
-            u, v = c[U][t], c[V][t]
+            U5, V5 = around(U), around(V)
+            u, v = U5[0], V5[0]
             u2, v2 = u + u, v + v
             ae, aw = cxe - hxe * u2, cxw + hxw * u2
             an, as_ = cyn - hyn * v2, cys + hys * v2
             ac = get(WET) - ((ae + aw) + (an + as_))
             wcor = get(WCOR)
-            p = c[PR][t]
-            px = hxe * (e[PR][t] - p) + hxw * (p - w[PR][t])
-            py = hyn * (n[PR][t] - p) + hys * (p - s[PR][t])
-
-            def combine(f, ac, ae, aw, an, as_):
-                return (ac * c[f][t] + (ae * e[f][t] + aw * w[f][t])) + (an * n[f][t] + as_ * s[f][t])
-
-            write(U, k, t, combine(U, ac, ae, aw, an, as_) + (wcor * v - px))
-            write(V, k, t, combine(V, ac, ae, aw, an, as_) - (wcor * u + py))
-            ae = cxe - hxe * (u + e[U][t])
-            aw = cxw + hxw * (u + w[U][t])
-            an = cyn - hyn * (v + n[V][t])
-            as_ = cys + hys * (v + s[V][t])
+            p, pe, pw, pn, ps = around(PR)
+            px = hxe * (pe - p) + hxw * (p - pw)
+            py = hyn * (pn - p) + hys * (p - ps)
+
+            def combine(X5, ac, ae, aw, an, as_):
+                c, e, w, n, s = X5
+                return (ac * c + (ae * e + aw * w)) + (an * n + as_ * s)
+
+            write(U, k, t, combine(U5, ac, ae, aw, an, as_) + (wcor * v - px))
+            write(V, k, t, combine(V5, ac, ae, aw, an, as_) - (wcor * u + py))
+            ae = cxe - hxe * (u + U5[1])
+            aw = cxw + hxw * (u + U5[2])
+            an = cyn - hyn * (v + V5[3])
+            as_ = cys + hys * (v + V5[4])
             ac = get(WCEN) + ((ae + aw) + (an + as_))
-            t_new = combine(T, ac, ae, aw, an, as_)
-            s_new = combine(S, ac, ae, aw, an, as_)
+            t_new = combine(around(T), ac, ae, aw, an, as_)
+            s_new = combine(around(S), ac, ae, aw, an, as_)
             write(T, k, t, t_new)
             write(S, k, t, s_new)
             rho = density(t_new, s_new, k)
@@ -309,33 +317,25 @@
     params = pltpu.CompilerParams(vmem_limit_bytes=VMEM_LIMIT)
     f32 = jnp.float32
     column = jax.ShapeDtypeStruct((rows, LANES), f32)
-    col_a, col_b = pl.pallas_call(
-        pack_columns, out_shape=(column, column), compiler_params=params, name="pack_columns"
+    row = jax.ShapeDtypeStruct((4 * PLANES + 4, cols), f32)
+    col_a, col_b, row_a, row_b = pl.pallas_call(
+        pack_edges,
+        in_specs=[pl.BlockSpec(memory_space=pltpu.HBM)] * 9,
+        out_shape=(column, column, row, row),
+        scratch_shapes=[pltpu.VMEM(a.shape, a.dtype) for a in args] + [pltpu.SemaphoreType.DMA((9,))],
+        compiler_params=pltpu.CompilerParams(vmem_limit_bytes=62 * 1024 * 1024),
+        name="pack_edges",
     )(*args)
     col_a = lax.ppermute(col_a, axes, lon_pairs(nlon, nlat, lambda i: i ^ 1))
     col_b = lax.ppermute(
         col_b, axes, lon_pairs(nlon, nlat, lambda i: (i + 1 if i % 2 else i - 1) % nlon)
     )
-
-    def edge(block):
-        def spec(a):
-            if a.ndim == 3:
-                return pl.BlockSpec((K, 8, cols), lambda i: (0, block, 0))
-            return pl.BlockSpec((8, cols), lambda i: (block, 0))
-        return [spec(a) for a in args]
-
-    whole = pl.BlockSpec((rows, LANES), lambda i: (0, 0))
-    row = jax.ShapeDtypeStruct((4 * PLANES + 4, cols), f32)
-    row_spec = pl.BlockSpec(row.shape, lambda i: (0, 0))
     row_a, row_b = pl.pallas_call(
-        pack_rows,
-        grid=(1,),
-        in_specs=edge(0) + edge(rows // 8 - 1) + [whole, whole],
-        out_specs=(row_spec, row_spec),
+        add_corners,
         out_shape=(row, row),
         compiler_params=params,
-        name="pack_rows",
-    )(*args, *args, col_a, col_b)
+        name="add_corners",
+    )(col_a, col_b, row_a, row_b)
     row_b = lax.ppermute(row_b, axes, lat_pairs(nlon, nlat, True))
     row_a = lax.ppermute(row_a, axes, lat_pairs(nlon, nlat, False))
     tall = rows + 32

time: 47.7 us -> 42.5 us (0.89)
  local copies, waits for them, and re-layouts: 8.3 us -> 1.8 us
  Pallas kernels: 18.2 us -> 19.3 us
    unnamed x18 -> x22, local copies, waits for them, and re-layouts: 8.3 us -> 1.8 us
    pallas_call x2, Pallas kernels: 0.52 us -> 2.71 us  [the longest x1 2.7 us: body(): pl.pallas_call(pack_edges, in_specs=[pl.BlockSpec(memory_space=pltpu.HBM)...]
    pallas_call x1, Pallas kernels: 17.7 us -> 16.5 us  [body(): pl.pallas_call(run_steps, out_shape=(out,) * 4, scratch_shapes=[pltpu.VME...]
where the time goes in v2:
time: 42.5 us; the launch traced here: 42.3 us
  Pallas kernels  19.3 us (45%)
  starting transfers between devices  15.4 us (36%)
  waiting for transfers between devices  5.04 us (12%)
  local copies, waits for them, and re-layouts  1.8 us (4%)
  between operations  0.78 us (2%)
    pallas_call x1, Pallas kernels, body(): pl.pallas_call(run_steps, out_shape=(out,) * 4, scratch_shapes=[pltpu.VME...  16.5 us
    ppermute x1, starting transfers between devices, body(): lax.ppermute(col_b, axes, lon_pairs(nlon, nlat, lambda i: (i + 1 if i % 2...  7.52 us
    ppermute x1, starting transfers between devices, body(): row_b = lax.ppermute(row_b, axes, lat_pairs(nlon, nlat, True))  6.28 us
    ppermute x1, waiting for transfers between devices, body(): row_b = lax.ppermute(row_b, axes, lat_pairs(nlon, nlat, True))  2.97 us
    pallas_call x1, Pallas kernels, body(): pl.pallas_call(pack_edges, in_specs=[pl.BlockSpec(memory_space=pltpu.HBM)...  2.7 us
    ppermute x1, waiting for transfers between devices, body(): lax.ppermute(col_b, axes, lon_pairs(nlon, nlat, lambda i: (i + 1 if i % 2...  2.06 us
    unnamed x22, local copies, waits for them, and re-layouts  1.8 us
    ppermute x1, starting transfers between devices, body(): row_a = lax.ppermute(row_a, axes, lat_pairs(nlon, nlat, False))  1.52 us
  transfers between devices with their start and end apart: 4, of which 2 were waited for; matrix products, arithmetic and copies ran while one was open for 0% of the time, Pallas kernels for 0%

profile of v2, /device:TPU:26, one launch (start us, length us, event | category | flops | bytes accessed | tf_op | source)
XLA Modules:
  0.0 42.3 jit_solution(17712672245635961866)
XLA Ops:
  0.6 0.0 copy-start
  0.6 0.0 copy-start.1
  0.7 0.0 copy-start.2
  0.7 0.0 copy-start.3
  0.7 0.0 copy-start.6
  0.7 0.0 copy-start.7
  0.7 0.0 copy-start.8
  0.7 2.7 %pack_edges.1 = (f32[96,128]{1,0:T(8,128)}, f32[96,128]{1,0:T(8,128)}, f32[72,256]{1,0:T(8,128)}, f32[72,256]{1,0:T(8,128)}) custom-call(f32[3,96,256]{2,1,0:T(8,128)} %refs_0_.3, f32[3,96,256]{2,1,0:T(8,128)} %refs_1_.3, f32[3,96,256]{2,1,0:T(8,128)} %refs_2_.3, f32[3,96,256]{2,1,0:T(8,128)} %refs_3_.3, s32[96,256]{1,0:T(8,128)} %refs_4_.3, ...), custom_call_target="tpu_custom_call" | custom-call | tf_op jit(solution)/shard_map/pack_edges/pallas_call | solution.py:321
  3.4 0.1 collective-permute-start
  3.5 7.5 %collective-permute-start.1 = (f32[96,128]{1,0:T(8,128)}, f32[96,128]{1,0:T(8,128)S(1)}, u32[]{:S(2)}, u32[]{:S(2)}) collective-permute-start(f32[96,128]{1,0:T(8,128)} %get-tuple-element.11), channel_id=1, source_target_pairs={{0,248},{1,249},{2,250},{3,251},{4,252},{5,253},{6,254},{7,255},{8... | collective-permute-start | bytes 147464 | tf_op jit(solution)/shard_map/ppermute | solution.py:330
  11.0 0.0 collective-permute-done.col_a.refs_9_
  11.0 2.1 %collective-permute-done.1.col_b.refs_10_ = f32[96,128]{1,0:T(8,128)S(1)} collective-permute-done((f32[96,128]{1,0:T(8,128)}, f32[96,128]{1,0:T(8,128)S(1)}, u32[]{:S(2)}, u32[]{:S(2)}) %collective-permute-start.1) | collective-permute-done | bytes 49184 | tf_op jit(solution)/shard_map/ppermute | solution.py:330
  13.1 0.0 copy-start.9
  13.1 0.9 %copy-done.9 = f32[72,256]{1,0:T(8,128)S(1)} copy-done((f32[72,256]{1,0:T(8,128)S(1)}, f32[72,256]{1,0:T(8,128)}, u32[]{:S(2)}) %copy-start.9) | copy-done | bytes 73752
  14.0 0.0 copy-start.10
  14.0 0.9 %copy-done.10 = f32[72,256]{1,0:T(8,128)S(1)} copy-done((f32[72,256]{1,0:T(8,128)S(1)}, f32[72,256]{1,0:T(8,128)}, u32[]{:S(2)}) %copy-start.10) | copy-done | bytes 73752
  14.9 0.0 copy-start.4
  14.9 0.0 copy-start.5
  14.9 1.5 %collective-permute-start.2 = (f32[72,256]{1,0:T(8,128)S(1)}, f32[72,256]{1,0:T(8,128)S(1)}, u32[]{:S(2)}, u32[]{:S(2)}) collective-permute-start(f32[72,256]{1,0:T(8,128)S(1)} %get-tuple-element.14), channel_id=1, source_target_pairs={{0,1},{1,0},{2,3},{3,2},{4,5},{5,4},{6,7},{7,6},{8,9},{9,8},{10,11... | collective-permute-start | bytes 221192 | tf_op jit(solution)/shard_map/ppermute | solution.py:340
  16.4 6.3 %collective-permute-start.3 = (f32[72,256]{1,0:T(8,128)S(1)}, f32[72,256]{1,0:T(8,128)S(1)}, u32[]{:S(2)}, u32[]{:S(2)}) collective-permute-start(f32[72,256]{1,0:T(8,128)S(1)} %get-tuple-element.15), channel_id=1, source_target_pairs={{1,2},{2,1},{3,4},{4,3},{5,6},{6,5},{7,255},{9,10},{10,9},{11,12},... | collective-permute-start | bytes 221192 | tf_op jit(solution)/shard_map/ppermute | solution.py:339
  22.7 0.0 collective-permute-done.2.refs_11_
  22.7 3.0 %collective-permute-done.3.refs_12_ = f32[72,256]{1,0:T(8,128)S(1)} collective-permute-done((f32[72,256]{1,0:T(8,128)S(1)}, f32[72,256]{1,0:T(8,128)S(1)}, u32[]{:S(2)}, u32[]{:S(2)}) %collective-permute-start.3) | collective-permute-done | bytes 73760 | tf_op jit(solution)/shard_map/ppermute | solution.py:339
  25.7 0.0 copy-done
  25.7 0.0 copy-done.1
  25.7 0.0 copy-done.2
  25.7 0.0 copy-done.3
  25.7 0.0 copy-done.6
  25.7 0.0 copy-done.7
  25.7 0.0 copy-done.8
  25.7 0.0 copy-done.4
  25.7 0.0 copy-done.5
  25.8 16.5 %run_steps.1 = (f32[3,96,256]{2,1,0:T(8,128)}, f32[3,96,256]{2,1,0:T(8,128)}, f32[3,96,256]{2,1,0:T(8,128)}, f32[3,96,256]{2,1,0:T(8,128)}) custom-call(f32[3,96,256]{2,1,0:T(8,128)S(1)} %copy-done, f32[3,96,256]{2,1,0:T(8,128)S(1)} %copy-done.1, f32[3,96,256]{2,1,0:T(8,128)S(1)} %copy-done.2, f32[3,96,256]{2,1,0:T(8,128)S(1)} %copy-done.3, ...), custom_call_target="tpu_custom_call" | custom-call | tf_op jit(solution)/shard_map/run_steps/pallas_call | solution.py:343
  (1 shorter events, 0.0 us)
Async XLA Ops:
  0.6 25.1 %copy-start = (f32[3,96,256]{2,1,0:T(8,128)S(1)}, f32[3,96,256]{2,1,0:T(8,128)}, u32[]{:S(2)}) copy-start(f32[3,96,256]{2,1,0:T(8,128)} %refs_0_.3) | copy-start | bytes 884740
  0.6 25.0 %copy-start.1 = (f32[3,96,256]{2,1,0:T(8,128)S(1)}, f32[3,96,256]{2,1,0:T(8,128)}, u32[]{:S(2)}) copy-start(f32[3,96,256]{2,1,0:T(8,128)} %refs_1_.3) | copy-start | bytes 884740
  0.7 25.0 %copy-start.2 = (f32[3,96,256]{2,1,0:T(8,128)S(1)}, f32[3,96,256]{2,1,0:T(8,128)}, u32[]{:S(2)}) copy-start(f32[3,96,256]{2,1,0:T(8,128)} %refs_2_.3) | copy-start | bytes 884740
  0.7 25.0 %copy-start.3 = (f32[3,96,256]{2,1,0:T(8,128)S(1)}, f32[3,96,256]{2,1,0:T(8,128)}, u32[]{:S(2)}) copy-start(f32[3,96,256]{2,1,0:T(8,128)} %refs_3_.3) | copy-start | bytes 884740
  0.7 25.0 %copy-start.6 = (f32[96,256]{1,0:T(8,128)S(1)}, f32[96,256]{1,0:T(8,128)}, u32[]{:S(2)}) copy-start(f32[96,256]{1,0:T(8,128)} %refs_6_.3) | copy-start | bytes 294916
  0.7 25.0 %copy-start.7 = (f32[96,256]{1,0:T(8,128)S(1)}, f32[96,256]{1,0:T(8,128)}, u32[]{:S(2)}) copy-start(f32[96,256]{1,0:T(8,128)} %refs_7_.3) | copy-start | bytes 294916
  0.7 25.0 %copy-start.8 = (f32[96,256]{1,0:T(8,128)S(1)}, f32[96,256]{1,0:T(8,128)}, u32[]{:S(2)}) copy-start(f32[96,256]{1,0:T(8,128)} %refs_8_.3) | copy-start | bytes 294916
  3.4 7.6 %collective-permute-start = (f32[96,128]{1,0:T(8,128)}, f32[96,128]{1,0:T(8,128)S(1)}, u32[]{:S(2)}, u32[]{:S(2)}) collective-permute-start(f32[96,128]{1,0:T(8,128)} %get-tuple-element.10), channel_id=1, source_target_pairs={{0,8},{1,9},{2,10},{3,11},{4,12},{5,13},{6,14},{7,15},{8,0},{9,1},... | collective-permute-start | bytes 147464 | tf_op jit(solution)/shard_map/ppermute | solution.py:329
  3.5 9.6 %collective-permute-start.1 = (f32[96,128]{1,0:T(8,128)}, f32[96,128]{1,0:T(8,128)S(1)}, u32[]{:S(2)}, u32[]{:S(2)}) collective-permute-start(f32[96,128]{1,0:T(8,128)} %get-tuple-element.11), channel_id=1, source_target_pairs={{0,248},{1,249},{2,250},{3,251},{4,252},{5,253},{6,254},{7,255},{8... | collective-permute-start | bytes 147464 | tf_op jit(solution)/shard_map/ppermute | solution.py:330
  13.1 0.9 %copy-start.9 = (f32[72,256]{1,0:T(8,128)S(1)}, f32[72,256]{1,0:T(8,128)}, u32[]{:S(2)}) copy-start(f32[72,256]{1,0:T(8,128)} %get-tuple-element.12.in_a) | copy-start | bytes 221188
  14.0 0.9 %copy-start.10 = (f32[72,256]{1,0:T(8,128)S(1)}, f32[72,256]{1,0:T(8,128)}, u32[]{:S(2)}) copy-start(f32[72,256]{1,0:T(8,128)} %get-tuple-element.13.in_b) | copy-start | bytes 221188
  14.9 10.9 %copy-start.4 = (s32[96,256]{1,0:T(8,128)S(1)}, s32[96,256]{1,0:T(8,128)}, u32[]{:S(2)}) copy-start(s32[96,256]{1,0:T(8,128)} %refs_4_.3) | copy-start | bytes 294916
  14.9 10.9 %copy-start.5 = (s32[96,256]{1,0:T(8,128)S(1)}, s32[96,256]{1,0:T(8,128)}, u32[]{:S(2)}) copy-start(s32[96,256]{1,0:T(8,128)} %refs_5_.3) | copy-start | bytes 294916
  14.9 7.8 %collective-permute-start.2 = (f32[72,256]{1,0:T(8,128)S(1)}, f32[72,256]{1,0:T(8,128)S(1)}, u32[]{:S(2)}, u32[]{:S(2)}) collective-permute-start(f32[72,256]{1,0:T(8,128)S(1)} %get-tuple-element.14), channel_id=1, source_target_pairs={{0,1},{1,0},{2,3},{3,2},{4,5},{5,4},{6,7},{7,6},{8,9},{9,8},{10,11... | collective-permute-start | bytes 221192 | tf_op jit(solution)/shard_map/ppermute | solution.py:340
  16.4 9.3 %collective-permute-start.3 = (f32[72,256]{1,0:T(8,128)S(1)}, f32[72,256]{1,0:T(8,128)S(1)}, u32[]{:S(2)}, u32[]{:S(2)}) collective-permute-start(f32[72,256]{1,0:T(8,128)S(1)} %get-tuple-element.15), channel_id=1, source_target_pairs={{1,2},{2,1},{3,4},{4,3},{5,6},{6,5},{7,255},{9,10},{10,9},{11,12},... | collective-permute-start | bytes 221192 | tf_op jit(solution)/shard_map/ppermute | solution.py:339

commit v3 on v2

--- a/solution.py
+++ b/solution.py
@@ -26,43 +26,42 @@
     return lax.broadcasted_iota(jnp.int32, shape, len(shape) - 1)
 
 
-def pack_edges(*refs):
-    args, (col_a, col_b, row_a, row_b), ins, sems = refs[:9], refs[9:13], refs[13:22], refs[22]
+def pack_columns(*refs):
+    args, (out_b, out_a), ins, sems = refs[:9], refs[9:11], refs[11:20], refs[20]
     copies = [pltpu.make_async_copy(a, i, sems.at[n]) for n, (a, i) in enumerate(zip(args, ins))]
     for copy in copies:
         copy.start()
-    for copy in copies:
-        copy.wait()
     rows, cols = ins[4].shape
     even = lax.rem(lax.axis_index("lon"), 2) == 0
     lane = lane_index((8, LANES))
-    for r in range(0, rows, 8):
-        west = east = None
-        for p in range(PLANES):
+    blocks = range(0, rows, 8)
+    west, east = {}, {}
+    for p in range(PLANES):
+        if p % 3 == 0 or p > 12:
+            copies[p // 3 if p < 12 else p - 8].wait()
+        for r in blocks:
             w = plane_values(ins, p, slice(r, r + 8), slice(0, LANES))
             e = plane_values(ins, p, slice(r, r + 8), slice(cols - LANES, cols))
             w = pltpu.roll(w, 4 * p, 1) if p else w
             e = pltpu.roll(e, (4 * p + HALO) % LANES, 1)
-            if p == 0:
-                west, east = w, e
-            else:
-                mine = lane >= 4 * p
-                west, east = jnp.where(mine, w, west), jnp.where(mine, e, east)
-        col_a[r : r + 8, :] = jnp.where(even, east, west)
-        col_b[r : r + 8, :] = jnp.where(even, west, east)
+            mine = lane >= 4 * p
+            west[r] = jnp.where(mine, w, west[r]) if p else w
+            east[r] = jnp.where(mine, e, east[r]) if p else e
+    for r in blocks:
+        out_a[r : r + 8, :] = jnp.where(even, east[r], west[r])
+        out_b[r : r + 8, :] = jnp.where(even, west[r], east[r])
+
+
+def pack_rows(*refs):
+    south, north = refs[0:9], refs[9:18]
+    col_b, col_a, out_b, out_a = refs[18:]
+    rows = col_a.shape[0]
     even = lax.rem(lax.axis_index("lat"), 2) == 0
     for p in range(PLANES):
-        s = plane_values(ins, p, slice(0, 8), slice(None))[:HALO]
-        n = plane_values(ins, p, slice(rows - 8, rows), slice(None))[HALO:]
-        row_a[4 * p : 4 * p + 4, :] = jnp.where(even, n, s)
-        row_b[4 * p : 4 * p + 4, :] = jnp.where(even, s, n)
-
-
-def add_corners(col_a, col_b, in_a, in_b, out_a, out_b):
-    rows = col_a.shape[0]
-    even = lax.rem(lax.axis_index("lat"), 2) == 0
-    out_a[...] = in_a[...]
-    out_b[...] = in_b[...]
+        s = plane_values(south, p, slice(0, 8), slice(None))[:HALO]
+        n = plane_values(north, p, slice(0, 8), slice(None))[HALO:]
+        out_a[4 * p : 4 * p + 4, :] = jnp.where(even, n, s)
+        out_b[4 * p : 4 * p + 4, :] = jnp.where(even, s, n)
     for ref, lanes in ((col_a, slice(0, LANES)), (col_b, slice(LANES, 2 * LANES))):
         s = ref[0:HALO, :]
         n = ref[rows - HALO : rows, :]
@@ -173,7 +172,7 @@
 
 
 def run_steps(*refs):
-    ins, (col_a, col_b, row_a, row_b), outs = refs[:9], refs[9:13], refs[13:17]
+    ins, (col_b, col_a, row_b, row_a), outs = refs[:9], refs[9:13], refs[13:17]
     field, coef, wet, geo, cols, north = refs[17:]
     rows = ins[0].shape[1]
     top = OFFSET + rows
@@ -317,25 +316,38 @@
     params = pltpu.CompilerParams(vmem_limit_bytes=VMEM_LIMIT)
     f32 = jnp.float32
     column = jax.ShapeDtypeStruct((rows, LANES), f32)
-    row = jax.ShapeDtypeStruct((4 * PLANES + 4, cols), f32)
-    col_a, col_b, row_a, row_b = pl.pallas_call(
-        pack_edges,
+    col_b, col_a = pl.pallas_call(
+        pack_columns,
         in_specs=[pl.BlockSpec(memory_space=pltpu.HBM)] * 9,
-        out_shape=(column, column, row, row),
+        out_shape=(column, column),
         scratch_shapes=[pltpu.VMEM(a.shape, a.dtype) for a in args] + [pltpu.SemaphoreType.DMA((9,))],
         compiler_params=pltpu.CompilerParams(vmem_limit_bytes=62 * 1024 * 1024),
-        name="pack_edges",
+        name="pack_columns",
     )(*args)
-    col_a = lax.ppermute(col_a, axes, lon_pairs(nlon, nlat, lambda i: i ^ 1))
     col_b = lax.ppermute(
         col_b, axes, lon_pairs(nlon, nlat, lambda i: (i + 1 if i % 2 else i - 1) % nlon)
     )
-    row_a, row_b = pl.pallas_call(
-        add_corners,
+    col_a = lax.ppermute(col_a, axes, lon_pairs(nlon, nlat, lambda i: i ^ 1))
+
+    def edge(block):
+        def spec(a):
+            if a.ndim == 3:
+                return pl.BlockSpec((K, 8, cols), lambda i: (0, block, 0))
+            return pl.BlockSpec((8, cols), lambda i: (block, 0))
+        return [spec(a) for a in args]
+
+    whole = pl.BlockSpec((rows, LANES), lambda i: (0, 0))
+    row = jax.ShapeDtypeStruct((4 * PLANES + 4, cols), f32)
+    row_spec = pl.BlockSpec(row.shape, lambda i: (0, 0))
+    row_b, row_a = pl.pallas_call(
+        pack_rows,
+        grid=(1,),
+        in_specs=edge(0) + edge(rows // 8 - 1) + [whole, whole],
+        out_specs=(row_spec, row_spec),
         out_shape=(row, row),
         compiler_params=params,
-        name="add_corners",
-    )(col_a, col_b, row_a, row_b)
+        name="pack_rows",
+    )(*args, *args, col_b, col_a)
     row_b = lax.ppermute(row_b, axes, lat_pairs(nlon, nlat, True))
     row_a = lax.ppermute(row_a, axes, lat_pairs(nlon, nlat, False))
     tall = rows + 32
@@ -353,7 +365,7 @@
         ],
         compiler_params=params,
         name="run_steps",
-    )(*args, col_a, col_b, row_a, row_b)
+    )(*args, col_b, col_a, row_b, row_a)
 
 
 def solution(mesh):

time: 42.5 us -> 41 us (0.965)
  local copies, waits for them, and re-layouts: 1.8 us -> 0.04 us
  waiting for transfers between devices: 5.04 us -> 6.41 us
  starting transfers between devices: 15.4 us -> 14.2 us
    unnamed x22 -> x18, local copies, waits for them, and re-layouts: 1.8 us -> 0.04 us
    ppermute x1, starting transfers between devices: 1.52 us -> 0.09 us  [body(): row_a = lax.ppermute(row_a, axes, lat_pairs(nlon, nlat, False))]
    ppermute x1, starting transfers between devices: 6.28 us -> 7.19 us  [body(): row_b = lax.ppermute(row_b, axes, lat_pairs(nlon, nlat, True))]
    ppermute x1, waiting for transfers between devices: 0.01 us -> 0.75 us  [body(): row_a = lax.ppermute(row_a, axes, lat_pairs(nlon, nlat, False))]
    ppermute x1, waiting for transfers between devices: 2.97 us -> 3.59 us  [body(): row_b = lax.ppermute(row_b, axes, lat_pairs(nlon, nlat, True))]
    ppermute x1, starting transfers between devices: 7.52 us -> 6.94 us  [body(): lax.ppermute(col_b, axes, lon_pairs(nlon, nlat, lambda i: (i + 1 if i % 2...]
  transfers between devices with their start and end apart: 4 -> 4, of which waited for: 2 -> 3; matrix products, arithmetic and copies ran while one was open for 0% -> 0% of each run, Pallas kernels for 0% -> 0%
where the time goes in v3:
time: 41 us; the launch traced here: 40.9 us
  Pallas kernels  19.4 us (47%)
  starting transfers between devices  14.2 us (35%)
  waiting for transfers between devices  6.41 us (16%)
  between operations  0.79 us (2%)
    pallas_call x1, Pallas kernels, body(): pl.pallas_call(run_steps, out_shape=(out,) * 4, scratch_shapes=[pltpu.VME...  16.5 us
    ppermute x1, starting transfers between devices, body(): row_b = lax.ppermute(row_b, axes, lat_pairs(nlon, nlat, True))  7.19 us
    ppermute x1, starting transfers between devices, body(): lax.ppermute(col_b, axes, lon_pairs(nlon, nlat, lambda i: (i + 1 if i % 2...  6.94 us
    ppermute x1, waiting for transfers between devices, body(): row_b = lax.ppermute(row_b, axes, lat_pairs(nlon, nlat, True))  3.59 us
    pallas_call x1, Pallas kernels, body(): pl.pallas_call(pack_columns, in_specs=[pl.BlockSpec(memory_space=pltpu.HB...  2.83 us
    ppermute x1, waiting for transfers between devices, body(): lax.ppermute(col_b, axes, lon_pairs(nlon, nlat, lambda i: (i + 1 if i % 2...  2.06 us
  transfers between devices with their start and end apart: 4, of which 3 were waited for; matrix products, arithmetic and copies ran while one was open for 0% of the time, Pallas kernels for 0%

profile of v3, /device:TPU:26, one launch (start us, length us, event | category | flops | bytes accessed | tf_op | source)
XLA Modules:
  0.0 40.9 jit_solution(4820458683826058469)
XLA Ops:
  0.6 0.0 copy-start.8
  0.6 0.0 copy-start.7
  0.7 0.0 copy-start.6
  0.7 0.0 copy-start.5
  0.7 0.0 copy-start.4
  0.7 0.0 copy-start.3
  0.7 0.0 copy-start.2
  0.7 0.0 copy-start.1
  0.7 0.0 copy-start
  0.7 2.8 %pack_columns.1 = (f32[96,128]{1,0:T(8,128)}, f32[96,128]{1,0:T(8,128)}) custom-call(f32[3,96,256]{2,1,0:T(8,128)} %refs_0_.5, f32[3,96,256]{2,1,0:T(8,128)} %refs_1_.5, f32[3,96,256]{2,1,0:T(8,128)} %refs_2_.5, f32[3,96,256]{2,1,0:T(8,128)} %refs_3_.5, s32[96,256]{1,0:T(8,128)} %refs_4_.5, s32[96,256]{1,0:T(8,128)} %refs_5_.5, f32[96,256]{1,0:T(8,128)} %refs_6_.5, ...), custom_call_target="tpu_custom_call" | custom-call | tf_op jit(solution)/shard_map/pack_columns/pallas_call | solution.py:319
  3.6 6.9 %collective-permute-start = (f32[96,128]{1,0:T(8,128)}, f32[96,128]{1,0:T(8,128)S(1)}, u32[]{:S(2)}, u32[]{:S(2)}) collective-permute-start(f32[96,128]{1,0:T(8,128)} %get-tuple-element.8), channel_id=1, source_target_pairs={{0,248},{1,249},{2,250},{3,251},{4,252},{5,253},{6,254},{7,255},{8... | collective-permute-start | bytes 147464 | tf_op jit(solution)/shard_map/ppermute | solution.py:327
  10.5 0.0 collective-permute-start.1
  10.5 2.1 %collective-permute-done.refs_18_.refs_9_ = f32[96,128]{1,0:T(8,128)S(1)} collective-permute-done((f32[96,128]{1,0:T(8,128)}, f32[96,128]{1,0:T(8,128)S(1)}, u32[]{:S(2)}, u32[]{:S(2)}) %collective-permute-start) | collective-permute-done | bytes 49184 | tf_op jit(solution)/shard_map/ppermute | solution.py:327
  12.6 0.0 collective-permute-done.1.refs_19_.refs_10_
  12.6 0.0 copy-done.8
  12.6 0.0 copy-done.7
  12.6 0.0 copy-done.6
  12.6 0.0 copy-done.5
  12.6 0.0 copy-done.4
  12.6 0.0 copy-done.3
  12.6 0.0 copy-done.2
  12.6 0.0 copy-done.1
  12.6 0.0 copy-done
  12.6 0.1 pack_rows.1
  12.7 7.2 %collective-permute-start.2 = (f32[72,256]{1,0:T(8,128)S(1)}, f32[72,256]{1,0:T(8,128)S(1)}, u32[]{:S(2)}, u32[]{:S(2)}) collective-permute-start(f32[72,256]{1,0:T(8,128)S(1)} %get-tuple-element.10), channel_id=1, source_target_pairs={{1,2},{2,1},{3,4},{4,3},{5,6},{6,5},{7,255},{9,10},{10,9},{11,12},... | collective-permute-start | bytes 221192 | tf_op jit(solution)/shard_map/ppermute | solution.py:351
  19.9 0.1 collective-permute-start.3
  20.0 3.6 %collective-permute-done.2.refs_11_ = f32[72,256]{1,0:T(8,128)S(1)} collective-permute-done((f32[72,256]{1,0:T(8,128)S(1)}, f32[72,256]{1,0:T(8,128)S(1)}, u32[]{:S(2)}, u32[]{:S(2)}) %collective-permute-start.2) | collective-permute-done | bytes 73760 | tf_op jit(solution)/shard_map/ppermute | solution.py:351
  23.6 0.8 %collective-permute-done.3.refs_12_ = f32[72,256]{1,0:T(8,128)S(1)} collective-permute-done((f32[72,256]{1,0:T(8,128)S(1)}, f32[72,256]{1,0:T(8,128)S(1)}, u32[]{:S(2)}, u32[]{:S(2)}) %collective-permute-start.3) | collective-permute-done | bytes 73760 | tf_op jit(solution)/shard_map/ppermute | solution.py:352
  24.3 16.5 %run_steps.1 = (f32[3,96,256]{2,1,0:T(8,128)}, f32[3,96,256]{2,1,0:T(8,128)}, f32[3,96,256]{2,1,0:T(8,128)}, f32[3,96,256]{2,1,0:T(8,128)}) custom-call(f32[3,96,256]{2,1,0:T(8,128)S(1)} %copy-done, f32[3,96,256]{2,1,0:T(8,128)S(1)} %copy-done.1, f32[3,96,256]{2,1,0:T(8,128)S(1)} %copy-done.2, f32[3,96,256]{2,1,0:T(8,128)S(1)} %copy-done.3, ...), custom_call_target="tpu_custom_call" | custom-call | tf_op jit(solution)/shard_map/run_steps/pallas_call | solution.py:355
Async XLA Ops:
  0.6 11.9 %copy-start.8 = (f32[96,256]{1,0:T(8,128)S(1)}, f32[96,256]{1,0:T(8,128)}, u32[]{:S(2)}) copy-start(f32[96,256]{1,0:T(8,128)} %refs_8_.5) | copy-start | bytes 294916
  0.6 11.9 %copy-start.7 = (f32[96,256]{1,0:T(8,128)S(1)}, f32[96,256]{1,0:T(8,128)}, u32[]{:S(2)}) copy-start(f32[96,256]{1,0:T(8,128)} %refs_7_.5) | copy-start | bytes 294916
  0.7 11.9 %copy-start.6 = (f32[96,256]{1,0:T(8,128)S(1)}, f32[96,256]{1,0:T(8,128)}, u32[]{:S(2)}) copy-start(f32[96,256]{1,0:T(8,128)} %refs_6_.5) | copy-start | bytes 294916
  0.7 11.9 %copy-start.5 = (s32[96,256]{1,0:T(8,128)S(1)}, s32[96,256]{1,0:T(8,128)}, u32[]{:S(2)}) copy-start(s32[96,256]{1,0:T(8,128)} %refs_5_.5) | copy-start | bytes 294916
  0.7 11.9 %copy-start.4 = (s32[96,256]{1,0:T(8,128)S(1)}, s32[96,256]{1,0:T(8,128)}, u32[]{:S(2)}) copy-start(s32[96,256]{1,0:T(8,128)} %refs_4_.5) | copy-start | bytes 294916
  0.7 11.9 %copy-start.3 = (f32[3,96,256]{2,1,0:T(8,128)S(1)}, f32[3,96,256]{2,1,0:T(8,128)}, u32[]{:S(2)}) copy-start(f32[3,96,256]{2,1,0:T(8,128)} %refs_3_.5) | copy-start | bytes 884740
  0.7 11.9 %copy-start.2 = (f32[3,96,256]{2,1,0:T(8,128)S(1)}, f32[3,96,256]{2,1,0:T(8,128)}, u32[]{:S(2)}) copy-start(f32[3,96,256]{2,1,0:T(8,128)} %refs_2_.5) | copy-start | bytes 884740
  0.7 11.9 %copy-start.1 = (f32[3,96,256]{2,1,0:T(8,128)S(1)}, f32[3,96,256]{2,1,0:T(8,128)}, u32[]{:S(2)}) copy-start(f32[3,96,256]{2,1,0:T(8,128)} %refs_1_.5) | copy-start | bytes 884740
  0.7 11.9 %copy-start = (f32[3,96,256]{2,1,0:T(8,128)S(1)}, f32[3,96,256]{2,1,0:T(8,128)}, u32[]{:S(2)}) copy-start(f32[3,96,256]{2,1,0:T(8,128)} %refs_0_.5) | copy-start | bytes 884740
  3.6 9.0 %collective-permute-start = (f32[96,128]{1,0:T(8,128)}, f32[96,128]{1,0:T(8,128)S(1)}, u32[]{:S(2)}, u32[]{:S(2)}) collective-permute-start(f32[96,128]{1,0:T(8,128)} %get-tuple-element.8), channel_id=1, source_target_pairs={{0,248},{1,249},{2,250},{3,251},{4,252},{5,253},{6,254},{7,255},{8... | collective-permute-start | bytes 147464 | tf_op jit(solution)/shard_map/ppermute | solution.py:327
  10.5 2.1 %collective-permute-start.1 = (f32[96,128]{1,0:T(8,128)}, f32[96,128]{1,0:T(8,128)S(1)}, u32[]{:S(2)}, u32[]{:S(2)}) collective-permute-start(f32[96,128]{1,0:T(8,128)} %get-tuple-element.9), channel_id=1, source_target_pairs={{0,8},{1,9},{2,10},{3,11},{4,12},{5,13},{6,14},{7,15},{8,0},{9,1},... | collective-permute-start | bytes 147464 | tf_op jit(solution)/shard_map/ppermute | solution.py:330
  12.7 10.9 %collective-permute-start.2 = (f32[72,256]{1,0:T(8,128)S(1)}, f32[72,256]{1,0:T(8,128)S(1)}, u32[]{:S(2)}, u32[]{:S(2)}) collective-permute-start(f32[72,256]{1,0:T(8,128)S(1)} %get-tuple-element.10), channel_id=1, source_target_pairs={{1,2},{2,1},{3,4},{4,3},{5,6},{6,5},{7,255},{9,10},{10,9},{11,12},... | collective-permute-start | bytes 221192 | tf_op jit(solution)/shard_map/ppermute | solution.py:351
  19.9 4.4 %collective-permute-start.3 = (f32[72,256]{1,0:T(8,128)S(1)}, f32[72,256]{1,0:T(8,128)S(1)}, u32[]{:S(2)}, u32[]{:S(2)}) collective-permute-start(f32[72,256]{1,0:T(8,128)S(1)} %get-tuple-element.11), channel_id=1, source_target_pairs={{0,1},{1,0},{2,3},{3,2},{4,5},{5,4},{6,7},{7,6},{8,9},{9,8},{10,11... | collective-permute-start | bytes 221192 | tf_op jit(solution)/shard_map/ppermute | solution.py:352

commit v4 on v3

v4 whole, which is shorter than its diff:
```python
import jax
import jax.numpy as jnp
from jax import lax
from jax.experimental import pallas as pl
from jax.experimental.pallas import tpu as pltpu
from jax.sharding import PartitionSpec as P

STEPS = 4
K = 3
HALO = 4
PLANES = 17
LANES = 128
OFFSET = 16
U, V, T, S, PR = range(5)
CXE, CXW, CYN, CYS, HXE, HXW, HYN, HYS, WET, WCEN, WCOR = range(11)
VMEM_LIMIT = 28 * 1024 * 1024


def plane_values(refs, p, rows, lanes):
    if p < 12:
        return refs[p // 3][p % 3, rows, lanes]
    return refs[4 + p - 12][rows, lanes].astype(jnp.float32)


def lane_index(shape):
    return lax.broadcasted_iota(jnp.int32, shape, len(shape) - 1)


def pack_columns(*refs):
    args, (out_b, out_a), ins, sems = refs[:9], refs[9:11], refs[11:20], refs[20]
    copies = [pltpu.make_async_copy(a, i, sems.at[n]) for n, (a, i) in enumerate(zip(args, ins))]
    for copy in copies:
        copy.start()
    rows, cols = ins[4].shape
    even = lax.rem(lax.axis_index("lon"), 2) == 0
    lane = lane_index((8, LANES))
    blocks = range(0, rows, 8)
    west, east = {}, {}
    for p in range(PLANES):
        if p % 3 == 0 or p > 12:
            copies[p // 3 if p < 12 else p - 8].wait()
        for r in blocks:
            w = plane_values(ins, p, slice(r, r + 8), slice(0, LANES))
            e = plane_values(ins, p, slice(r, r + 8), slice(cols - LANES, cols))
            w = pltpu.roll(w, 4 * p, 1) if p else w
            e = pltpu.roll(e, (4 * p + HALO) % LANES, 1)
            mine = lane >= 4 * p
            west[r] = jnp.where(mine, w, west[r]) if p else w
            east[r] = jnp.where(mine, e, east[r]) if p else e
    for r in blocks:
        out_a[r : r + 8, :] = jnp.where(even, east[r], west[r])
        out_b[r : r + 8, :] = jnp.where(even, west[r], east[r])


def pack_rows(*refs):
    south, north = refs[0:9], refs[9:18]
    col_b, col_a, out_b, out_a = refs[18:]
    rows = col_a.shape[0]
    even = lax.rem(lax.axis_index("lat"), 2) == 0
    for p in range(PLANES):
        s = plane_values(south, p, slice(0, 8), slice(None))[:HALO]
        n = plane_values(north, p, slice(0, 8), slice(None))[HALO:]
        out_a[4 * p : 4 * p + 4, :] = jnp.where(even, n, s)
        out_b[4 * p : 4 * p + 4, :] = jnp.where(even, s, n)
    for ref, lanes in ((col_a, slice(0, LANES)), (col_b, slice(LANES, 2 * LANES))):
        s = ref[0:HALO, :]
        n = ref[rows - HALO : rows, :]
        out_a[4 * PLANES : 4 * PLANES + 4, lanes] = jnp.where(even, n, s)
        out_b[4 * PLANES : 4 * PLANES + 4, lanes] = jnp.where(even, s, n)


def xor_rows(x, bit):
    row = lax.broadcasted_iota(jnp.int32, x.shape, 0)
    return jnp.where((row & bit) != 0, pltpu.roll(x, bit, 0), pltpu.roll(x, 8 - bit, 0))


def xor_lanes(x, bit):
    lane = lane_index(x.shape)
    if bit == LANES // 2:
        return pltpu.roll(x, bit, 1)
    return jnp.where((lane & bit) != 0, pltpu.roll(x, bit, 1), pltpu.roll(x, LANES - bit, 1))


def fold_rows(ref, out):
    lane = lane_index((8, LANES))
    row = lax.broadcasted_iota(jnp.int32, (8, LANES), 0)
    for r in range(0, 4 * PLANES + 4, 8):
        turned, short = [], []
        for t in range(2):
            x = ref[r : r + 8, t * LANES : (t + 1) * LANES]
            x = xor_rows(xor_rows(x, 1), 2)
            x = xor_lanes(xor_lanes(x, 1), 2)
            short.append(x)
            for bit in (4, 8, 16, 32, 64):
                x = xor_lanes(x, bit)
            turned.append(x)
        for t in range(2):
            x = turned[1 - t]
            if r < 24:
                x = -x
            if r + 8 > 4 * PLANES:
                packed = jnp.where(lane < 24, -short[t], short[t])
                x = jnp.where(row < 4, x, packed)
            out[r : r + 8, t * LANES : (t + 1) * LANES] = x


def density(t, s, slope):
    return t * (slope - 0.08 * t - 0.035 * s) + 0.7 * s


def slope_of(level):
    return -0.8 - 0.24 * ((level + 0.5) / K)


def column_pressure(rhos):
    above, out = None, []
    for rho in rhos:
        half = 0.5 * rho
        out.append(half if above is None else above + half)
        above = rho if above is None else above + rho
    return out


def coefficients(c, e, w, n, s, coriolis, idx, idy):
    hx, hy = 0.025 * idx, 0.025 * idy
    hxe, hxw, hyn, hys = c * e * hx, c * w * hx, c * n * hy, c * s * hy
    cx, cy = 1.2 * idx, 1.2 * idy
    cxe, cxw, cyn, cys = hxe * cx, hxw * cx, hyn * cy, hys * cy
    total = (cxe + cxw) + (cyn + cys)
    return cxe, cxw, cyn, cys, hxe, hxw, hyn, hys, c, c - 2.0 * total, 0.1 * c * coriolis


def advance(around, get):
    cxe, cxw, cyn, cys = get(CXE), get(CXW), get(CYN), get(CYS)
    hxe, hxw, hyn, hys = get(HXE), get(HXW), get(HYN), get(HYS)
    us, vs = around(U), around(V)
    u, v = us[0], vs[0]
    u2, v2 = u + u, v + v
    ae, aw = cxe - hxe * u2, cxw + hxw * u2
    an, as_ = cyn - hyn * v2, cys + hys * v2
    ac = get(WET) - ((ae + aw) + (an + as_))
    wcor = get(WCOR)
    p, pe, pw, pn, ps = around(PR)
    px = hxe * (pe - p) + hxw * (p - pw)
    py = hyn * (pn - p) + hys * (p - ps)

    def combine(xs, ac, ae, aw, an, as_):
        c, e, w, n, s = xs
        return (ac * c + (ae * e + aw * w)) + (an * n + as_ * s)

    u_new = combine(us, ac, ae, aw, an, as_) + (wcor * v - px)
    v_new = combine(vs, ac, ae, aw, an, as_) - (wcor * u + py)
    ae = cxe - hxe * (u + us[1])
    aw = cxw + hxw * (u + us[2])
    an = cyn - hyn * (v + vs[3])
    as_ = cys + hys * (v + vs[4])
    ac = get(WCEN) + ((ae + aw) + (an + as_))
    t_new = combine(around(T), ac, ae, aw, an, as_)
    s_new = combine(around(S), ac, ae, aw, an, as_)
    return u_new, v_new, t_new, s_new


def east_west(c, other, t):
    lane = lane_index(c.shape)
    if t == 0:
        e = pltpu.roll(jnp.where(lane == 0, other, c), LANES - 1, 1)
        w = pltpu.roll(c, 1, 1)
    else:
        e = pltpu.roll(c, LANES - 1, 1)
        w = pltpu.roll(jnp.where(lane == LANES - 1, other, c), 1, 1)
    return e, w


def advance_tiles(field, coef, r, write, last=False):
    for t in range(2):
        above = None
        for k in range(K):
            def around(f):
                c = field(f, k, t, r)
                e, w = east_west(c, field(f, k, 1 - t, r), t)
                return c, e, w, field(f, k, t, r + 1), field(f, k, t, r - 1)

            new = advance(around, lambda i: coef(i, k, t, r))
            for f in range(4):
                write(f, k, t, new[f])
            if not last:
                rho = density(new[T], new[S], slope_of(k))
                half = 0.5 * rho
                write(PR, k, t, half if k == 0 else above + half)
                above = rho if k == 0 else above + rho


def tile_coefficients(wet, geo, r, write):
    for k in range(K):
        for t in range(2):
            c = wet(k, t, r)
            e, w = east_west(c, wet(k, 1 - t, r), t)
            values = coefficients(
                c, e, w, wet(k, t, r + 1), wet(k, t, r - 1), geo(0, t, r), geo(1, t, r), geo(2, t, r)
            )
            for i, value in enumerate(values):
                write(i, k, t, value)


def strip_of(tiles):
    lane = lane_index((8, LANES))
    out = None
    for k, (low, high) in enumerate(tiles):
        x = pltpu.roll(low, 32 * k + 4, 1)
        y = pltpu.roll(high, (32 * k - 100) % LANES, 1)
        both = jnp.where(lane >= 32 * k + 16, y, x)
        out = both if k == 0 else jnp.where(lane >= 32 * k, both, out)
    return out


def run_interior(*refs):
    ins, states, outs, strip = refs[:9], refs[10:14], refs[14:18], refs[18]
    coef, wet = refs[19:]
    rows = ins[4].shape[0]
    tiles = [slice(t * LANES, (t + 1) * LANES) for t in range(2)]

    @pl.loop(0, rows // 8)
    def _(b):
        q = pl.multiple_of(8 * b, 8)
        r = pl.multiple_of(8 * b + 8, 8)
        at, own = pl.ds(r, 8), pl.ds(q, 8)
        for f in range(4):
            for k in range(K):
                for t in range(2):
                    states[0][f, k, t, at, :] = ins[f][k, own, tiles[t]]
            strip[f, own, :] = strip_of([[ins[f][k, own, tiles[t]] for t in range(2)] for k in range(K)])
        for i in range(5):
            strip[4 + i, own, :] = strip_of([[ins[4 + i][own, tiles[t]].astype(jnp.float32) for t in range(2)]] * K)
        for t in range(2):
            sea = ins[5][own, tiles[t]] == 1
            rhos = []
            for k in range(K):
                wet[k, t, at, :] = jnp.where(sea & (ins[4][own, tiles[t]] > k), 1.0, 0.0)
                rhos.append(density(ins[T][k, own, tiles[t]], ins[S][k, own, tiles[t]], slope_of(k)))
            for k, value in enumerate(column_pressure(rhos)):
                states[0][PR, k, t, at, :] = value

    @pl.loop(0, rows // 8)
    def _(b):
        r = pl.multiple_of(8 * b + 8, 8)

        def write(i, k, t, value):
            coef[i, k, t, pl.ds(r, 8), :] = value

        tile_coefficients(
            lambda k, t, row: wet[k, t, pl.ds(row, 8), :],
            lambda i, t, row: ins[6 + i][pl.ds(pl.multiple_of(8 * b, 8), 8), tiles[t]],
            r,
            write,
        )

    for step in range(STEPS):
        @pl.loop(0, rows // 8)
        def _(b):
            r = pl.multiple_of(8 * b + 8, 8)

            def write(f, k, t, value):
                if step < STEPS - 1:
                    states[step + 1][f, k, t, pl.ds(r, 8), :] = value
                else:
                    outs[f][k, pl.ds(pl.multiple_of(8 * b, 8), 8), tiles[t]] = value

            advance_tiles(
                lambda f, k, t, row: states[step][f, k, t, pl.ds(row, 8), :],
                lambda i, k, t, row: coef[i, k, t, pl.ds(row, 8), :],
                r,
                write,
                last=step == STEPS - 1,
            )


def run_rims(*refs):
    geo_in, states, parts, strip_in = refs[0:5], refs[5:9], refs[9:13], refs[13]
    col_b, col_a, row_b, row_a = refs[14:18]
    outs = refs[18:22]
    north, cols, band, band_geo, band_wet, band_coef, sf, sg, sw, sc = refs[22:]
    rows = geo_in[0].shape[0]
    top = OFFSET + rows
    lon_even = lax.rem(lax.axis_index("lon"), 2) == 0
    lat = lax.axis_index("lat")
    lat_even = lax.rem(lat, 2) == 0
    lane = lane_index((8, LANES))
    tiles = [slice(t * LANES, (t + 1) * LANES) for t in range(2)]
    fold = lat == lax.axis_size("lat") - 1

    @pl.when(fold)
    def _():
        fold_rows(row_b, north)

    @pl.when(jnp.logical_not(fold))
    def _():
        north[...] = jnp.where(lat_even, row_a[...], row_b[...])

    def south_rows(p, lanes):
        rows_p = slice(4 * p, 4 * p + 4)
        return jnp.where(lat_even, row_b[rows_p, lanes], row_a[rows_p, lanes])

    def north_rows(p, lanes):
        return north[4 * p : 4 * p + 4, lanes]

    def place(dst, a, b):
        cols[0, dst, :] = jnp.where(lon_even, b, a)
        cols[1, dst, :] = jnp.where(lon_even, a, b)

    place(slice(OFFSET, top), col_a[...], col_b[...])
    place(slice(OFFSET - HALO, OFFSET), *(south_rows(PLANES, tiles[i]) for i in range(2)))
    place(slice(top, top + HALO), *(north_rows(PLANES, tiles[i]) for i in range(2)))

    own = ((16, 0), (8, rows - 16))
    far = ((24, 8), (8, rows - 16))
    halo = ((12, south_rows), (24, north_rows))
    blocks = ((8, 16), (16, 24))
    for side in range(2):
        put, first = own[side]
        place_h, rows_of = halo[side]
        for t in range(2):
            for f in range(4):
                for k in range(K):
                    band[side, 0, f, k, t, place_h : place_h + 4, :] = rows_of(3 * f + k, tiles[t])
            for i in range(5):
                band_geo[side, i, t, put : put + 16, :] = geo_in[i][first : first + 16, tiles[t]].astype(jnp.float32)
                band_geo[side, i, t, place_h : place_h + 4, :] = rows_of(12 + i, tiles[t])
            for k in range(K):
                for f in range(5):
                    band[side, 0, f, k, t, put : put + 16, :] = states[0][f, k, t, first + 8 : first + 24, :]
                    for step in range(1, STEPS):
                        at, start = far[side]
                        band[side, step, f, k, t, at : at + 8, :] = states[step][f, k, t, start + 8 : start + 16, :]
            at = 8 if side == 0 else 24
            rhos = [
                density(band[side, 0, T, k, t, at : at + 8, :], band[side, 0, S, k, t, at : at + 8, :], slope_of(k))
                for k in range(K)
            ]
            for k, value in enumerate(column_pressure(rhos)):
                band[side, 0, PR, k, t, at : at + 8, :] = value
            for at in (8, 16, 24):
                sea = band_geo[side, 1, t, at : at + 8, :] == 1.0
                for k in range(K):
                    wet = sea & (band_geo[side, 0, t, at : at + 8, :] > k)
                    band_wet[side, k, t, at : at + 8, :] = jnp.where(wet, 1.0, 0.0)

    own_rows = slice(OFFSET, top)
    for f in range(4):
        sf[0, f, own_rows, :] = strip_in[f]
    for i in range(5):
        sg[i, own_rows, :] = strip_in[4 + i]
    for side, (at, to) in enumerate(((8, OFFSET - 8), (24, top))):
        for f in range(4):
            sf[0, f, to : to + 8, :] = strip_of(
                [[band[side, 0, f, k, t, at : at + 8, :] for t in range(2)] for k in range(K)]
            )
        for i in range(5):
            sg[i, to : to + 8, :] = strip_of([[band_geo[side, i, t, at : at + 8, :] for t in range(2)]] * K)
    level = lane // 32
    slope = slope_of(level.astype(jnp.float32))

    def strip_pressure(t, s):
        rho = density(t, s, slope)
        one = jnp.where(lane >= 32, pltpu.roll(rho, 32, 1), 0.0)
        two = jnp.where(lane >= 64, pltpu.roll(rho, 64, 1), 0.0)
        return 0.5 * rho + (one + two)

    @pl.loop(0, (rows + 16) // 8)
    def _(b):
        r = pl.multiple_of(OFFSET - 8 + 8 * b, 8)
        at = pl.ds(r, 8)
        west, east = cols[0, at, :], cols[1, at, :]

        def insert(x, planes):
            for k, p in enumerate(planes):
                w = pltpu.roll(west, (32 * k - 4 * p) % LANES, 1)
                e = pltpu.roll(east, (32 * k + 28 - 4 * p) % LANES, 1)
                x = jnp.where((lane >= 32 * k) & (lane < 32 * k + 4), w, x)
                x = jnp.where((lane >= 32 * k + 28) & (lane < 32 * k + 32), e, x)
            return x

        for f in range(4):
            sf[0, f, at, :] = insert(sf[0, f, at, :], (3 * f, 3 * f + 1, 3 * f + 2))
        for i in range(5):
            sg[i, at, :] = insert(sg[i, at, :], (12 + i,) * K)
        sf[0, PR, at, :] = strip_pressure(sf[0, T, at, :], sf[0, S, at, :])
        wet = (sg[1, at, :] == 1.0) & (sg[0, at, :] > level.astype(jnp.float32))
        sw[at, :] = jnp.where(wet, 1.0, 0.0)

    def rolled(c):
        return pltpu.roll(c, LANES - 1, 1), pltpu.roll(c, 1, 1)

    @pl.loop(0, (rows + 16) // 8)
    def _(b):
        r = pl.multiple_of(OFFSET - 8 + 8 * b, 8)
        at = pl.ds(r, 8)
        c = sw[at, :]
        e, w = rolled(c)
        values = coefficients(
            c, e, w, sw[pl.ds(r + 1, 8), :], sw[pl.ds(r - 1, 8), :], sg[2, at, :], sg[3, at, :], sg[4, at, :]
        )
        for i, value in enumerate(values):
            sc[i, at, :] = value

    for side in range(2):
        @pl.loop(0, 2)
        def _(b):
            r = pl.multiple_of(blocks[side][0] + 8 * b, 8)

            def write(i, k, t, value):
                band_coef[side, i, k, t, pl.ds(r, 8), :] = value

            tile_coefficients(
                lambda k, t, row: band_wet[side, k, t, pl.ds(row, 8), :],
                lambda i, t, row: band_geo[side, 2 + i, t, pl.ds(row, 8), :],
                r,
                write,
            )

    for step in range(STEPS):
        final = step == STEPS - 1

        @pl.loop(0, 2 if final else 4)
        def _(n):
            side = n if final else lax.div(n, 2)
            r = pl.multiple_of(16 + 0 * n if final else 8 + 8 * (lax.rem(n, 2) + side), 8)

            def write(f, k, t, value):
                if final:
                    to = pl.multiple_of(side * (rows - 8), 8)
                    outs[f][k, pl.ds(to, 8), tiles[t]] = value
                else:
                    band[side, step + 1, f, k, t, pl.ds(r, 8), :] = value

            advance_tiles(
                lambda f, k, t, row: band[side, step, f, k, t, pl.ds(row, 8), :],
                lambda i, k, t, row: band_coef[side, i, k, t, pl.ds(row, 8), :],
                r,
                write,
                last=final,
            )

    def strip_step(step, r):
        at = pl.ds(r, 8)

        def around(f):
            c = sf[step % 2, f, at, :]
            return (c,) + rolled(c) + (sf[step % 2, f, pl.ds(r + 1, 8), :], sf[step % 2, f, pl.ds(r - 1, 8), :])

        return advance(around, lambda i: sc[i, at, :])

    for step in range(STEPS - 1):
        @pl.loop(0, (rows + 16) // 8)
        def _(b):
            r = pl.multiple_of(OFFSET - 8 + 8 * b, 8)
            new = strip_step(step, r)
            for f in range(4):
                sf[(step + 1) % 2, f, pl.ds(r, 8), :] = new[f]
            sf[(step + 1) % 2, PR, pl.ds(r, 8), :] = strip_pressure(new[T], new[S])

    def finish(q, source):
        new = strip_step(STEPS - 1, q + OFFSET)
        at = pl.ds(q, 8)
        for f in range(4):
            for k in range(K):
                low = pltpu.roll(new[f], (-32 * k - 4) % LANES, 1)
                high = pltpu.roll(new[f], 100 - 32 * k, 1)
                outs[f][k, at, tiles[0]] = jnp.where(lane < HALO, low, source[f][k, at, tiles[0]])
                outs[f][k, at, tiles[1]] = jnp.where(lane >= LANES - HALO, high, source[f][k, at, tiles[1]])

    finish(0, outs)
    finish(rows - 8, outs)

    @pl.loop(1, rows // 8 - 1)
    def _(b):
        finish(pl.multiple_of(8 * b, 8), parts)


def lon_pairs(nlon, nlat, partner):
    return [(i * nlat + j, partner(i) * nlat + j) for i in range(nlon) for j in range(nlat)]


def lat_pairs(nlon, nlat, odd):
    pairs = []
    for i in range(nlon):
        for j in range(nlat):
            up = (j % 2 == 0) != odd
            to, at = (j + 1 if up else j - 1), i
            if to < 0:
                continue
            if to == nlat:
                to, at = nlat - 1, nlon - 1 - i
            pairs.append((i * nlat + j, at * nlat + to))
    return pairs


def body(u_vel, v_vel, temp, salt, levels, land_sea, coriolis, inv_dx, inv_dy):
    args = (u_vel, v_vel, temp, salt, levels, land_sea, coriolis, inv_dx, inv_dy)
    rows, cols = levels.shape
    nlon, nlat = lax.axis_size("lon"), lax.axis_size("lat")
    axes = ("lon", "lat")
    params = pltpu.CompilerParams(vmem_limit_bytes=VMEM_LIMIT)
    f32 = jnp.float32
    column = jax.ShapeDtypeStruct((rows, LANES), f32)
    col_b, col_a = pl.pallas_call(
        pack_columns,
        in_specs=[pl.BlockSpec(memory_space=pltpu.HBM)] * 9,
        out_shape=(column, column),
        scratch_shapes=[pltpu.VMEM(a.shape, a.dtype) for a in args] + [pltpu.SemaphoreType.DMA((9,))],
        compiler_params=pltpu.CompilerParams(vmem_limit_bytes=62 * 1024 * 1024),
        name="pack_columns",
    )(*args)
    col_b = lax.ppermute(
        col_b, axes, lon_pairs(nlon, nlat, lambda i: (i + 1 if i % 2 else i - 1) % nlon)
    )
    col_a = lax.ppermute(col_a, axes, lon_pairs(nlon, nlat, lambda i: i ^ 1))

    def edge(block):
        def spec(a):
            if a.ndim == 3:
                return pl.BlockSpec((K, 8, cols), lambda i: (0, block, 0))
            return pl.BlockSpec((8, cols), lambda i: (block, 0))
        return [spec(a) for a in args]

    whole = pl.BlockSpec((rows, LANES), lambda i: (0, 0))
    row = jax.ShapeDtypeStruct((4 * PLANES + 4, cols), f32)
    row_spec = pl.BlockSpec(row.shape, lambda i: (0, 0))
    row_b, row_a = pl.pallas_call(
        pack_rows,
        grid=(1,),
        in_specs=edge(0) + edge(rows // 8 - 1) + [whole, whole],
        out_specs=(row_spec, row_spec),
        out_shape=(row, row),
        compiler_params=params,
        name="pack_rows",
    )(*args, *args, col_b, col_a)
    sent = row_a
    row_b = lax.ppermute(row_b, axes, lat_pairs(nlon, nlat, True))
    row_a = lax.ppermute(row_a, axes, lat_pairs(nlon, nlat, False))
    out = jax.ShapeDtypeStruct(u_vel.shape, f32)
    state = jax.ShapeDtypeStruct((5, K, 2, rows + 16, LANES), f32)
    vmem = pl.BlockSpec(memory_space=pltpu.VMEM)
    *kept, strip = pl.pallas_call(
        run_interior,
        in_specs=[vmem] * 9 + [pl.BlockSpec(memory_space=pl.ANY)],
        out_shape=(state,) * 4 + (out,) * 4 + (jax.ShapeDtypeStruct((9, rows, LANES), f32),),
        scratch_shapes=[
            pltpu.VMEM((11, K, 2, rows + 16, LANES), f32),
            pltpu.VMEM((K, 2, rows + 16, LANES), f32),
        ],
        compiler_params=params,
        cost_estimate=pl.CostEstimate(flops=30_000_000, bytes_accessed=16_000_000, transcendentals=0),
        name="run_interior",
    )(*args, sent)
    tall = rows + 32
    return pl.pallas_call(
        run_rims,
        out_shape=(out,) * 4,
        scratch_shapes=[
            pltpu.VMEM(row.shape, f32),
            pltpu.VMEM((2, tall, LANES), f32),
            pltpu.VMEM((2, 4, 5, K, 2, 40, LANES), f32),
            pltpu.VMEM((2, 5, 2, 40, LANES), f32),
            pltpu.VMEM((2, K, 2, 40, LANES), f32),
            pltpu.VMEM((2, 11, K, 2, 40, LANES), f32),
            pltpu.VMEM((2, 5, tall, LANES), f32),
            pltpu.VMEM((5, tall, LANES), f32),
            pltpu.VMEM((tall, LANES), f32),
            pltpu.VMEM((11, tall, LANES), f32),
        ],
        compiler_params=params,
        name="run_rims",
    )(*args[4:], *kept, strip, col_b, col_a, row_b, row_a)


def solution(mesh):
    block, plane = P(None, "lat", "lon"), P("lat", "lon")
    return jax.shard_map(
        body,
        mesh=mesh,
        in_specs=(block,) * 4 + (plane,) * 5,
        out_specs=(block,) * 4,
        check_vma=False,
    )
```

time: 41 us -> 47.4 us (1.16)
  the two profiles are of different devices: /device:TPU:26 before, /device:TPU:24 now
where the time goes in v4:
time: 47.4 us; the launch traced here: 47.3 us
  Pallas kernels  28.7 us (61%)
  starting transfers between devices  15.7 us (33%)
  waiting for transfers between devices  2.07 us (4%)
  between operations  0.81 us (2%)
    pallas_call x1, Pallas kernels, body(): pl.pallas_call(run_rims, out_shape=(out,) * 4, scratch_shapes=[pltpu.VMEM...  15.9 us
    pallas_call x1, Pallas kernels, body(): pl.pallas_call(run_interior, in_specs=[vmem] * 9 + [pl.BlockSpec(memory_s...  9.9 us
    ppermute x1, starting transfers between devices, body(): lax.ppermute(col_b, axes, lon_pairs(nlon, nlat, lambda i: (i + 1 if i % 2...  7.84 us
    ppermute x1, starting transfers between devices, body(): row_a = lax.ppermute(row_a, axes, lat_pairs(nlon, nlat, False))  5.19 us
    pallas_call x1, Pallas kernels, body(): pl.pallas_call(pack_columns, in_specs=[pl.BlockSpec(memory_space=pltpu.HB...  2.83 us
    ppermute x1, starting transfers between devices, body(): row_b = lax.ppermute(row_b, axes, lat_pairs(nlon, nlat, True))  2.68 us
    ppermute x1, waiting for transfers between devices, body(): lax.ppermute(col_b, axes, lon_pairs(nlon, nlat, lambda i: (i + 1 if i % 2...  2.06 us
  transfers between devices with their start and end apart: 4, of which 1 were waited for; matrix products, arithmetic and copies ran while one was open for 0% of the time, Pallas kernels for 21%

profile of v4, /device:TPU:24, one launch (start us, length us, event | category | flops | bytes accessed | tf_op | source)
XLA Modules:
  0.0 47.3 jit_solution(16960020709693601456)
XLA Ops:
  0.6 0.0 copy-start.8
  0.6 0.0 copy-start.7
  0.7 0.0 copy-start.6
  0.7 0.0 copy-start.5
  0.7 0.0 copy-start.4
  0.7 0.0 copy-start.3
  0.7 0.0 copy-start.2
  0.7 0.0 copy-start.1
  0.7 0.0 copy-start
  0.7 2.8 %pack_columns.1 = (f32[96,128]{1,0:T(8,128)}, f32[96,128]{1,0:T(8,128)}) custom-call(f32[3,96,256]{2,1,0:T(8,128)} %refs_0_.6, f32[3,96,256]{2,1,0:T(8,128)} %refs_1_.6, f32[3,96,256]{2,1,0:T(8,128)} %refs_2_.6, f32[3,96,256]{2,1,0:T(8,128)} %refs_3_.6, s32[96,256]{1,0:T(8,128)} %refs_0_.7, s32[96,256]{1,0:T(8,128)} %refs_1_.7, f32[96,256]{1,0:T(8,128)} %refs_2_.7, ...), custom_call_target="tpu_custom_call" | custom-call | tf_op jit(solution)/shard_map/pack_columns/pallas_call | solution.py:505
  3.6 7.8 %collective-permute-start = (f32[96,128]{1,0:T(8,128)}, f32[96,128]{1,0:T(8,128)S(1)}, u32[]{:S(2)}, u32[]{:S(2)}) collective-permute-start(f32[96,128]{1,0:T(8,128)} %get-tuple-element.17), channel_id=1, source_target_pairs={{0,248},{1,249},{2,250},{3,251},{4,252},{5,253},{6,254},{7,255},{8... | collective-permute-start | bytes 147464 | tf_op jit(solution)/shard_map/ppermute | solution.py:513
  11.4 0.0 collective-permute-start.1
  11.4 2.1 %collective-permute-done.refs_18_.refs_14_ = f32[96,128]{1,0:T(8,128)S(1)} collective-permute-done((f32[96,128]{1,0:T(8,128)}, f32[96,128]{1,0:T(8,128)S(1)}, u32[]{:S(2)}, u32[]{:S(2)}) %collective-permute-start) | collective-permute-done | bytes 49184 | tf_op jit(solution)/shard_map/ppermute | solution.py:513
  13.5 0.0 collective-permute-done.1.refs_19_.refs_15_
  13.5 0.0 copy-done.8
  13.5 0.0 copy-done.7
  13.5 0.0 copy-done.6
  13.5 0.0 copy-done.5
  13.5 0.0 copy-done.4
  13.5 0.0 copy-done.3
  13.5 0.0 copy-done.2
  13.5 0.0 copy-done.1
  13.5 0.0 copy-done
  13.5 0.1 pack_rows.1
  13.6 2.7 %collective-permute-start.2 = (f32[72,256]{1,0:T(8,128)S(1)}, f32[72,256]{1,0:T(8,128)S(1)}, u32[]{:S(2)}, u32[]{:S(2)}) collective-permute-start(f32[72,256]{1,0:T(8,128)S(1)} %get-tuple-element.29), channel_id=1, source_target_pairs={{1,2},{2,1},{3,4},{4,3},{5,6},{6,5},{7,255},{9,10},{10,9},{11,12},... | collective-permute-start | bytes 221192 | tf_op jit(solution)/shard_map/ppermute | solution.py:538
  16.3 5.2 %collective-permute-start.3 = (f32[72,256]{1,0:T(8,128)S(1)}, f32[72,256]{1,0:T(8,128)S(1)}, u32[]{:S(2)}, u32[]{:S(2)}) collective-permute-start(f32[72,256]{1,0:T(8,128)S(1)} %get-tuple-element.19.refs_9_), channel_id=1, source_target_pairs={{0,1},{1,0},{2,3},{3,2},{4,5},{5,4},{6,7},{7,6},{8,9},{9,8},{10,11... | collective-permute-start | bytes 221192 | tf_op jit(solution)/shard_map/ppermute | solution.py:539
  21.5 9.9 %run_interior.1 = (f32[5,3,2,112,128]{4,3,2,1,0:T(8,128)S(1)}, f32[5,3,2,112,128]{4,3,2,1,0:T(8,128)S(1)}, f32[5,3,2,112,128]{4,3,2,1,0:T(8,128)S(1)}, f32[5,3,2...) custom-call(f32[3,96,256]{2,1,0:T(8,128)S(1)} %copy-done, ...), custom_call_target="tpu_custom_call" | custom-call | flops 30000000 | bytes 16000000 | tf_op jit(solution)/shard_map/run_interior/pallas_call | solution.py:543
  31.4 0.0 collective-permute-done.2.refs_16_
  31.4 0.0 collective-permute-done.3.refs_17_
  31.4 15.9 %run_rims.1 = (f32[3,96,256]{2,1,0:T(8,128)}, f32[3,96,256]{2,1,0:T(8,128)}, f32[3,96,256]{2,1,0:T(8,128)}, f32[3,96,256]{2,1,0:T(8,128)}) custom-call(s32[96,256]{1,0:T(8,128)S(1)} %copy-done.4, s32[96,256]{1,0:T(8,128)S(1)} %copy-done.5, f32[96,256]{1,0:T(8,128)S(1)} %copy-done.6, f32[96,256]{1,0:T(8,128)S(1)} %copy-done.7, f32[96,256]{1,0:T(8,128)S(1)} %copy-done.8, ...), custom_call_target="tpu_custom_call" | custom-call | tf_op jit(solution)/shard_map/run_rims/pallas_call | solution.py:556
Async XLA Ops:
  0.6 12.8 %copy-start.8 = (f32[96,256]{1,0:T(8,128)S(1)}, f32[96,256]{1,0:T(8,128)}, u32[]{:S(2)}) copy-start(f32[96,256]{1,0:T(8,128)} %refs_4_.7) | copy-start | bytes 294916
  0.6 12.8 %copy-start.7 = (f32[96,256]{1,0:T(8,128)S(1)}, f32[96,256]{1,0:T(8,128)}, u32[]{:S(2)}) copy-start(f32[96,256]{1,0:T(8,128)} %refs_3_.7) | copy-start | bytes 294916
  0.7 12.8 %copy-start.6 = (f32[96,256]{1,0:T(8,128)S(1)}, f32[96,256]{1,0:T(8,128)}, u32[]{:S(2)}) copy-start(f32[96,256]{1,0:T(8,128)} %refs_2_.7) | copy-start | bytes 294916
  0.7 12.8 %copy-start.5 = (s32[96,256]{1,0:T(8,128)S(1)}, s32[96,256]{1,0:T(8,128)}, u32[]{:S(2)}) copy-start(s32[96,256]{1,0:T(8,128)} %refs_1_.7) | copy-start | bytes 294916
  0.7 12.8 %copy-start.4 = (s32[96,256]{1,0:T(8,128)S(1)}, s32[96,256]{1,0:T(8,128)}, u32[]{:S(2)}) copy-start(s32[96,256]{1,0:T(8,128)} %refs_0_.7) | copy-start | bytes 294916
  0.7 12.8 %copy-start.3 = (f32[3,96,256]{2,1,0:T(8,128)S(1)}, f32[3,96,256]{2,1,0:T(8,128)}, u32[]{:S(2)}) copy-start(f32[3,96,256]{2,1,0:T(8,128)} %refs_3_.6) | copy-start | bytes 884740
  0.7 12.8 %copy-start.2 = (f32[3,96,256]{2,1,0:T(8,128)S(1)}, f32[3,96,256]{2,1,0:T(8,128)}, u32[]{:S(2)}) copy-start(f32[3,96,256]{2,1,0:T(8,128)} %refs_2_.6) | copy-start | bytes 884740
  0.7 12.8 %copy-start.1 = (f32[3,96,256]{2,1,0:T(8,128)S(1)}, f32[3,96,256]{2,1,0:T(8,128)}, u32[]{:S(2)}) copy-start(f32[3,96,256]{2,1,0:T(8,128)} %refs_1_.6) | copy-start | bytes 884740
  0.7 12.8 %copy-start = (f32[3,96,256]{2,1,0:T(8,128)S(1)}, f32[3,96,256]{2,1,0:T(8,128)}, u32[]{:S(2)}) copy-start(f32[3,96,256]{2,1,0:T(8,128)} %refs_0_.6) | copy-start | bytes 884740
  3.6 9.9 %collective-permute-start = (f32[96,128]{1,0:T(8,128)}, f32[96,128]{1,0:T(8,128)S(1)}, u32[]{:S(2)}, u32[]{:S(2)}) collective-permute-start(f32[96,128]{1,0:T(8,128)} %get-tuple-element.17), channel_id=1, source_target_pairs={{0,248},{1,249},{2,250},{3,251},{4,252},{5,253},{6,254},{7,255},{8... | collective-permute-start | bytes 147464 | tf_op jit(solution)/shard_map/ppermute | solution.py:513
  11.4 2.1 %collective-permute-start.1 = (f32[96,128]{1,0:T(8,128)}, f32[96,128]{1,0:T(8,128)S(1)}, u32[]{:S(2)}, u32[]{:S(2)}) collective-permute-start(f32[96,128]{1,0:T(8,128)} %get-tuple-element.18), channel_id=1, source_target_pairs={{0,8},{1,9},{2,10},{3,11},{4,12},{5,13},{6,14},{7,15},{8,0},{9,1},... | collective-permute-start | bytes 147464 | tf_op jit(solution)/shard_map/ppermute | solution.py:516
  13.6 17.8 %collective-permute-start.2 = (f32[72,256]{1,0:T(8,128)S(1)}, f32[72,256]{1,0:T(8,128)S(1)}, u32[]{:S(2)}, u32[]{:S(2)}) collective-permute-start(f32[72,256]{1,0:T(8,128)S(1)} %get-tuple-element.29), channel_id=1, source_target_pairs={{1,2},{2,1},{3,4},{4,3},{5,6},{6,5},{7,255},{9,10},{10,9},{11,12},... | collective-permute-start | bytes 221192 | tf_op jit(solution)/shard_map/ppermute | solution.py:538
  16.3 15.1 %collective-permute-start.3 = (f32[72,256]{1,0:T(8,128)S(1)}, f32[72,256]{1,0:T(8,128)S(1)}, u32[]{:S(2)}, u32[]{:S(2)}) collective-permute-start(f32[72,256]{1,0:T(8,128)S(1)} %get-tuple-element.19.refs_9_), channel_id=1, source_target_pairs={{0,1},{1,0},{2,3},{3,2},{4,5},{5,4},{6,7},{7,6},{8,9},{9,8},{10,11... | collective-permute-start | bytes 221192 | tf_op jit(solution)/shard_map/ppermute | solution.py:539

commit v5 on v4

--- a/solution.py
+++ b/solution.py
@@ -219,7 +219,7 @@
     rows = ins[4].shape[0]
     tiles = [slice(t * LANES, (t + 1) * LANES) for t in range(2)]
 
-    @pl.loop(0, rows // 8)
+    @pl.loop(0, rows // 8, unroll=6)
     def _(b):
         q = pl.multiple_of(8 * b, 8)
         r = pl.multiple_of(8 * b + 8, 8)
@@ -240,7 +240,7 @@
             for k, value in enumerate(column_pressure(rhos)):
                 states[0][PR, k, t, at, :] = value
 
-    @pl.loop(0, rows // 8)
+    @pl.loop(0, rows // 8, unroll=6)
     def _(b):
         r = pl.multiple_of(8 * b + 8, 8)
 
@@ -255,7 +255,7 @@
         )
 
     for step in range(STEPS):
-        @pl.loop(0, rows // 8)
+        @pl.loop(0, rows // 8, unroll=4)
         def _(b):
             r = pl.multiple_of(8 * b + 8, 8)
 
@@ -365,7 +365,7 @@
         two = jnp.where(lane >= 64, pltpu.roll(rho, 64, 1), 0.0)
         return 0.5 * rho + (one + two)
 
-    @pl.loop(0, (rows + 16) // 8)
+    @pl.loop(0, (rows + 16) // 8, unroll=2)
     def _(b):
         r = pl.multiple_of(OFFSET - 8 + 8 * b, 8)
         at = pl.ds(r, 8)
@@ -390,7 +390,7 @@
     def rolled(c):
         return pltpu.roll(c, LANES - 1, 1), pltpu.roll(c, 1, 1)
 
-    @pl.loop(0, (rows + 16) // 8)
+    @pl.loop(0, (rows + 16) // 8, unroll=7)
     def _(b):
         r = pl.multiple_of(OFFSET - 8 + 8 * b, 8)
         at = pl.ds(r, 8)
@@ -403,7 +403,7 @@
             sc[i, at, :] = value
 
     for side in range(2):
-        @pl.loop(0, 2)
+        @pl.loop(0, 2, unroll=2)
         def _(b):
             r = pl.multiple_of(blocks[side][0] + 8 * b, 8)
 
@@ -420,7 +420,7 @@
     for step in range(STEPS):
         final = step == STEPS - 1
 
-        @pl.loop(0, 2 if final else 4)
+        @pl.loop(0, 2 if final else 4, unroll=2)
         def _(n):
             side = n if final else lax.div(n, 2)
             r = pl.multiple_of(16 + 0 * n if final else 8 + 8 * (lax.rem(n, 2) + side), 8)
@@ -450,7 +450,7 @@
         return advance(around, lambda i: sc[i, at, :])
 
     for step in range(STEPS - 1):
-        @pl.loop(0, (rows + 16) // 8)
+        @pl.loop(0, (rows + 16) // 8, unroll=7)
         def _(b):
             r = pl.multiple_of(OFFSET - 8 + 8 * b, 8)
             new = strip_step(step, r)
@@ -471,7 +471,7 @@
     finish(0, outs)
     finish(rows - 8, outs)
 
-    @pl.loop(1, rows // 8 - 1)
+    @pl.loop(1, rows // 8 - 1, unroll=5)
     def _(b):
         finish(pl.multiple_of(8 * b, 8), parts)
 

time: 47.4 us -> 35.4 us (0.75)
  Pallas kernels: 28.7 us -> 16.7 us
    pallas_call x1, Pallas kernels: 15.9 us -> 7.46 us  [body(): pl.pallas_call(run_rims, out_shape=(out,) * 4, scratch_shapes=[pltpu.VMEM...]
    pallas_call x1, Pallas kernels: 9.9 us -> 6.33 us  [body(): pl.pallas_call(run_interior, in_specs=[vmem] * 9 + [pl.BlockSpec(memory_s...]
  transfers between devices with their start and end apart: 4 -> 4, of which waited for: 1 -> 1; matrix products, arithmetic and copies ran while one was open for 0% -> 0% of each run, Pallas kernels for 21% -> 18%
where the time goes in v5:
time: 35.4 us; the launch traced here: 35.3 us
  Pallas kernels  16.7 us (47%)
  starting transfers between devices  15.7 us (44%)
  waiting for transfers between devices  2.07 us (6%)
  between operations  0.81 us (2%)
    ppermute x1, starting transfers between devices, body(): lax.ppermute(col_b, axes, lon_pairs(nlon, nlat, lambda i: (i + 1 if i % 2...  7.84 us
    pallas_call x1, Pallas kernels, body(): pl.pallas_call(run_rims, out_shape=(out,) * 4, scratch_shapes=[pltpu.VMEM...  7.46 us
    pallas_call x1, Pallas kernels, body(): pl.pallas_call(run_interior, in_specs=[vmem] * 9 + [pl.BlockSpec(memory_s...  6.33 us
    ppermute x1, starting transfers between devices, body(): row_a = lax.ppermute(row_a, axes, lat_pairs(nlon, nlat, False))  5.19 us
    pallas_call x1, Pallas kernels, body(): pl.pallas_call(pack_columns, in_specs=[pl.BlockSpec(memory_space=pltpu.HB...  2.83 us
    ppermute x1, starting transfers between devices, body(): row_b = lax.ppermute(row_b, axes, lat_pairs(nlon, nlat, True))  2.68 us
    ppermute x1, waiting for transfers between devices, body(): lax.ppermute(col_b, axes, lon_pairs(nlon, nlat, lambda i: (i + 1 if i % 2...  2.06 us
  transfers between devices with their start and end apart: 4, of which 1 were waited for; matrix products, arithmetic and copies ran while one was open for 0% of the time, Pallas kernels for 18%

profile of v5, /device:TPU:24, one launch (start us, length us, event | category | flops | bytes accessed | tf_op | source)
XLA Modules:
  0.0 35.3 jit_solution(6687760960531569067)
XLA Ops:
  0.6 0.0 copy-start.8
  0.6 0.0 copy-start.7
  0.7 0.0 copy-start.6
  0.7 0.0 copy-start.5
  0.7 0.0 copy-start.4
  0.7 0.0 copy-start.3
  0.7 0.0 copy-start.2
  0.7 0.0 copy-start.1
  0.7 0.0 copy-start
  0.7 2.8 %pack_columns.1 = (f32[96,128]{1,0:T(8,128)}, f32[96,128]{1,0:T(8,128)}) custom-call(f32[3,96,256]{2,1,0:T(8,128)} %refs_0_.6, f32[3,96,256]{2,1,0:T(8,128)} %refs_1_.6, f32[3,96,256]{2,1,0:T(8,128)} %refs_2_.6, f32[3,96,256]{2,1,0:T(8,128)} %refs_3_.6, s32[96,256]{1,0:T(8,128)} %refs_0_.7, s32[96,256]{1,0:T(8,128)} %refs_1_.7, f32[96,256]{1,0:T(8,128)} %refs_2_.7, ...), custom_call_target="tpu_custom_call" | custom-call | tf_op jit(solution)/shard_map/pack_columns/pallas_call | solution.py:505
  3.6 7.8 %collective-permute-start = (f32[96,128]{1,0:T(8,128)}, f32[96,128]{1,0:T(8,128)S(1)}, u32[]{:S(2)}, u32[]{:S(2)}) collective-permute-start(f32[96,128]{1,0:T(8,128)} %get-tuple-element.17), channel_id=1, source_target_pairs={{0,248},{1,249},{2,250},{3,251},{4,252},{5,253},{6,254},{7,255},{8... | collective-permute-start | bytes 147464 | tf_op jit(solution)/shard_map/ppermute | solution.py:513
  11.4 0.0 collective-permute-start.1
  11.4 2.1 %collective-permute-done.refs_18_.refs_14_ = f32[96,128]{1,0:T(8,128)S(1)} collective-permute-done((f32[96,128]{1,0:T(8,128)}, f32[96,128]{1,0:T(8,128)S(1)}, u32[]{:S(2)}, u32[]{:S(2)}) %collective-permute-start) | collective-permute-done | bytes 49184 | tf_op jit(solution)/shard_map/ppermute | solution.py:513
  13.5 0.0 collective-permute-done.1.refs_19_.refs_15_
  13.5 0.0 copy-done.8
  13.5 0.0 copy-done.7
  13.5 0.0 copy-done.6
  13.5 0.0 copy-done.5
  13.5 0.0 copy-done.4
  13.5 0.0 copy-done.3
  13.5 0.0 copy-done.2
  13.5 0.0 copy-done.1
  13.5 0.0 copy-done
  13.5 0.1 pack_rows.1
  13.6 2.7 %collective-permute-start.2 = (f32[72,256]{1,0:T(8,128)S(1)}, f32[72,256]{1,0:T(8,128)S(1)}, u32[]{:S(2)}, u32[]{:S(2)}) collective-permute-start(f32[72,256]{1,0:T(8,128)S(1)} %get-tuple-element.29), channel_id=1, source_target_pairs={{1,2},{2,1},{3,4},{4,3},{5,6},{6,5},{7,255},{9,10},{10,9},{11,12},... | collective-permute-start | bytes 221192 | tf_op jit(solution)/shard_map/ppermute | solution.py:538
  16.3 5.2 %collective-permute-start.3 = (f32[72,256]{1,0:T(8,128)S(1)}, f32[72,256]{1,0:T(8,128)S(1)}, u32[]{:S(2)}, u32[]{:S(2)}) collective-permute-start(f32[72,256]{1,0:T(8,128)S(1)} %get-tuple-element.19.refs_9_), channel_id=1, source_target_pairs={{0,1},{1,0},{2,3},{3,2},{4,5},{5,4},{6,7},{7,6},{8,9},{9,8},{10,11... | collective-permute-start | bytes 221192 | tf_op jit(solution)/shard_map/ppermute | solution.py:539
  21.5 6.3 %run_interior.1 = (f32[5,3,2,112,128]{4,3,2,1,0:T(8,128)S(1)}, f32[5,3,2,112,128]{4,3,2,1,0:T(8,128)S(1)}, f32[5,3,2,112,128]{4,3,2,1,0:T(8,128)S(1)}, f32[5,3,2...) custom-call(f32[3,96,256]{2,1,0:T(8,128)S(1)} %copy-done, ...), custom_call_target="tpu_custom_call" | custom-call | flops 30000000 | bytes 16000000 | tf_op jit(solution)/shard_map/run_interior/pallas_call | solution.py:543
  27.8 0.0 collective-permute-done.2.refs_16_
  27.8 0.0 collective-permute-done.3.refs_17_
  27.8 7.5 %run_rims.1 = (f32[3,96,256]{2,1,0:T(8,128)}, f32[3,96,256]{2,1,0:T(8,128)}, f32[3,96,256]{2,1,0:T(8,128)}, f32[3,96,256]{2,1,0:T(8,128)}) custom-call(s32[96,256]{1,0:T(8,128)S(1)} %copy-done.4, s32[96,256]{1,0:T(8,128)S(1)} %copy-done.5, f32[96,256]{1,0:T(8,128)S(1)} %copy-done.6, f32[96,256]{1,0:T(8,128)S(1)} %copy-done.7, f32[96,256]{1,0:T(8,128)S(1)} %copy-done.8, ...), custom_call_target="tpu_custom_call" | custom-call | tf_op jit(solution)/shard_map/run_rims/pallas_call | solution.py:556
Async XLA Ops:
  0.6 12.8 %copy-start.8 = (f32[96,256]{1,0:T(8,128)S(1)}, f32[96,256]{1,0:T(8,128)}, u32[]{:S(2)}) copy-start(f32[96,256]{1,0:T(8,128)} %refs_4_.7) | copy-start | bytes 294916
  0.6 12.8 %copy-start.7 = (f32[96,256]{1,0:T(8,128)S(1)}, f32[96,256]{1,0:T(8,128)}, u32[]{:S(2)}) copy-start(f32[96,256]{1,0:T(8,128)} %refs_3_.7) | copy-start | bytes 294916
  0.7 12.8 %copy-start.6 = (f32[96,256]{1,0:T(8,128)S(1)}, f32[96,256]{1,0:T(8,128)}, u32[]{:S(2)}) copy-start(f32[96,256]{1,0:T(8,128)} %refs_2_.7) | copy-start | bytes 294916
  0.7 12.8 %copy-start.5 = (s32[96,256]{1,0:T(8,128)S(1)}, s32[96,256]{1,0:T(8,128)}, u32[]{:S(2)}) copy-start(s32[96,256]{1,0:T(8,128)} %refs_1_.7) | copy-start | bytes 294916
  0.7 12.8 %copy-start.4 = (s32[96,256]{1,0:T(8,128)S(1)}, s32[96,256]{1,0:T(8,128)}, u32[]{:S(2)}) copy-start(s32[96,256]{1,0:T(8,128)} %refs_0_.7) | copy-start | bytes 294916
  0.7 12.8 %copy-start.3 = (f32[3,96,256]{2,1,0:T(8,128)S(1)}, f32[3,96,256]{2,1,0:T(8,128)}, u32[]{:S(2)}) copy-start(f32[3,96,256]{2,1,0:T(8,128)} %refs_3_.6) | copy-start | bytes 884740
  0.7 12.8 %copy-start.2 = (f32[3,96,256]{2,1,0:T(8,128)S(1)}, f32[3,96,256]{2,1,0:T(8,128)}, u32[]{:S(2)}) copy-start(f32[3,96,256]{2,1,0:T(8,128)} %refs_2_.6) | copy-start | bytes 884740
  0.7 12.8 %copy-start.1 = (f32[3,96,256]{2,1,0:T(8,128)S(1)}, f32[3,96,256]{2,1,0:T(8,128)}, u32[]{:S(2)}) copy-start(f32[3,96,256]{2,1,0:T(8,128)} %refs_1_.6) | copy-start | bytes 884740
  0.7 12.8 %copy-start = (f32[3,96,256]{2,1,0:T(8,128)S(1)}, f32[3,96,256]{2,1,0:T(8,128)}, u32[]{:S(2)}) copy-start(f32[3,96,256]{2,1,0:T(8,128)} %refs_0_.6) | copy-start | bytes 884740
  3.6 9.9 %collective-permute-start = (f32[96,128]{1,0:T(8,128)}, f32[96,128]{1,0:T(8,128)S(1)}, u32[]{:S(2)}, u32[]{:S(2)}) collective-permute-start(f32[96,128]{1,0:T(8,128)} %get-tuple-element.17), channel_id=1, source_target_pairs={{0,248},{1,249},{2,250},{3,251},{4,252},{5,253},{6,254},{7,255},{8... | collective-permute-start | bytes 147464 | tf_op jit(solution)/shard_map/ppermute | solution.py:513
  11.4 2.1 %collective-permute-start.1 = (f32[96,128]{1,0:T(8,128)}, f32[96,128]{1,0:T(8,128)S(1)}, u32[]{:S(2)}, u32[]{:S(2)}) collective-permute-start(f32[96,128]{1,0:T(8,128)} %get-tuple-element.18), channel_id=1, source_target_pairs={{0,8},{1,9},{2,10},{3,11},{4,12},{5,13},{6,14},{7,15},{8,0},{9,1},... | collective-permute-start | bytes 147464 | tf_op jit(solution)/shard_map/ppermute | solution.py:516
  13.6 14.2 %collective-permute-start.2 = (f32[72,256]{1,0:T(8,128)S(1)}, f32[72,256]{1,0:T(8,128)S(1)}, u32[]{:S(2)}, u32[]{:S(2)}) collective-permute-start(f32[72,256]{1,0:T(8,128)S(1)} %get-tuple-element.29), channel_id=1, source_target_pairs={{1,2},{2,1},{3,4},{4,3},{5,6},{6,5},{7,255},{9,10},{10,9},{11,12},... | collective-permute-start | bytes 221192 | tf_op jit(solution)/shard_map/ppermute | solution.py:538
  16.3 11.5 %collective-permute-start.3 = (f32[72,256]{1,0:T(8,128)S(1)}, f32[72,256]{1,0:T(8,128)S(1)}, u32[]{:S(2)}, u32[]{:S(2)}) collective-permute-start(f32[72,256]{1,0:T(8,128)S(1)} %get-tuple-element.19.refs_9_), channel_id=1, source_target_pairs={{0,1},{1,0},{2,3},{3,2},{4,5},{5,4},{6,7},{7,6},{8,9},{9,8},{10,11... | collective-permute-start | bytes 221192 | tf_op jit(solution)/shard_map/ppermute | solution.py:539

commit v6 on v5

--- a/solution.py
+++ b/solution.py
@@ -54,7 +54,7 @@
 
 def pack_rows(*refs):
     south, north = refs[0:9], refs[9:18]
-    col_b, col_a, out_b, out_a = refs[18:]
+    col_b, col_a, _, out_b, out_a = refs[18:]
     rows = col_a.shape[0]
     even = lax.rem(lax.axis_index("lat"), 2) == 0
     for p in range(PLANES):
@@ -213,9 +213,8 @@
     return out
 
 
-def run_interior(*refs):
-    ins, states, outs, strip = refs[:9], refs[10:14], refs[14:18], refs[18]
-    coef, wet = refs[19:]
+def prepare_interior(*refs):
+    ins, (state, coef, strip, wet) = refs[:9], refs[10:]
     rows = ins[4].shape[0]
     tiles = [slice(t * LANES, (t + 1) * LANES) for t in range(2)]
 
@@ -227,7 +226,7 @@
         for f in range(4):
             for k in range(K):
                 for t in range(2):
-                    states[0][f, k, t, at, :] = ins[f][k, own, tiles[t]]
+                    state[f, k, t, at, :] = ins[f][k, own, tiles[t]]
             strip[f, own, :] = strip_of([[ins[f][k, own, tiles[t]] for t in range(2)] for k in range(K)])
         for i in range(5):
             strip[4 + i, own, :] = strip_of([[ins[4 + i][own, tiles[t]].astype(jnp.float32) for t in range(2)]] * K)
@@ -238,7 +237,7 @@
                 wet[k, t, at, :] = jnp.where(sea & (ins[4][own, tiles[t]] > k), 1.0, 0.0)
                 rhos.append(density(ins[T][k, own, tiles[t]], ins[S][k, own, tiles[t]], slope_of(k)))
             for k, value in enumerate(column_pressure(rhos)):
-                states[0][PR, k, t, at, :] = value
+                state[PR, k, t, at, :] = value
 
     @pl.loop(0, rows // 8, unroll=6)
     def _(b):
@@ -254,8 +253,14 @@
             write,
         )
 
+
+def run_interior(*refs):
+    coef, states, outs = refs[1], (refs[0],) + refs[3:6], refs[6:10]
+    rows = outs[0].shape[1]
+    tiles = [slice(t * LANES, (t + 1) * LANES) for t in range(2)]
+
     for step in range(STEPS):
-        @pl.loop(0, rows // 8, unroll=4)
+        @pl.loop(0, rows // 8, unroll=6)
         def _(b):
             r = pl.multiple_of(8 * b + 8, 8)
 
@@ -510,10 +515,27 @@
         compiler_params=pltpu.CompilerParams(vmem_limit_bytes=62 * 1024 * 1024),
         name="pack_columns",
     )(*args)
+    packed = col_b
     col_b = lax.ppermute(
         col_b, axes, lon_pairs(nlon, nlat, lambda i: (i + 1 if i % 2 else i - 1) % nlon)
     )
     col_a = lax.ppermute(col_a, axes, lon_pairs(nlon, nlat, lambda i: i ^ 1))
+
+    state = jax.ShapeDtypeStruct((5, K, 2, rows + 16, LANES), f32)
+    vmem = pl.BlockSpec(memory_space=pltpu.VMEM)
+    state0, coef, strip = pl.pallas_call(
+        prepare_interior,
+        in_specs=[vmem] * 9 + [pl.BlockSpec(memory_space=pl.ANY)],
+        out_shape=(
+            state,
+            jax.ShapeDtypeStruct((11, K, 2, rows + 16, LANES), f32),
+            jax.ShapeDtypeStruct((9, rows, LANES), f32),
+        ),
+        scratch_shapes=[pltpu.VMEM((K, 2, rows + 16, LANES), f32)],
+        compiler_params=params,
+        cost_estimate=pl.CostEstimate(flops=10_000_000, bytes_accessed=8_000_000, transcendentals=0),
+        name="prepare_interior",
+    )(*args, packed)
 
     def edge(block):
         def spec(a):
@@ -528,30 +550,24 @@
     row_b, row_a = pl.pallas_call(
         pack_rows,
         grid=(1,),
-        in_specs=edge(0) + edge(rows // 8 - 1) + [whole, whole],
+        in_specs=edge(0) + edge(rows // 8 - 1) + [whole, whole, pl.BlockSpec(memory_space=pl.ANY)],
         out_specs=(row_spec, row_spec),
         out_shape=(row, row),
         compiler_params=params,
         name="pack_rows",
-    )(*args, *args, col_b, col_a)
-    sent = row_a
+    )(*args, *args, col_b, col_a, strip)
+    sent = row_b
     row_b = lax.ppermute(row_b, axes, lat_pairs(nlon, nlat, True))
     row_a = lax.ppermute(row_a, axes, lat_pairs(nlon, nlat, False))
     out = jax.ShapeDtypeStruct(u_vel.shape, f32)
-    state = jax.ShapeDtypeStruct((5, K, 2, rows + 16, LANES), f32)
-    vmem = pl.BlockSpec(memory_space=pltpu.VMEM)
-    *kept, strip = pl.pallas_call(
+    *kept, = pl.pallas_call(
         run_interior,
-        in_specs=[vmem] * 9 + [pl.BlockSpec(memory_space=pl.ANY)],
-        out_shape=(state,) * 4 + (out,) * 4 + (jax.ShapeDtypeStruct((9, rows, LANES), f32),),
-        scratch_shapes=[
-            pltpu.VMEM((11, K, 2, rows + 16, LANES), f32),
-            pltpu.VMEM((K, 2, rows + 16, LANES), f32),
-        ],
+        in_specs=[vmem] * 2 + [pl.BlockSpec(memory_space=pl.ANY)],
+        out_shape=(state,) * 3 + (out,) * 4,
         compiler_params=params,
         cost_estimate=pl.CostEstimate(flops=30_000_000, bytes_accessed=16_000_000, transcendentals=0),
         name="run_interior",
-    )(*args, sent)
+    )(state0, coef, sent)
     tall = rows + 32
     return pl.pallas_call(
         run_rims,
@@ -570,7 +586,7 @@
         ],
         compiler_params=params,
         name="run_rims",
-    )(*args[4:], *kept, strip, col_b, col_a, row_b, row_a)
+    )(*args[4:], state0, *kept, strip, col_b, col_a, row_b, row_a)
 
 
 def solution(mesh):

time: 35.4 us -> 33.9 us (0.958)
  waiting for transfers between devices: 2.07 us -> 0.03 us
  local copies, waits for them, and re-layouts: 0.04 us -> 0.83 us
    ppermute x1, waiting for transfers between devices: 2.06 us -> 0.02 us  [body(): lax.ppermute(col_b, axes, lon_pairs(nlon, nlat, lambda i: (i + 1 if i % 2...]
    unnamed x18 -> x20, local copies, waits for them, and re-layouts: 0.04 us -> 0.83 us
    pallas_call x1 -> x2, Pallas kernels: 6.33 us -> 6.03 us  [the longest x1 4.87 us: body(): pl.pallas_call(run_interior, in_specs=[vmem] * 2 + [pl.BlockSpec(memory_s...]
  transfers between devices with their start and end apart: 4 -> 4, of which waited for: 1 -> 0; matrix products, arithmetic and copies ran while one was open for 0% -> 0% of each run, Pallas kernels for 18% -> 18%
where the time goes in v6:
time: 33.9 us; the launch traced here: 33.7 us
  Pallas kernels  16.4 us (48%)
  starting transfers between devices  15.7 us (46%)
  local copies, waits for them, and re-layouts  0.83 us (2%)
  between operations  0.83 us (2%)
    ppermute x1, starting transfers between devices, body(): lax.ppermute(col_b, axes, lon_pairs(nlon, nlat, lambda i: (i + 1 if i % 2...  7.84 us
    pallas_call x1, Pallas kernels, body(): pl.pallas_call(run_rims, out_shape=(out,) * 4, scratch_shapes=[pltpu.VMEM...  7.47 us
    ppermute x1, starting transfers between devices, body(): row_a = lax.ppermute(row_a, axes, lat_pairs(nlon, nlat, False))  5.17 us
    pallas_call x1, Pallas kernels, body(): pl.pallas_call(run_interior, in_specs=[vmem] * 2 + [pl.BlockSpec(memory_s...  4.87 us
    pallas_call x1, Pallas kernels, body(): pl.pallas_call(pack_columns, in_specs=[pl.BlockSpec(memory_space=pltpu.HB...  2.81 us
    ppermute x1, starting transfers between devices, body(): row_b = lax.ppermute(row_b, axes, lat_pairs(nlon, nlat, True))  2.68 us
    pallas_call x1, Pallas kernels, body(): pl.pallas_call(prepare_interior, in_specs=[vmem] * 9 + [pl.BlockSpec(memo...  1.15 us
    unnamed x20, local copies, waits for them, and re-layouts  0.83 us
  transfers between devices with their start and end apart: 4, of which 0 were waited for; matrix products, arithmetic and copies ran while one was open for 0% of the time, Pallas kernels for 18%

profile of v6, /device:TPU:24, one launch (start us, length us, event | category | flops | bytes accessed | tf_op | source)
XLA Modules:
  0.0 33.7 jit_solution(3651460690852498618)
XLA Ops:
  0.6 0.0 copy-start.1
  0.6 0.0 copy-start.2
  0.7 0.0 copy-start.3
  0.7 0.0 copy-start.4
  0.7 0.0 copy-start.5
  0.7 0.0 copy-start.6
  0.7 0.0 copy-start.7
  0.7 0.0 copy-start.8
  0.7 0.0 copy-start
  0.7 2.8 %pack_columns.1 = (f32[96,128]{1,0:T(8,128)}, f32[96,128]{1,0:T(8,128)}) custom-call(f32[3,96,256]{2,1,0:T(8,128)} %refs_9_.1, f32[3,96,256]{2,1,0:T(8,128)} %refs_10_.1, f32[3,96,256]{2,1,0:T(8,128)} %refs_11_.1, f32[3,96,256]{2,1,0:T(8,128)} %refs_12_.1, s32[96,256]{1,0:T(8,128)} %refs_0_.7, s32[96,256]{1,0:T(8,128)} %refs_1_.7, f32[96,256]{1,0:T(8,128)} %refs_2_.7, ...), custom_call_target="tpu_custom_call" | custom-call | tf_op jit(solution)/shard_map/pack_columns/pallas_call | solution.py:510
  3.5 7.8 %collective-permute-start = (f32[96,128]{1,0:T(8,128)}, f32[96,128]{1,0:T(8,128)S(1)}, u32[]{:S(2)}, u32[]{:S(2)}) collective-permute-start(f32[96,128]{1,0:T(8,128)} %get-tuple-element.18.refs_9_), channel_id=1, source_target_pairs={{0,248},{1,249},{2,250},{3,251},{4,252},{5,253},{6,254},{7,255},{8... | collective-permute-start | bytes 147464 | tf_op jit(solution)/shard_map/ppermute | solution.py:519
  11.4 0.0 collective-permute-start.1
  11.4 0.0 copy-done.1
  11.4 0.0 copy-done.2
  11.4 0.0 copy-done.3
  11.4 0.0 copy-done.4
  11.4 0.0 copy-done.5
  11.4 0.0 copy-done.6
  11.4 0.0 copy-done.7
  11.4 0.0 copy-done.8
  11.5 0.0 copy-done
  11.5 0.0 copy-start.9
  11.5 0.8 %copy-done.9 = f32[96,128]{1,0:T(8,128)S(1)} copy-done((f32[96,128]{1,0:T(8,128)S(1)}, f32[96,128]{1,0:T(8,128)}, u32[]{:S(2)}) %copy-start.9) | copy-done | bytes 49176
  12.3 1.2 %prepare_interior.1 = (f32[5,3,2,112,128]{4,3,2,1,0:T(8,128)S(1)}, f32[11,3,2,112,128]{4,3,2,1,0:T(8,128)S(1)}, f32[9,96,128]{2,1,0:T(8,128)S(1)}) custom-call(f32[3,96,256]{2,1,0:T(8,128)S(1)} %copy-done, f32[3,96,256]{2,1,0:T(8,128)S(1)} %copy-done.1, f32[3,96,256]{2,1,0:T(8,128)S(1)} %copy-done.2, f32[3,96,256]{2,1,0:T(8,128)S(1)} %copy-done.3, ...), custom_call_target="tpu_custom_call" | custom-call | flops 10000000 | bytes 8000000 | tf_op jit(solution)/shard_map/prepare_interior/pallas_call | solution.py:526
  13.4 0.0 collective-permute-done.refs_18_.refs_14_
  13.5 0.0 collective-permute-done.1.refs_19_.refs_15_
  13.5 2.7 %collective-permute-start.2 = (f32[72,256]{1,0:T(8,128)S(1)}, f32[72,256]{1,0:T(8,128)S(1)}, u32[]{:S(2)}, u32[]{:S(2)}) collective-permute-start(f32[72,256]{1,0:T(8,128)S(1)} %get-tuple-element.23.refs_2_), channel_id=1, source_target_pairs={{1,2},{2,1},{3,4},{4,3},{5,6},{6,5},{7,255},{9,10},{10,9},{11,12},... | collective-permute-start | bytes 221192 | tf_op jit(solution)/shard_map/ppermute | solution.py:560
  16.2 5.2 %collective-permute-start.3 = (f32[72,256]{1,0:T(8,128)S(1)}, f32[72,256]{1,0:T(8,128)S(1)}, u32[]{:S(2)}, u32[]{:S(2)}) collective-permute-start(f32[72,256]{1,0:T(8,128)S(1)} %get-tuple-element.31), channel_id=1, source_target_pairs={{0,1},{1,0},{2,3},{3,2},{4,5},{5,4},{6,7},{7,6},{8,9},{9,8},{10,11... | collective-permute-start | bytes 221192 | tf_op jit(solution)/shard_map/ppermute | solution.py:561
  21.4 4.9 %run_interior.1 = (f32[5,3,2,112,128]{4,3,2,1,0:T(8,128)S(1)}, f32[5,3,2,112,128]{4,3,2,1,0:T(8,128)S(1)}, f32[5,3,2,112,128]{4,3,2,1,0:T(8,128)S(1)}, f32[3,96,...) custom-call(f32[5,3,2,112,128]{4,3,2,1,0:T(8,128)S(1)} %get-tuple-element.1, ...), custom_call_target="tpu_custom_call" | custom-call | flops 30000000 | bytes 16000000 | tf_op jit(solution)/shard_map/run_interior/pallas_call | solution.py:563
  26.3 0.0 collective-permute-done.2.refs_16_
  26.3 0.0 collective-permute-done.3.refs_17_
  26.3 7.5 %run_rims.1 = (f32[3,96,256]{2,1,0:T(8,128)}, f32[3,96,256]{2,1,0:T(8,128)}, f32[3,96,256]{2,1,0:T(8,128)}, f32[3,96,256]{2,1,0:T(8,128)}) custom-call(s32[96,256]{1,0:T(8,128)S(1)} %copy-done.4, s32[96,256]{1,0:T(8,128)S(1)} %copy-done.5, f32[96,256]{1,0:T(8,128)S(1)} %copy-done.6, f32[96,256]{1,0:T(8,128)S(1)} %copy-done.7, f32[96,256]{1,0:T(8,128)S(1)} %copy-done.8, ...), custom_call_target="tpu_custom_call" | custom-call | tf_op jit(solution)/shard_map/run_rims/pallas_call | solution.py:572
  (1 shorter events, 0.0 us)
Async XLA Ops:
  0.6 10.8 %copy-start.1 = (f32[3,96,256]{2,1,0:T(8,128)S(1)}, f32[3,96,256]{2,1,0:T(8,128)}, u32[]{:S(2)}) copy-start(f32[3,96,256]{2,1,0:T(8,128)} %refs_10_.1) | copy-start | bytes 884740
  0.6 10.7 %copy-start.2 = (f32[3,96,256]{2,1,0:T(8,128)S(1)}, f32[3,96,256]{2,1,0:T(8,128)}, u32[]{:S(2)}) copy-start(f32[3,96,256]{2,1,0:T(8,128)} %refs_11_.1) | copy-start | bytes 884740
  0.7 10.7 %copy-start.3 = (f32[3,96,256]{2,1,0:T(8,128)S(1)}, f32[3,96,256]{2,1,0:T(8,128)}, u32[]{:S(2)}) copy-start(f32[3,96,256]{2,1,0:T(8,128)} %refs_12_.1) | copy-start | bytes 884740
  0.7 10.7 %copy-start.4 = (s32[96,256]{1,0:T(8,128)S(1)}, s32[96,256]{1,0:T(8,128)}, u32[]{:S(2)}) copy-start(s32[96,256]{1,0:T(8,128)} %refs_0_.7) | copy-start | bytes 294916
  0.7 10.7 %copy-start.5 = (s32[96,256]{1,0:T(8,128)S(1)}, s32[96,256]{1,0:T(8,128)}, u32[]{:S(2)}) copy-start(s32[96,256]{1,0:T(8,128)} %refs_1_.7) | copy-start | bytes 294916
  0.7 10.7 %copy-start.6 = (f32[96,256]{1,0:T(8,128)S(1)}, f32[96,256]{1,0:T(8,128)}, u32[]{:S(2)}) copy-start(f32[96,256]{1,0:T(8,128)} %refs_2_.7) | copy-start | bytes 294916
  0.7 10.7 %copy-start.7 = (f32[96,256]{1,0:T(8,128)S(1)}, f32[96,256]{1,0:T(8,128)}, u32[]{:S(2)}) copy-start(f32[96,256]{1,0:T(8,128)} %refs_3_.7) | copy-start | bytes 294916
  0.7 10.7 %copy-start.8 = (f32[96,256]{1,0:T(8,128)S(1)}, f32[96,256]{1,0:T(8,128)}, u32[]{:S(2)}) copy-start(f32[96,256]{1,0:T(8,128)} %refs_4_.7) | copy-start | bytes 294916
  0.7 10.7 %copy-start = (f32[3,96,256]{2,1,0:T(8,128)S(1)}, f32[3,96,256]{2,1,0:T(8,128)}, u32[]{:S(2)}) copy-start(f32[3,96,256]{2,1,0:T(8,128)} %refs_9_.1) | copy-start | bytes 884740
  3.5 9.9 %collective-permute-start = (f32[96,128]{1,0:T(8,128)}, f32[96,128]{1,0:T(8,128)S(1)}, u32[]{:S(2)}, u32[]{:S(2)}) collective-permute-start(f32[96,128]{1,0:T(8,128)} %get-tuple-element.18.refs_9_), channel_id=1, source_target_pairs={{0,248},{1,249},{2,250},{3,251},{4,252},{5,253},{6,254},{7,255},{8... | collective-permute-start | bytes 147464 | tf_op jit(solution)/shard_map/ppermute | solution.py:519
  11.4 2.1 %collective-permute-start.1 = (f32[96,128]{1,0:T(8,128)}, f32[96,128]{1,0:T(8,128)S(1)}, u32[]{:S(2)}, u32[]{:S(2)}) collective-permute-start(f32[96,128]{1,0:T(8,128)} %get-tuple-element.21), channel_id=1, source_target_pairs={{0,8},{1,9},{2,10},{3,11},{4,12},{5,13},{6,14},{7,15},{8,0},{9,1},... | collective-permute-start | bytes 147464 | tf_op jit(solution)/shard_map/ppermute | solution.py:522
  11.5 0.8 %copy-start.9 = (f32[96,128]{1,0:T(8,128)S(1)}, f32[96,128]{1,0:T(8,128)}, u32[]{:S(2)}) copy-start(f32[96,128]{1,0:T(8,128)} %get-tuple-element.18.refs_9_) | copy-start | bytes 147460
  13.5 12.7 %collective-permute-start.2 = (f32[72,256]{1,0:T(8,128)S(1)}, f32[72,256]{1,0:T(8,128)S(1)}, u32[]{:S(2)}, u32[]{:S(2)}) collective-permute-start(f32[72,256]{1,0:T(8,128)S(1)} %get-tuple-element.23.refs_2_), channel_id=1, source_target_pairs={{1,2},{2,1},{3,4},{4,3},{5,6},{6,5},{7,255},{9,10},{10,9},{11,12},... | collective-permute-start | bytes 221192 | tf_op jit(solution)/shard_map/ppermute | solution.py:560
  16.2 10.1 %collective-permute-start.3 = (f32[72,256]{1,0:T(8,128)S(1)}, f32[72,256]{1,0:T(8,128)S(1)}, u32[]{:S(2)}, u32[]{:S(2)}) collective-permute-start(f32[72,256]{1,0:T(8,128)S(1)} %get-tuple-element.31), channel_id=1, source_target_pairs={{0,1},{1,0},{2,3},{3,2},{4,5},{5,4},{6,7},{7,6},{8,9},{9,8},{10,11... | collective-permute-start | bytes 221192 | tf_op jit(solution)/shard_map/ppermute | solution.py:561

commit v7 on v6

--- a/solution.py
+++ b/solution.py
@@ -42,11 +42,11 @@
         for r in blocks:
             w = plane_values(ins, p, slice(r, r + 8), slice(0, LANES))
             e = plane_values(ins, p, slice(r, r + 8), slice(cols - LANES, cols))
-            w = pltpu.roll(w, 4 * p, 1) if p else w
-            e = pltpu.roll(e, (4 * p + HALO) % LANES, 1)
-            mine = lane >= 4 * p
-            west[r] = jnp.where(mine, w, west[r]) if p else w
-            east[r] = jnp.where(mine, e, east[r]) if p else e
+            x = pltpu.roll(jnp.where(lane < LANES // 2, w, e), 4 * p + HALO, 1)
+            west[r] = jnp.where(lane >= 4 * p + HALO, x, west[r]) if p else x
+            east[r] = jnp.where(lane >= 4 * p, x, east[r]) if p else x
+    for r in blocks:
+        west[r] = pltpu.roll(west[r], LANES - HALO, 1)
     for r in blocks:
         out_a[r : r + 8, :] = jnp.where(even, east[r], west[r])
         out_b[r : r + 8, :] = jnp.where(even, west[r], east[r])
@@ -214,7 +214,7 @@
 
 
 def prepare_interior(*refs):
-    ins, (state, coef, strip, wet) = refs[:9], refs[10:]
+    ins, (state, coef, strip, wet) = refs[:9], refs[9:]
     rows = ins[4].shape[0]
     tiles = [slice(t * LANES, (t + 1) * LANES) for t in range(2)]
 
@@ -425,7 +425,7 @@
     for step in range(STEPS):
         final = step == STEPS - 1
 
-        @pl.loop(0, 2 if final else 4, unroll=2)
+        @pl.loop(0, 2 if final else 4, unroll=2 if final else 4)
         def _(n):
             side = n if final else lax.div(n, 2)
             r = pl.multiple_of(16 + 0 * n if final else 8 + 8 * (lax.rem(n, 2) + side), 8)
@@ -515,7 +515,6 @@
         compiler_params=pltpu.CompilerParams(vmem_limit_bytes=62 * 1024 * 1024),
         name="pack_columns",
     )(*args)
-    packed = col_b
     col_b = lax.ppermute(
         col_b, axes, lon_pairs(nlon, nlat, lambda i: (i + 1 if i % 2 else i - 1) % nlon)
     )
@@ -525,7 +524,7 @@
     vmem = pl.BlockSpec(memory_space=pltpu.VMEM)
     state0, coef, strip = pl.pallas_call(
         prepare_interior,
-        in_specs=[vmem] * 9 + [pl.BlockSpec(memory_space=pl.ANY)],
+        in_specs=[vmem] * 9,
         out_shape=(
             state,
             jax.ShapeDtypeStruct((11, K, 2, rows + 16, LANES), f32),
@@ -535,7 +534,7 @@
         compiler_params=params,
         cost_estimate=pl.CostEstimate(flops=10_000_000, bytes_accessed=8_000_000, transcendentals=0),
         name="prepare_interior",
-    )(*args, packed)
+    )(*args)
 
     def edge(block):
         def spec(a):

time: 33.9 us -> 32.4 us (0.956)
  Pallas kernels: 16.4 us -> 14.9 us
  local copies, waits for them, and re-layouts: 0.83 us -> 0.04 us
  waiting for transfers between devices: 0.03 us -> 0.82 us
    pallas_call x1, Pallas kernels: 7.47 us -> 6.13 us  [body(): pl.pallas_call(run_rims, out_shape=(out,) * 4, scratch_shapes=[pltpu.VMEM...]
    ppermute x1, waiting for transfers between devices: 0.02 us -> 0.82 us  [body(): lax.ppermute(col_b, axes, lon_pairs(nlon, nlat, lambda i: (i + 1 if i % 2...]
    unnamed x20 -> x18, local copies, waits for them, and re-layouts: 0.83 us -> 0.04 us
  transfers between devices with their start and end apart: 4 -> 4, of which waited for: 0 -> 1; matrix products, arithmetic and copies ran while one was open for 0% -> 0% of each run, Pallas kernels for 18% -> 19%
where the time goes in v7:
time: 32.4 us; the launch traced here: 32.3 us
  starting transfers between devices  15.7 us (48%)
  Pallas kernels  14.9 us (46%)
  waiting for transfers between devices  0.82 us (3%)
  between operations  0.82 us (3%)
    ppermute x1, starting transfers between devices, body(): lax.ppermute(col_b, axes, lon_pairs(nlon, nlat, lambda i: (i + 1 if i % 2...  7.84 us
    pallas_call x1, Pallas kernels, body(): pl.pallas_call(run_rims, out_shape=(out,) * 4, scratch_shapes=[pltpu.VMEM...  6.13 us
    ppermute x1, starting transfers between devices, body(): row_a = lax.ppermute(row_a, axes, lat_pairs(nlon, nlat, False))  5.18 us
    pallas_call x1, Pallas kernels, body(): pl.pallas_call(run_interior, in_specs=[vmem] * 2 + [pl.BlockSpec(memory_s...  4.87 us
    pallas_call x1, Pallas kernels, body(): pl.pallas_call(pack_columns, in_specs=[pl.BlockSpec(memory_space=pltpu.HB...  2.69 us
    ppermute x1, starting transfers between devices, body(): row_b = lax.ppermute(row_b, axes, lat_pairs(nlon, nlat, True))  2.68 us
    pallas_call x1, Pallas kernels, body(): pl.pallas_call(prepare_interior, in_specs=[vmem] * 9, out_shape=(state, j...  1.16 us
    ppermute x1, waiting for transfers between devices, body(): lax.ppermute(col_b, axes, lon_pairs(nlon, nlat, lambda i: (i + 1 if i % 2...  0.82 us
  transfers between devices with their start and end apart: 4, of which 1 were waited for; matrix products, arithmetic and copies ran while one was open for 0% of the time, Pallas kernels for 19%

profile of v7, /device:TPU:24, one launch (start us, length us, event | category | flops | bytes accessed | tf_op | source)
XLA Modules:
  0.0 32.3 jit_solution(1119098098001124371)
XLA Ops:
  0.6 0.0 copy-start.1
  0.6 0.0 copy-start.2
  0.7 0.0 copy-start.3
  0.7 0.0 copy-start.4
  0.7 0.0 copy-start.5
  0.7 0.0 copy-start.6
  0.7 0.0 copy-start.7
  0.7 0.0 copy-start.8
  0.7 0.0 copy-start
  0.7 2.7 %pack_columns.1 = (f32[96,128]{1,0:T(8,128)}, f32[96,128]{1,0:T(8,128)}) custom-call(f32[3,96,256]{2,1,0:T(8,128)} %refs_9_.1, f32[3,96,256]{2,1,0:T(8,128)} %refs_10_.1, f32[3,96,256]{2,1,0:T(8,128)} %refs_11_.1, f32[3,96,256]{2,1,0:T(8,128)} %refs_12_.1, s32[96,256]{1,0:T(8,128)} %refs_0_.7, s32[96,256]{1,0:T(8,128)} %refs_1_.7, f32[96,256]{1,0:T(8,128)} %refs_2_.7, ...), custom_call_target="tpu_custom_call" | custom-call | tf_op jit(solution)/shard_map/pack_columns/pallas_call | solution.py:510
  3.4 7.8 %collective-permute-start = (f32[96,128]{1,0:T(8,128)}, f32[96,128]{1,0:T(8,128)S(1)}, u32[]{:S(2)}, u32[]{:S(2)}) collective-permute-start(f32[96,128]{1,0:T(8,128)} %get-tuple-element.20), channel_id=1, source_target_pairs={{0,248},{1,249},{2,250},{3,251},{4,252},{5,253},{6,254},{7,255},{8... | collective-permute-start | bytes 147464 | tf_op jit(solution)/shard_map/ppermute | solution.py:518
  11.3 0.0 collective-permute-start.1
  11.3 0.0 copy-done.1
  11.3 0.0 copy-done.2
  11.3 0.0 copy-done.3
  11.3 0.0 copy-done.4
  11.3 0.0 copy-done.5
  11.3 0.0 copy-done.6
  11.3 0.0 copy-done.7
  11.3 0.0 copy-done.8
  11.3 0.0 copy-done
  11.3 1.2 %prepare_interior.1 = (f32[5,3,2,112,128]{4,3,2,1,0:T(8,128)S(1)}, f32[11,3,2,112,128]{4,3,2,1,0:T(8,128)S(1)}, f32[9,96,128]{2,1,0:T(8,128)S(1)}) custom-call(f32[3,96,256]{2,1,0:T(8,128)S(1)} %copy-done, f32[3,96,256]{2,1,0:T(8,128)S(1)} %copy-done.1, f32[3,96,256]{2,1,0:T(8,128)S(1)} %copy-done.2, f32[3,96,256]{2,1,0:T(8,128)S(1)} %copy-done.3, ...), custom_call_target="tpu_custom_call" | custom-call | flops 10000000 | bytes 8000000 | tf_op jit(solution)/shard_map/prepare_interior/pallas_call | solution.py:525
  12.5 0.8 %collective-permute-done.refs_18_.refs_14_ = f32[96,128]{1,0:T(8,128)S(1)} collective-permute-done((f32[96,128]{1,0:T(8,128)}, f32[96,128]{1,0:T(8,128)S(1)}, u32[]{:S(2)}, u32[]{:S(2)}) %collective-permute-start) | collective-permute-done | bytes 49184 | tf_op jit(solution)/shard_map/ppermute | solution.py:518
  13.3 0.0 collective-permute-done.1.refs_19_.refs_15_
  13.4 2.7 %collective-permute-start.2 = (f32[72,256]{1,0:T(8,128)S(1)}, f32[72,256]{1,0:T(8,128)S(1)}, u32[]{:S(2)}, u32[]{:S(2)}) collective-permute-start(f32[72,256]{1,0:T(8,128)S(1)} %get-tuple-element.23.refs_2_), channel_id=1, source_target_pairs={{1,2},{2,1},{3,4},{4,3},{5,6},{6,5},{7,255},{9,10},{10,9},{11,12},... | collective-permute-start | bytes 221192 | tf_op jit(solution)/shard_map/ppermute | solution.py:559
  16.1 5.2 %collective-permute-start.3 = (f32[72,256]{1,0:T(8,128)S(1)}, f32[72,256]{1,0:T(8,128)S(1)}, u32[]{:S(2)}, u32[]{:S(2)}) collective-permute-start(f32[72,256]{1,0:T(8,128)S(1)} %get-tuple-element.31), channel_id=1, source_target_pairs={{0,1},{1,0},{2,3},{3,2},{4,5},{5,4},{6,7},{7,6},{8,9},{9,8},{10,11... | collective-permute-start | bytes 221192 | tf_op jit(solution)/shard_map/ppermute | solution.py:560
  21.2 4.9 %run_interior.1 = (f32[5,3,2,112,128]{4,3,2,1,0:T(8,128)S(1)}, f32[5,3,2,112,128]{4,3,2,1,0:T(8,128)S(1)}, f32[5,3,2,112,128]{4,3,2,1,0:T(8,128)S(1)}, f32[3,96,...) custom-call(f32[5,3,2,112,128]{4,3,2,1,0:T(8,128)S(1)} %get-tuple-element.1, ...), custom_call_target="tpu_custom_call" | custom-call | flops 30000000 | bytes 16000000 | tf_op jit(solution)/shard_map/run_interior/pallas_call | solution.py:562
  26.1 0.0 collective-permute-done.2.refs_16_
  26.1 0.0 collective-permute-done.3.refs_17_
  26.1 6.1 %run_rims.1 = (f32[3,96,256]{2,1,0:T(8,128)}, f32[3,96,256]{2,1,0:T(8,128)}, f32[3,96,256]{2,1,0:T(8,128)}, f32[3,96,256]{2,1,0:T(8,128)}) custom-call(s32[96,256]{1,0:T(8,128)S(1)} %copy-done.4, s32[96,256]{1,0:T(8,128)S(1)} %copy-done.5, f32[96,256]{1,0:T(8,128)S(1)} %copy-done.6, f32[96,256]{1,0:T(8,128)S(1)} %copy-done.7, f32[96,256]{1,0:T(8,128)S(1)} %copy-done.8, ...), custom_call_target="tpu_custom_call" | custom-call | tf_op jit(solution)/shard_map/run_rims/pallas_call | solution.py:571
  (1 shorter events, 0.0 us)
Async XLA Ops:
  0.6 10.6 %copy-start.1 = (f32[3,96,256]{2,1,0:T(8,128)S(1)}, f32[3,96,256]{2,1,0:T(8,128)}, u32[]{:S(2)}) copy-start(f32[3,96,256]{2,1,0:T(8,128)} %refs_10_.1) | copy-start | bytes 884740
  0.6 10.6 %copy-start.2 = (f32[3,96,256]{2,1,0:T(8,128)S(1)}, f32[3,96,256]{2,1,0:T(8,128)}, u32[]{:S(2)}) copy-start(f32[3,96,256]{2,1,0:T(8,128)} %refs_11_.1) | copy-start | bytes 884740
  0.7 10.6 %copy-start.3 = (f32[3,96,256]{2,1,0:T(8,128)S(1)}, f32[3,96,256]{2,1,0:T(8,128)}, u32[]{:S(2)}) copy-start(f32[3,96,256]{2,1,0:T(8,128)} %refs_12_.1) | copy-start | bytes 884740
  0.7 10.6 %copy-start.4 = (s32[96,256]{1,0:T(8,128)S(1)}, s32[96,256]{1,0:T(8,128)}, u32[]{:S(2)}) copy-start(s32[96,256]{1,0:T(8,128)} %refs_0_.7) | copy-start | bytes 294916
  0.7 10.6 %copy-start.5 = (s32[96,256]{1,0:T(8,128)S(1)}, s32[96,256]{1,0:T(8,128)}, u32[]{:S(2)}) copy-start(s32[96,256]{1,0:T(8,128)} %refs_1_.7) | copy-start | bytes 294916
  0.7 10.6 %copy-start.6 = (f32[96,256]{1,0:T(8,128)S(1)}, f32[96,256]{1,0:T(8,128)}, u32[]{:S(2)}) copy-start(f32[96,256]{1,0:T(8,128)} %refs_2_.7) | copy-start | bytes 294916
  0.7 10.6 %copy-start.7 = (f32[96,256]{1,0:T(8,128)S(1)}, f32[96,256]{1,0:T(8,128)}, u32[]{:S(2)}) copy-start(f32[96,256]{1,0:T(8,128)} %refs_3_.7) | copy-start | bytes 294916
  0.7 10.6 %copy-start.8 = (f32[96,256]{1,0:T(8,128)S(1)}, f32[96,256]{1,0:T(8,128)}, u32[]{:S(2)}) copy-start(f32[96,256]{1,0:T(8,128)} %refs_4_.7) | copy-start | bytes 294916
  0.7 10.6 %copy-start = (f32[3,96,256]{2,1,0:T(8,128)S(1)}, f32[3,96,256]{2,1,0:T(8,128)}, u32[]{:S(2)}) copy-start(f32[3,96,256]{2,1,0:T(8,128)} %refs_9_.1) | copy-start | bytes 884740
  3.4 9.9 %collective-permute-start = (f32[96,128]{1,0:T(8,128)}, f32[96,128]{1,0:T(8,128)S(1)}, u32[]{:S(2)}, u32[]{:S(2)}) collective-permute-start(f32[96,128]{1,0:T(8,128)} %get-tuple-element.20), channel_id=1, source_target_pairs={{0,248},{1,249},{2,250},{3,251},{4,252},{5,253},{6,254},{7,255},{8... | collective-permute-start | bytes 147464 | tf_op jit(solution)/shard_map/ppermute | solution.py:518
  11.3 2.1 %collective-permute-start.1 = (f32[96,128]{1,0:T(8,128)}, f32[96,128]{1,0:T(8,128)S(1)}, u32[]{:S(2)}, u32[]{:S(2)}) collective-permute-start(f32[96,128]{1,0:T(8,128)} %get-tuple-element.21), channel_id=1, source_target_pairs={{0,8},{1,9},{2,10},{3,11},{4,12},{5,13},{6,14},{7,15},{8,0},{9,1},... | collective-permute-start | bytes 147464 | tf_op jit(solution)/shard_map/ppermute | solution.py:521
  13.4 12.8 %collective-permute-start.2 = (f32[72,256]{1,0:T(8,128)S(1)}, f32[72,256]{1,0:T(8,128)S(1)}, u32[]{:S(2)}, u32[]{:S(2)}) collective-permute-start(f32[72,256]{1,0:T(8,128)S(1)} %get-tuple-element.23.refs_2_), channel_id=1, source_target_pairs={{1,2},{2,1},{3,4},{4,3},{5,6},{6,5},{7,255},{9,10},{10,9},{11,12},... | collective-permute-start | bytes 221192 | tf_op jit(solution)/shard_map/ppermute | solution.py:559
  16.1 10.1 %collective-permute-start.3 = (f32[72,256]{1,0:T(8,128)S(1)}, f32[72,256]{1,0:T(8,128)S(1)}, u32[]{:S(2)}, u32[]{:S(2)}) collective-permute-start(f32[72,256]{1,0:T(8,128)S(1)} %get-tuple-element.31), channel_id=1, source_target_pairs={{0,1},{1,0},{2,3},{3,2},{4,5},{5,4},{6,7},{7,6},{8,9},{9,8},{10,11... | collective-permute-start | bytes 221192 | tf_op jit(solution)/shard_map/ppermute | solution.py:560

commit v8 on v7

--- a/solution.py
+++ b/solution.py
@@ -214,7 +214,7 @@
 
 
 def prepare_interior(*refs):
-    ins, (state, coef, strip, wet) = refs[:9], refs[9:]
+    ins, (state, coef, strip, after, wet) = refs[:9], refs[9:]
     rows = ins[4].shape[0]
     tiles = [slice(t * LANES, (t + 1) * LANES) for t in range(2)]
 
@@ -253,13 +253,27 @@
             write,
         )
 
+    @pl.loop(0, rows // 8, unroll=6)
+    def _(b):
+        r = pl.multiple_of(8 * b + 8, 8)
+
+        def write(f, k, t, value):
+            after[f, k, t, pl.ds(r, 8), :] = value
+
+        advance_tiles(
+            lambda f, k, t, row: state[f, k, t, pl.ds(row, 8), :],
+            lambda i, k, t, row: coef[i, k, t, pl.ds(row, 8), :],
+            r,
+            write,
+        )
+
 
 def run_interior(*refs):
-    coef, states, outs = refs[1], (refs[0],) + refs[3:6], refs[6:10]
+    coef, states, outs = refs[1], (None, refs[0]) + refs[3:5], refs[5:9]
     rows = outs[0].shape[1]
     tiles = [slice(t * LANES, (t + 1) * LANES) for t in range(2)]
 
-    for step in range(STEPS):
+    for step in range(1, STEPS):
         @pl.loop(0, rows // 8, unroll=6)
         def _(b):
             r = pl.multiple_of(8 * b + 8, 8)
@@ -522,13 +536,14 @@
 
     state = jax.ShapeDtypeStruct((5, K, 2, rows + 16, LANES), f32)
     vmem = pl.BlockSpec(memory_space=pltpu.VMEM)
-    state0, coef, strip = pl.pallas_call(
+    state0, coef, strip, state1 = pl.pallas_call(
         prepare_interior,
         in_specs=[vmem] * 9,
         out_shape=(
             state,
             jax.ShapeDtypeStruct((11, K, 2, rows + 16, LANES), f32),
             jax.ShapeDtypeStruct((9, rows, LANES), f32),
+            state,
         ),
         scratch_shapes=[pltpu.VMEM((K, 2, rows + 16, LANES), f32)],
         compiler_params=params,
@@ -555,18 +570,18 @@
         compiler_params=params,
         name="pack_rows",
     )(*args, *args, col_b, col_a, strip)
-    sent = row_b
+    sent = row_a
     row_b = lax.ppermute(row_b, axes, lat_pairs(nlon, nlat, True))
     row_a = lax.ppermute(row_a, axes, lat_pairs(nlon, nlat, False))
     out = jax.ShapeDtypeStruct(u_vel.shape, f32)
     *kept, = pl.pallas_call(
         run_interior,
         in_specs=[vmem] * 2 + [pl.BlockSpec(memory_space=pl.ANY)],
-        out_shape=(state,) * 3 + (out,) * 4,
+        out_shape=(state,) * 2 + (out,) * 4,
         compiler_params=params,
         cost_estimate=pl.CostEstimate(flops=30_000_000, bytes_accessed=16_000_000, transcendentals=0),
         name="run_interior",
-    )(state0, coef, sent)
+    )(state1, coef, sent)
     tall = rows + 32
     return pl.pallas_call(
         run_rims,
@@ -585,7 +600,7 @@
         ],
         compiler_params=params,
         name="run_rims",
-    )(*args[4:], state0, *kept, strip, col_b, col_a, row_b, row_a)
+    )(*args[4:], state0, state1, *kept, strip, col_b, col_a, row_b, row_a)
 
 
 def solution(mesh):

time: 32.4 us -> 31.2 us (0.963)
  waiting for transfers between devices: 0.82 us -> 0.01 us
  starting transfers between devices: 15.7 us -> 15.3 us
    pallas_call x1, Pallas kernels: 1.16 us -> 2.38 us  [body(): pl.pallas_call(prepare_interior, in_specs=[vmem] * 9, out_shape=(state, j...]
    pallas_call x1, Pallas kernels: 4.87 us -> 3.65 us  [body(): pl.pallas_call(run_interior, in_specs=[vmem] * 2 + [pl.BlockSpec(memory_s...]
    ppermute x1, waiting for transfers between devices: 0.82 us -> 0.01 us  [body(): lax.ppermute(col_b, axes, lon_pairs(nlon, nlat, lambda i: (i + 1 if i % 2...]
    ppermute x1, starting transfers between devices: 5.18 us -> 4.74 us  [body(): row_a = lax.ppermute(row_a, axes, lat_pairs(nlon, nlat, False))]
  transfers between devices with their start and end apart: 4 -> 4, of which waited for: 1 -> 0; matrix products, arithmetic and copies ran while one was open for 0% -> 0% of each run, Pallas kernels for 19% -> 19%
where the time goes in v8:
time: 31.2 us; the launch traced here: 31.1 us
  starting transfers between devices  15.3 us (49%)
  Pallas kernels  14.9 us (48%)
  between operations  0.83 us (3%)
    ppermute x1, starting transfers between devices, body(): lax.ppermute(col_b, axes, lon_pairs(nlon, nlat, lambda i: (i + 1 if i % 2...  7.84 us
    pallas_call x1, Pallas kernels, body(): pl.pallas_call(run_rims, out_shape=(out,) * 4, scratch_shapes=[pltpu.VMEM...  6.13 us
    ppermute x1, starting transfers between devices, body(): row_a = lax.ppermute(row_a, axes, lat_pairs(nlon, nlat, False))  4.74 us
    pallas_call x1, Pallas kernels, body(): pl.pallas_call(run_interior, in_specs=[vmem] * 2 + [pl.BlockSpec(memory_s...  3.65 us
    pallas_call x1, Pallas kernels, body(): pl.pallas_call(pack_columns, in_specs=[pl.BlockSpec(memory_space=pltpu.HB...  2.7 us
    ppermute x1, starting transfers between devices, body(): row_b = lax.ppermute(row_b, axes, lat_pairs(nlon, nlat, True))  2.68 us
    pallas_call x1, Pallas kernels, body(): pl.pallas_call(prepare_interior, in_specs=[vmem] * 9, out_shape=(state, j...  2.38 us
  transfers between devices with their start and end apart: 4, of which 0 were waited for; matrix products, arithmetic and copies ran while one was open for 0% of the time, Pallas kernels for 19%

profile of v8, /device:TPU:24, one launch (start us, length us, event | category | flops | bytes accessed | tf_op | source)
XLA Modules:
  0.0 31.1 jit_solution(6224529384024788293)
XLA Ops:
  0.6 0.0 copy-start.4
  0.6 0.0 copy-start.5
  0.7 0.0 copy-start.6
  0.7 0.0 copy-start.7
  0.7 0.0 copy-start.8
  0.7 0.0 copy-start
  0.7 0.0 copy-start.1
  0.7 0.0 copy-start.2
  0.7 0.0 copy-start.3
  0.7 2.7 %pack_columns.1 = (f32[96,128]{1,0:T(8,128)}, f32[96,128]{1,0:T(8,128)}) custom-call(f32[3,96,256]{2,1,0:T(8,128)} %refs_9_.1, f32[3,96,256]{2,1,0:T(8,128)} %refs_10_.1, f32[3,96,256]{2,1,0:T(8,128)} %refs_11_.1, f32[3,96,256]{2,1,0:T(8,128)} %refs_12_.1, s32[96,256]{1,0:T(8,128)} %refs_0_.7, s32[96,256]{1,0:T(8,128)} %refs_1_.7, f32[96,256]{1,0:T(8,128)} %refs_2_.7, ...), custom_call_target="tpu_custom_call" | custom-call | tf_op jit(solution)/shard_map/pack_columns/pallas_call | solution.py:524
  3.4 7.8 %collective-permute-start = (f32[96,128]{1,0:T(8,128)}, f32[96,128]{1,0:T(8,128)S(1)}, u32[]{:S(2)}, u32[]{:S(2)}) collective-permute-start(f32[96,128]{1,0:T(8,128)} %get-tuple-element.21), channel_id=1, source_target_pairs={{0,248},{1,249},{2,250},{3,251},{4,252},{5,253},{6,254},{7,255},{8... | collective-permute-start | bytes 147464 | tf_op jit(solution)/shard_map/ppermute | solution.py:532
  11.3 0.0 collective-permute-start.1
  11.3 0.0 copy-done.4
  11.3 0.0 copy-done.5
  11.3 0.0 copy-done.6
  11.3 0.0 copy-done.7
  11.3 0.0 copy-done.8
  11.3 0.0 copy-done
  11.3 0.0 copy-done.1
  11.3 0.0 copy-done.2
  11.3 0.0 copy-done.3
  11.4 2.4 %prepare_interior.1 = (f32[5,3,2,112,128]{4,3,2,1,0:T(8,128)S(1)}, f32[11,3,2,112,128]{4,3,2,1,0:T(8,128)S(1)}, f32[9,96,128]{2,1,0:T(8,128)S(1)}, f32[5,3,2,112,128]{4,3,2,1,0:T(8,128)S(1)}) custom-call(f32[3,96,256]{2,1,0:T(8,128)S(1)} %copy-done, f32[3,96,256]{2,1,0:T(8,128)S(1)} %copy-done.1, f32[3,96,256]{2,1,0:T(8,128)S(1)} %copy-done.2, ...), custom_call_target="tpu_custom_call" | custom-call | flops 10000000 | bytes 8000000 | tf_op jit(solution)/shard_map/prepare_interior/pallas_call | solution.py:539
  13.7 0.0 collective-permute-done.refs_18_.refs_14_
  13.8 0.0 collective-permute-done.1.refs_19_.refs_15_
  13.8 0.1 pack_rows.1
  13.8 2.7 %collective-permute-start.2 = (f32[72,256]{1,0:T(8,128)S(1)}, f32[72,256]{1,0:T(8,128)S(1)}, u32[]{:S(2)}, u32[]{:S(2)}) collective-permute-start(f32[72,256]{1,0:T(8,128)S(1)} %get-tuple-element.31), channel_id=1, source_target_pairs={{1,2},{2,1},{3,4},{4,3},{5,6},{6,5},{7,255},{9,10},{10,9},{11,12},... | collective-permute-start | bytes 221192 | tf_op jit(solution)/shard_map/ppermute | solution.py:574
  16.5 4.7 %collective-permute-start.3 = (f32[72,256]{1,0:T(8,128)S(1)}, f32[72,256]{1,0:T(8,128)S(1)}, u32[]{:S(2)}, u32[]{:S(2)}) collective-permute-start(f32[72,256]{1,0:T(8,128)S(1)} %get-tuple-element.24.refs_2_), channel_id=1, source_target_pairs={{0,1},{1,0},{2,3},{3,2},{4,5},{5,4},{6,7},{7,6},{8,9},{9,8},{10,11... | collective-permute-start | bytes 221192 | tf_op jit(solution)/shard_map/ppermute | solution.py:575
  21.3 3.7 %run_interior.1 = (f32[5,3,2,112,128]{4,3,2,1,0:T(8,128)S(1)}, f32[5,3,2,112,128]{4,3,2,1,0:T(8,128)S(1)}, f32[3,96,256]{2,1,0:T(8,128)S(1)}, f32[3,96,256]{2,1,...) custom-call(f32[5,3,2,112,128]{4,3,2,1,0:T(8,128)S(1)} %get-tuple-element.19.refs_0_.refs_6_, ...), custom_call_target="tpu_custom_call" | custom-call | flops 30000000 | bytes 16000000 | tf_op jit(solution)/shard_map/run_interior/pallas_call | solution.py:577
  24.9 0.0 collective-permute-done.2.refs_16_
  24.9 0.0 collective-permute-done.3.refs_17_
  24.9 6.1 %run_rims.1 = (f32[3,96,256]{2,1,0:T(8,128)}, f32[3,96,256]{2,1,0:T(8,128)}, f32[3,96,256]{2,1,0:T(8,128)}, f32[3,96,256]{2,1,0:T(8,128)}) custom-call(s32[96,256]{1,0:T(8,128)S(1)} %copy-done.4, s32[96,256]{1,0:T(8,128)S(1)} %copy-done.5, f32[96,256]{1,0:T(8,128)S(1)} %copy-done.6, f32[96,256]{1,0:T(8,128)S(1)} %copy-done.7, f32[96,256]{1,0:T(8,128)S(1)} %copy-done.8, ...), custom_call_target="tpu_custom_call" | custom-call | tf_op jit(solution)/shard_map/run_rims/pallas_call | solution.py:586
Async XLA Ops:
  0.6 10.6 %copy-start.4 = (s32[96,256]{1,0:T(8,128)S(1)}, s32[96,256]{1,0:T(8,128)}, u32[]{:S(2)}) copy-start(s32[96,256]{1,0:T(8,128)} %refs_0_.7) | copy-start | bytes 294916
  0.6 10.6 %copy-start.5 = (s32[96,256]{1,0:T(8,128)S(1)}, s32[96,256]{1,0:T(8,128)}, u32[]{:S(2)}) copy-start(s32[96,256]{1,0:T(8,128)} %refs_1_.7) | copy-start | bytes 294916
  0.7 10.6 %copy-start.6 = (f32[96,256]{1,0:T(8,128)S(1)}, f32[96,256]{1,0:T(8,128)}, u32[]{:S(2)}) copy-start(f32[96,256]{1,0:T(8,128)} %refs_2_.7) | copy-start | bytes 294916
  0.7 10.6 %copy-start.7 = (f32[96,256]{1,0:T(8,128)S(1)}, f32[96,256]{1,0:T(8,128)}, u32[]{:S(2)}) copy-start(f32[96,256]{1,0:T(8,128)} %refs_3_.7) | copy-start | bytes 294916
  0.7 10.6 %copy-start.8 = (f32[96,256]{1,0:T(8,128)S(1)}, f32[96,256]{1,0:T(8,128)}, u32[]{:S(2)}) copy-start(f32[96,256]{1,0:T(8,128)} %refs_4_.7) | copy-start | bytes 294916
  0.7 10.6 %copy-start = (f32[3,96,256]{2,1,0:T(8,128)S(1)}, f32[3,96,256]{2,1,0:T(8,128)}, u32[]{:S(2)}) copy-start(f32[3,96,256]{2,1,0:T(8,128)} %refs_9_.1) | copy-start | bytes 884740
  0.7 10.6 %copy-start.1 = (f32[3,96,256]{2,1,0:T(8,128)S(1)}, f32[3,96,256]{2,1,0:T(8,128)}, u32[]{:S(2)}) copy-start(f32[3,96,256]{2,1,0:T(8,128)} %refs_10_.1) | copy-start | bytes 884740
  0.7 10.6 %copy-start.2 = (f32[3,96,256]{2,1,0:T(8,128)S(1)}, f32[3,96,256]{2,1,0:T(8,128)}, u32[]{:S(2)}) copy-start(f32[3,96,256]{2,1,0:T(8,128)} %refs_11_.1) | copy-start | bytes 884740
  0.7 10.6 %copy-start.3 = (f32[3,96,256]{2,1,0:T(8,128)S(1)}, f32[3,96,256]{2,1,0:T(8,128)}, u32[]{:S(2)}) copy-start(f32[3,96,256]{2,1,0:T(8,128)} %refs_12_.1) | copy-start | bytes 884740
  3.4 10.3 %collective-permute-start = (f32[96,128]{1,0:T(8,128)}, f32[96,128]{1,0:T(8,128)S(1)}, u32[]{:S(2)}, u32[]{:S(2)}) collective-permute-start(f32[96,128]{1,0:T(8,128)} %get-tuple-element.21), channel_id=1, source_target_pairs={{0,248},{1,249},{2,250},{3,251},{4,252},{5,253},{6,254},{7,255},{8... | collective-permute-start | bytes 147464 | tf_op jit(solution)/shard_map/ppermute | solution.py:532
  11.3 2.5 %collective-permute-start.1 = (f32[96,128]{1,0:T(8,128)}, f32[96,128]{1,0:T(8,128)S(1)}, u32[]{:S(2)}, u32[]{:S(2)}) collective-permute-start(f32[96,128]{1,0:T(8,128)} %get-tuple-element.22), channel_id=1, source_target_pairs={{0,8},{1,9},{2,10},{3,11},{4,12},{5,13},{6,14},{7,15},{8,0},{9,1},... | collective-permute-start | bytes 147464 | tf_op jit(solution)/shard_map/ppermute | solution.py:535
  13.8 11.1 %collective-permute-start.2 = (f32[72,256]{1,0:T(8,128)S(1)}, f32[72,256]{1,0:T(8,128)S(1)}, u32[]{:S(2)}, u32[]{:S(2)}) collective-permute-start(f32[72,256]{1,0:T(8,128)S(1)} %get-tuple-element.31), channel_id=1, source_target_pairs={{1,2},{2,1},{3,4},{4,3},{5,6},{6,5},{7,255},{9,10},{10,9},{11,12},... | collective-permute-start | bytes 221192 | tf_op jit(solution)/shard_map/ppermute | solution.py:574
  16.5 8.4 %collective-permute-start.3 = (f32[72,256]{1,0:T(8,128)S(1)}, f32[72,256]{1,0:T(8,128)S(1)}, u32[]{:S(2)}, u32[]{:S(2)}) collective-permute-start(f32[72,256]{1,0:T(8,128)S(1)} %get-tuple-element.24.refs_2_), channel_id=1, source_target_pairs={{0,1},{1,0},{2,3},{3,2},{4,5},{5,4},{6,7},{7,6},{8,9},{9,8},{10,11... | collective-permute-start | bytes 221192 | tf_op jit(solution)/shard_map/ppermute | solution.py:575
